TPU v7x, 32 devices: a whole 2x2x4 slice. The times are simulated.
32 devices in a mesh: grp: 2 (over y), ft: 4 (over z), bl: 4 (over x, core).
Axes of the slice: x: 2, y: 2, z: 4, core: 2. Of those that a mesh axis runs over, the one named last changes fastest.
Arguments:
- voltages: bfloat16 [2, 16384, 1024], P(None, ('grp', 'ft'), 'bl'), parts along dimension 1, may hold values from -11 to 11
- coefs: float32 [8, 2048], replicated, may hold values from -2 to 2
- block_ids: int32 [4], replicated, may hold values from 0 to 3, each once
- tile_owner: int32 [20], P('grp'), parts along dimension 0, may hold values from 0 to 3, as said below
Outputs:
- vis: float32 [2, 64, 20, 256, 256], P(None, ('grp', 'ft'), 'bl'), parts along dimension 1
There are 2 independent parts, one for each index of `grp`. A program takes and returns all parts, laid end to end along the dimension named above; an argument that names none is the same for every part. Nothing has to cross between parts.
Inputs may be any that keep to these rules, and one draw needn't show every extreme that they name: tile_owner[t] is the index along bl of the device that owns tile t; one owner holds exactly 5 tiles, the others share the remaining tiles as evenly as counts allow.
All inputs are finite; a program needn't handle non-finite values.
Results may differ from a plain program's by a relative error of at most 0.00099.
Values may be sent and summed in bfloat16 or wider, within the bound.
No kernel may reach another device: no remote copies, remote signals or barrier semaphores. Data moves between devices by JAX's collectives and lax.ppermute only.
A program may use at most 128 MiB of HBM per device.

v0:
```python
import functools
import math

import jax
import jax.numpy as jnp
import ml_dtypes
import numpy as np
from jax import lax
from jax.experimental import pallas as pl
from jax.experimental.pallas import tpu as pltpu
from jax.sharding import PartitionSpec as P

AVG = 64
MXU = 256
LANES = 128
ROWS16 = 16
VMEM_BYTES = 48 * 1024 * 1024


def split_bf16(table):
    high = table.astype(ml_dtypes.bfloat16)
    low = (table - high.astype(np.float64)).astype(ml_dtypes.bfloat16)
    return high, low


def matrix_tables(inner_len):
    steps = np.arange(inner_len)
    angles = 2.0 * np.pi * (np.outer(steps, steps) % inner_len) / inner_len
    cos_part, sin_part = np.cos(angles), np.sin(angles)
    high, low = split_bf16(np.block([[cos_part, -sin_part], [sin_part, cos_part]]))
    return np.concatenate([high, high, low])


def twiddle_tables(radix, inner_len):
    chan_count = radix * inner_len
    angles = 2.0 * np.pi * np.outer(np.arange(radix), np.arange(inner_len)) / chan_count
    scale = 1.0 / math.sqrt(chan_count)
    return np.stack([np.cos(angles) * scale, np.sin(angles) * scale]).astype(np.float32)


def rotate(real, imag, step, count):
    step = step % count
    if step == 0:
        return real, imag
    if 4 * step == count:
        return imag, -real
    if 2 * step == count:
        return -real, -imag
    if 4 * step == 3 * count:
        return -imag, real
    cos_step = math.cos(2.0 * math.pi * step / count)
    sin_step = math.sin(2.0 * math.pi * step / count)
    if 8 * step == count:
        return cos_step * (real + imag), cos_step * (imag - real)
    return cos_step * real + sin_step * imag, cos_step * imag - sin_step * real


def butterflies(parts):
    count = len(parts)
    if count == 1:
        return parts
    half = count // 2
    sums, diffs = [], []
    for k in range(half):
        (ar, ai), (br, bi) = parts[k], parts[k + half]
        sums.append((ar + br, ai + bi))
        diffs.append(rotate(ar - br, ai - bi, k, count))
    even, odd = butterflies(sums), butterflies(diffs)
    out = []
    for k in range(half):
        out += [even[k], odd[k]]
    return out


def pack_kernel(radix, place_ref, v_ref, *rest):
    o_refs, (wide, turned) = rest[:-2], rest[-2:]
    dests, rows, samples = turned.shape
    inner = samples // radix
    wide[...] = v_ref[0].astype(jnp.float32)
    for phase in range(radix):
        part = wide[pl.ds(phase, inner, stride=radix), :].T.astype(jnp.bfloat16)
        for dest in range(dests):
            turned[dest, :, phase * inner : (phase + 1) * inner] = part[
                dest * rows : (dest + 1) * rows
            ]
    for shift in range(dests):
        o_refs[shift][0] = turned[place_ref[shift]]


def pack(voltages, place, dests, radix):
    _, samples, inputs = voltages.shape
    chunks = inputs // LANES
    rows = LANES // dests
    return pl.pallas_call(
        functools.partial(pack_kernel, radix),
        grid_spec=pltpu.PrefetchScalarGridSpec(
            num_scalar_prefetch=1,
            grid=(2, chunks),
            in_specs=[pl.BlockSpec((1, samples, LANES), lambda p, h, t: (p, 0, h))],
            out_specs=[pl.BlockSpec((1, rows, samples), lambda p, h, t: (p, h, 0))] * dests,
            scratch_shapes=[
                pltpu.VMEM((samples, LANES), jnp.float32),
                pltpu.VMEM((dests, rows, samples), jnp.bfloat16),
            ],
        ),
        out_shape=[jax.ShapeDtypeStruct((2, chunks * rows, samples), jnp.bfloat16)] * dests,
        compiler_params=pltpu.CompilerParams(vmem_limit_bytes=VMEM_BYTES),
        name="pack_inputs",
    )(place, voltages)


def stage_kernel(*refs):
    half = len(refs) // 2
    for source, target in zip(refs[:half], refs[half:]):
        target[...] = source[...]


def stage(*tables):
    vmem = pl.BlockSpec(memory_space=pltpu.VMEM)
    return pl.pallas_call(
        stage_kernel,
        in_specs=[vmem] * len(tables),
        out_specs=[vmem] * len(tables),
        out_shape=[jax.ShapeDtypeStruct(table.shape, table.dtype) for table in tables],
        compiler_params=pltpu.CompilerParams(vmem_limit_bytes=VMEM_BYTES // 4),
        name="stage_tables",
    )(*tables)


def transform_kernel(radix, dests, units, place_ref, *rest):
    v_refs = rest[:dests]
    c_ref, tw_ref, g_ref = rest[dests : dests + 3]
    out_refs = rest[dests + 4 : -4]
    held, split, prod, made = rest[-4:]
    spectra, _, rows, samples = held.shape
    taps = c_ref.shape[0]
    inner = samples // radix
    group = spectra * rows
    for shift in range(dests):
        held[place_ref[dests + shift]] = v_refs[shift][...]

    @pl.loop(0, radix)
    def _(phase):
        lane0 = pl.multiple_of(phase * inner, inner)
        row0 = pl.multiple_of(phase * group, group)
        for part in range(2):
            for sub in range(0, rows, ROWS16):
                blocks = [
                    held[b, part, pl.ds(sub, ROWS16), pl.ds(lane0, inner)].astype(jnp.float32)
                    for b in range(spectra)
                ]
                for s in range(spectra):
                    total = None
                    for b in range(max(0, s - taps + 1), s + 1):
                        term = c_ref[taps - 1 - s + b, pl.ds(phase, 1), :] * blocks[b]
                        total = term if total is None else total + term
                    high = total.astype(jnp.bfloat16)
                    low = (total - high.astype(jnp.float32)).astype(jnp.bfloat16)
                    at = pl.ds(pl.multiple_of(row0 + s * rows + sub, ROWS16), ROWS16)
                    split[at, part * inner : (part + 1) * inner] = high
                    split[at, (2 + part) * inner : (3 + part) * inner] = low

    @pl.loop(0, radix // 2)
    def _(pair):
        at = pl.ds(pl.multiple_of(pair * 2 * group, 2 * group), 2 * group)
        high = split[at, : 2 * inner]
        line = jnp.concatenate([high, split[at, 2 * inner :], high], axis=1)
        prod[at, :] = jnp.dot(line, g_ref[...], preferred_element_type=jnp.float32)

    halves = radix // dests
    lane_cuts = inner // LANES

    @pl.loop(0, spectra)
    def _(s):
        for sub in range(0, rows, ROWS16):
            for cut in range(lane_cuts):
                lane = cut * LANES
                parts = []
                for phase in range(radix):
                    at = pl.ds(pl.multiple_of(phase * group + s * rows + sub, ROWS16), ROWS16)
                    yr = prod[at, lane : lane + LANES]
                    yi = prod[at, inner + lane : inner + lane + LANES]
                    cos_here = tw_ref[0, phase : phase + 1, lane : lane + LANES]
                    sin_here = tw_ref[1, phase : phase + 1, lane : lane + LANES]
                    if phase == 0:
                        parts.append((yr * cos_here, yi * cos_here))
                    else:
                        parts.append(
                            (yr * cos_here + yi * sin_here, yi * cos_here - yr * sin_here)
                        )
                for step, pair in enumerate(butterflies(parts)):
                    unit = step % halves * lane_cuts + cut
                    for part in range(2):
                        made[step // halves, unit, part, s, sub : sub + ROWS16, :] = pair[
                            part
                        ].astype(jnp.bfloat16)

    for shift in range(dests):
        for unit in range(units):
            out_refs[unit * dests + shift][...] = made[place_ref[shift], unit]


def transform_all(blocks, place, tables, radix, after):
    dests = len(blocks)
    _, rows, samples = blocks[0].shape
    spectra = dests
    inner = samples // radix
    units = samples // dests // LANES
    anywhere = pl.BlockSpec(memory_space=pl.ANY)
    vmem = pl.BlockSpec(memory_space=pltpu.VMEM)
    total = radix * spectra * rows
    made = pl.pallas_call(
        functools.partial(transform_kernel, radix, dests, units),
        grid_spec=pltpu.PrefetchScalarGridSpec(
            num_scalar_prefetch=1,
            grid=(),
            in_specs=[vmem] * (dests + 3) + [anywhere],
            out_specs=[vmem] * (units * dests),
            scratch_shapes=[
                pltpu.VMEM((spectra, 2, rows, samples), jnp.bfloat16),
                pltpu.VMEM((total, 4 * inner), jnp.bfloat16),
                pltpu.VMEM((total, 2 * inner), jnp.float32),
                pltpu.VMEM((dests, units, 2, spectra, rows, LANES), jnp.bfloat16),
            ],
        ),
        out_shape=[jax.ShapeDtypeStruct((2, spectra, rows, LANES), jnp.bfloat16)]
        * (units * dests),
        cost_estimate=pl.CostEstimate(
            flops=3 * 2 * total * 4 * inner * inner, bytes_accessed=6 << 20, transcendentals=0
        ),
        compiler_params=pltpu.CompilerParams(vmem_limit_bytes=VMEM_BYTES),
        name="filter_transform",
    )(
        place,
        *blocks,
        *tables,
        after,
    )
    return [made[unit * dests : (unit + 1) * dests] for unit in range(units)]


def join(pieces, place, before, after):
    count = len(pieces)
    vmem = pl.BlockSpec(memory_space=pltpu.VMEM)
    shapes = [jax.ShapeDtypeStruct((count, *pieces[0].shape), pieces[0].dtype)]
    if before:
        shapes.append(jax.ShapeDtypeStruct((2, *before[0].shape), before[0].dtype))

    def kernel(place_ref, *rest):
        ins, outs = rest[: count + len(before)], rest[count + len(before) + 1 :]
        for shift in range(count):
            outs[0][place_ref[count + shift]] = ins[shift][...]
        for at in range(len(before)):
            outs[1][at] = ins[count + at][...]

    return pl.pallas_call(
        kernel,
        grid_spec=pltpu.PrefetchScalarGridSpec(
            num_scalar_prefetch=1,
            grid=(),
            in_specs=[vmem] * (count + len(before)) + [pl.BlockSpec(memory_space=pl.ANY)],
            out_specs=[vmem] * len(shapes),
        ),
        out_shape=shapes,
        compiler_params=pltpu.CompilerParams(vmem_limit_bytes=VMEM_BYTES // 4),
        name="join_pieces",
    )(place, *pieces, *before, after)


def pair(own, other, after):
    def kernel(own_ref, other_ref, _, out_ref):
        out_ref[0] = own_ref[...]
        out_ref[1] = other_ref[...]

    vmem = pl.BlockSpec(memory_space=pltpu.VMEM)
    return pl.pallas_call(
        kernel,
        in_specs=[vmem, vmem, pl.BlockSpec(memory_space=pl.ANY)],
        out_specs=vmem,
        out_shape=jax.ShapeDtypeStruct((2, *own.shape), own.dtype),
        compiler_params=pltpu.CompilerParams(vmem_limit_bytes=VMEM_BYTES // 4),
        name="pair_blocks",
    )(own, other, after)


def correlate_kernel(chunks, scale, first, table_ref, low_ref, high_ref, *rest):
    o_ref, token_ref, left, tiles, empty, sems = rest[-6:]
    half, senders, _, spectra, rows, lanes = low_ref.shape
    order = block_order(2 * half)
    slots = o_ref.shape[2]
    coarse = lanes // AVG
    side = senders * rows
    run = rows // chunks
    count = table_ref[2 * slots]
    token_ref[...] = jnp.zeros_like(token_ref)
    empty[...] = jnp.zeros_like(empty)

    def copy_out(source, c, slot):
        return pltpu.make_async_copy(source, o_ref.at[:, first + c, slot], sems.at[c, slot])

    for slot in range(slots):

        @pl.when(slot >= count)
        def _(slot=slot):
            for c in range(coarse):
                copy_out(empty, c, slot).start()

    for at, block in enumerate(order):
        source = (low_ref, high_ref)[at // half].at[at % half]

        @pl.loop(0, senders)
        def _(sender, block=block, source=source):
            for part in range(2):
                for chunk in range(chunks):
                    row = pl.multiple_of(part * side + (chunk * senders + sender) * run, run)
                    pieces = [
                        source[sender, part, s, chunk * run : (chunk + 1) * run]
                        for s in range(spectra)
                    ]
                    for c in range(coarse):
                        left[c, block, pl.ds(row, run), :] = jnp.concatenate(
                            [piece[:, c * AVG : (c + 1) * AVG] for piece in pieces], axis=1
                        )

    for slot in range(slots):

        @pl.when(slot < count)
        def _(slot=slot):
            for c in range(coarse):
                rows_of = left[c, table_ref[slot]]
                with_real, with_imag = [
                    lax.dot_general(
                        rows_of,
                        left[c, table_ref[slots + slot], pl.ds(part * side, side), :],
                        (((1,), (1,)), ((), ())),
                        preferred_element_type=jnp.float32,
                    )
                    for part in range(2)
                ]
                tiles[c, slot, 0] = (with_real[:side] + with_imag[side:]) * scale
                tiles[c, slot, 1] = (with_real[side:] - with_imag[:side]) * scale
                copy_out(tiles.at[c, slot], c, slot).start()

    for slot in range(slots):
        for c in range(coarse):
            copy_out(empty, c, slot).wait()


def correlate(table, gathered, unit, units, chunks, slots, vis):
    half, senders, _, spectra, rows, lanes = gathered[0].shape
    coarse = lanes // AVG
    side = senders * rows
    vmem = pl.BlockSpec(memory_space=pltpu.VMEM)
    anywhere = pl.BlockSpec(memory_space=pl.ANY)
    args = [table, *gathered]
    aliases = {}
    if vis is not None:
        args.append(vis)
        aliases = {len(args) - 1: 0}
    return pl.pallas_call(
        functools.partial(correlate_kernel, chunks, 1.0 / (AVG * spectra), unit * coarse),
        grid_spec=pltpu.PrefetchScalarGridSpec(
            num_scalar_prefetch=1,
            grid=(),
            in_specs=[vmem, vmem] + [anywhere] * (len(args) - 3),
            out_specs=[anywhere, vmem],
            scratch_shapes=[
                pltpu.VMEM((coarse, 2 * half, 2 * side, spectra * AVG), jnp.bfloat16),
                pltpu.VMEM((coarse, slots, 2, side, side), jnp.float32),
                pltpu.VMEM((2, side, side), jnp.float32),
                pltpu.SemaphoreType.DMA((coarse, slots)),
            ],
        ),
        out_shape=[
            jax.ShapeDtypeStruct((2, units * coarse, slots, side, side), jnp.float32),
            jax.ShapeDtypeStruct((8, LANES), jnp.float32),
        ],
        input_output_aliases=aliases,
        cost_estimate=pl.CostEstimate(flops=0, bytes_accessed=0, transcendentals=0),
        compiler_params=pltpu.CompilerParams(vmem_limit_bytes=VMEM_BYTES),
        name="correlate_tiles",
    )(*args)


def places(count):
    steps = np.arange(count, dtype=np.int32)
    index = lax.axis_index("ft").astype(jnp.int32)
    return jnp.concatenate([(index + steps) % count, (index + count - steps) % count])


def spread(pieces):
    count = len(pieces)
    return [pieces[0]] + [
        lax.ppermute(pieces[d], "ft", [(i, (i + d) % count) for i in range(count)])
        for d in range(1, count)
    ]


def exchange(own, bit):
    count = lax.axis_size("bl")
    return lax.ppermute(own, "bl", [(i, i ^ bit) for i in range(count)])


def gather_blocks(held, after):
    bit = lax.axis_size("bl") // 4
    other = exchange(held, bit)
    while bit > 1:
        bit //= 2
        held = pair(held, other, after).reshape(-1, *held.shape[1:])
        other = exchange(held, bit)
    return held, other


def block_order(count):
    order, bit = [0], count // 2
    while bit:
        order += [r ^ bit for r in order]
        bit //= 2
    return order


def tile_tables(block_ids, tile_owner):
    block_count = lax.axis_size("bl")
    tile_count = block_count * (block_count + 1) // 2
    slot_cap = 2 * tile_count // block_count
    pairs = [(i, j) for i in range(block_count) for j in range(i, block_count)]
    row_table = np.array([i for i, _ in pairs], np.int32)
    col_table = np.array([j for _, j in pairs], np.int32)
    mine = (tile_owner == lax.axis_index("bl")).astype(jnp.int32)
    earlier = np.tril(np.ones((tile_count, tile_count), np.int32), -1)
    rank = jnp.sum(earlier * mine[None, :], axis=1)
    labels = np.arange(block_count, dtype=np.int32)
    shard_of = jnp.sum(jnp.where(block_ids[None, :] == labels[:, None], labels[None, :], 0), axis=1)
    row_shard = jnp.sum(
        jnp.where(row_table[:, None] == labels[None, :], shard_of[None, :], 0), axis=1
    )
    col_shard = jnp.sum(
        jnp.where(col_table[:, None] == labels[None, :], shard_of[None, :], 0), axis=1
    )
    here = (mine[None, :] == 1) & (rank[None, :] == np.arange(slot_cap, dtype=np.int32)[:, None])
    rows = jnp.sum(jnp.where(here, row_shard[None, :], 0), axis=1)
    cols = jnp.sum(jnp.where(here, col_shard[None, :], 0), axis=1)
    index = lax.axis_index("bl")
    table = jnp.concatenate(
        [rows ^ index, cols ^ index, jnp.sum(mine, keepdims=True)]
    ).astype(jnp.int32)
    return table, slot_cap


def takes_kernels(mesh, voltages, coefs):
    dests = mesh.shape["ft"]
    blocks = mesh.shape["bl"]
    inputs = voltages.shape[2] // mesh.shape["bl"]
    per_dev = voltages.shape[1] // (mesh.shape["grp"] * dests)
    chan_count = coefs.shape[1]
    radix = chan_count // MXU
    return (
        per_dev == chan_count
        and chan_count % MXU == 0
        and radix & (radix - 1) == 0
        and radix % dests == 0
        and radix <= 8
        and blocks & (blocks - 1) == 0
        and blocks > 2
        and inputs % LANES == 0
        and LANES % dests == 0
        and (LANES // dests) % ROWS16 == 0
        and (dests * AVG) % LANES == 0
    )


def per_device_kernels(voltages, coefs, block_ids, tile_owner):
    dests = lax.axis_size("ft")
    taps, chan_count = coefs.shape
    radix = chan_count // MXU
    chunks = voltages.shape[2] // LANES
    coef_table = coefs.reshape(taps, MXU, radix).transpose(0, 2, 1)
    place = places(dests)
    table, slot_cap = tile_tables(block_ids, tile_owner)
    tables = stage(coef_table, twiddle_tables(radix, MXU), matrix_tables(MXU))
    arrived = spread(pack(voltages, place, dests, radix))
    made = transform_all(arrived, place, tables, radix, table)
    half = lax.axis_size("bl") // 2
    units = len(made)
    own, other, arrived, tokens, vis = None, None, None, [], None
    for unit in range(units + 1):
        held = None
        if unit < units:
            parts = made[unit]
            if unit > 1:
                parts, _ = lax.optimization_barrier((parts, arrived))
            arrived = spread(parts)
            after = tokens[-1] if tokens else table
            if unit > 0:
                own, held = join(arrived, place, (own, other), after)
            else:
                (own,) = join(arrived, place, (), after)
            other = exchange(own, half)
        else:
            held = pair(own, other, tokens[-1])
        if unit > 0:
            gathered = gather_blocks(held, table)
            vis, token = correlate(table, gathered, unit - 1, units, chunks, slot_cap, vis)
            tokens.append(token)
    return vis


def tile_product(row_part, col_part, norm_scale):
    products = jnp.einsum(
        "pscax,qscay->cpqxy", row_part, col_part, preferred_element_type=jnp.float32
    )
    real_part = products[:, 0, 0] + products[:, 1, 1]
    imag_part = products[:, 1, 0] - products[:, 0, 1]
    return jnp.stack([real_part, imag_part]) * norm_scale


def dft_tables(order_len):
    steps_one = jnp.arange(order_len, dtype=jnp.int32)
    phase_grid = steps_one[:, None] * steps_one[None, :] % order_len
    angles = phase_grid.astype(jnp.float32) * (2.0 * math.pi / order_len)
    return (jnp.cos(angles), jnp.sin(angles))


def transform(filtered):
    per_dev = filtered.shape[1]
    chan_count = filtered.shape[2]
    rows_here = filtered.shape[3]
    outer_len = math.isqrt(chan_count)
    while chan_count % outer_len != 0:
        outer_len = outer_len - 1
    inner_len = chan_count // outer_len
    highest = lax.Precision.HIGHEST
    reshaped = filtered.reshape(2, per_dev, outer_len, inner_len, rows_here)
    real_in = reshaped[0]
    imag_in = reshaped[1]
    cos_outer, sin_outer = dft_tables(outer_len)
    section_re = jnp.einsum("snkb,nm->smkb", real_in, cos_outer, precision=highest) + jnp.einsum(
        "snkb,nm->smkb", imag_in, sin_outer, precision=highest
    )
    section_im = jnp.einsum("snkb,nm->smkb", imag_in, cos_outer, precision=highest) - jnp.einsum(
        "snkb,nm->smkb", real_in, sin_outer, precision=highest
    )
    twiddle_grid = (
        jnp.arange(outer_len, dtype=jnp.int32)[:, None]
        * jnp.arange(inner_len, dtype=jnp.int32)[None, :]
        % chan_count
    )
    twiddle_angles = twiddle_grid.astype(jnp.float32) * (2.0 * math.pi / chan_count)
    cos_twiddle = jnp.cos(twiddle_angles)[None, :, :, None]
    sin_twiddle = jnp.sin(twiddle_angles)[None, :, :, None]
    rot_re = section_re * cos_twiddle + section_im * sin_twiddle
    rot_im = section_im * cos_twiddle - section_re * sin_twiddle
    cos_inner, sin_inner = dft_tables(inner_len)
    final_re = jnp.einsum("smkb,kq->sqmb", rot_re, cos_inner, precision=highest) + jnp.einsum(
        "smkb,kq->sqmb", rot_im, sin_inner, precision=highest
    )
    final_im = jnp.einsum("smkb,kq->sqmb", rot_im, cos_inner, precision=highest) - jnp.einsum(
        "smkb,kq->sqmb", rot_re, sin_inner, precision=highest
    )
    stacked = jnp.stack([final_re, final_im]).reshape(2, per_dev, chan_count, rows_here)
    return (stacked * (1.0 / math.sqrt(chan_count))).astype(jnp.bfloat16)


def apply_taps(window, coef_part, taps_count, out_len):
    filtered = jnp.zeros((2, out_len, window.shape[2], window.shape[3]), jnp.float32)
    for tap_index in range(taps_count):
        filtered = filtered + coef_part[tap_index][None, None, :, None] * window[
            :, tap_index : tap_index + out_len
        ].astype(jnp.float32)
    return filtered


def per_device(voltages, coefs, block_ids, tile_owner):
    taps_count = coefs.shape[0]
    chan_count = coefs.shape[1]
    rows_here = voltages.shape[2]
    per_dev = voltages.shape[1] // chan_count
    volt_blocks = voltages.reshape(2, per_dev, chan_count, rows_here)
    phase_block = lax.all_to_all(volt_blocks, "ft", split_axis=2, concat_axis=1, tiled=True)
    spectra_count = phase_block.shape[1]
    phase_here = phase_block.shape[2]
    coef_part = lax.dynamic_slice_in_dim(coefs, lax.axis_index("ft") * phase_here, phase_here, 1)
    zero_front = jnp.zeros((2, taps_count - 1, phase_here, rows_here), phase_block.dtype)
    long_window = jnp.concatenate([zero_front, phase_block], axis=1)
    phase_filtered = apply_taps(long_window, coef_part, taps_count, spectra_count)
    filtered = lax.all_to_all(phase_filtered, "ft", split_axis=1, concat_axis=2, tiled=True)
    spectra = transform(filtered)
    turned = lax.all_to_all(spectra, "ft", split_axis=2, concat_axis=1, tiled=True)
    spectra_all = turned.shape[1]
    chan_here = turned.shape[2]
    coarse_here = chan_here // AVG
    coarse_view = turned.reshape(2, spectra_all, coarse_here, AVG, rows_here)
    norm_scale = 1.0 / (AVG * spectra_all)
    block_count = lax.axis_size("bl")
    my_index = lax.axis_index("bl")
    tile_count = block_count * (block_count + 1) // 2
    slot_cap = 2 * tile_count // block_count
    row_table = jnp.asarray(
        np.array(
            [
                first_id
                for first_id in range(block_count)
                for second_id in range(first_id, block_count)
            ],
            dtype=np.int32,
        )
    )
    col_table = jnp.asarray(
        np.array(
            [
                second_id
                for first_id in range(block_count)
                for second_id in range(first_id, block_count)
            ],
            dtype=np.int32,
        )
    )
    tile_pos = jnp.arange(tile_count, dtype=jnp.int32)
    same_owner = tile_owner[None, :] == tile_owner[:, None]
    before_mask = tile_pos[None, :] < tile_pos[:, None]
    slot_rank = jnp.sum((same_owner & before_mask).astype(jnp.int32), axis=1)
    labels = jnp.arange(block_count, dtype=jnp.int32)
    shard_of = jnp.sum(jnp.where(block_ids[None, :] == labels[:, None], labels[None, :], 0), axis=1)
    gathered = lax.all_gather(coarse_view[None], "bl", axis=0, tiled=True)
    mine_mask = tile_owner == my_index
    own_count = jnp.sum(mine_mask.astype(jnp.int32))
    slot_steps = jnp.arange(slot_cap, dtype=jnp.int32)
    slot_tile = jnp.sum(
        jnp.where(
            mine_mask[None, :] & (slot_rank[None, :] == slot_steps[:, None]), tile_pos[None, :], 0
        ),
        axis=1,
    )

    def one_tile(slot_pos, result_tiles):
        tile_id = slot_tile[slot_pos]
        row_block = gathered[shard_of[row_table[tile_id]]]
        col_block = gathered[shard_of[col_table[tile_id]]]
        tile = tile_product(row_block, col_block, norm_scale)
        return lax.dynamic_update_slice(result_tiles, tile[:, :, None], (0, 0, slot_pos, 0, 0))

    empty_tiles = jnp.zeros((2, coarse_here, slot_cap, rows_here, rows_here), jnp.float32)
    return lax.fori_loop(0, own_count, one_tile, empty_tiles)


def solution(mesh):
    def correlator(voltages, coefs, block_ids, tile_owner):
        fits = takes_kernels(mesh, voltages, coefs)
        return jax.shard_map(
            per_device_kernels if fits else per_device,
            mesh=mesh,
            in_specs=(P(None, ("grp", "ft"), "bl"), P(), P(), P("grp")),
            out_specs=P(None, ("grp", "ft"), "bl", None, None),
            check_vma=False,
        )(voltages, coefs, block_ids, tile_owner)

    return correlator
```

profile of v0, /device:TPU:0, one launch (start us, length us, event | category | flops | bytes accessed | tf_op | source)
XLA Modules:
  0.0 142.5 jit_solution(4499107061182950588)
XLA Ops:
  0.0 0.1 pad_add_fusion.1.place_ref
  0.1 1.6 %copy-done = bf16[2,2048,256]{2,1,0:T(8,128)(2,1)S(1)} copy-done((bf16[2,2048,256]{2,1,0:T(8,128)(2,1)S(1)}, bf16[2,2048,256]{2,1,0:T(8,128)(2,1)}, u32[]{:S(2)}) %copy-start) | copy-done | bytes 2097176
  1.7 3.1 %pack_inputs.1 = (bf16[2,64,2048]{2,1,0:T(8,128)(2,1)S(1)}, bf16[2,64,2048]{2,1,0:T(8,128)(2,1)}, bf16[2,64,2048]{2,1,0:T(8,128)(2,1)S(1)}, bf16[2,64,2048]{2,1,0:T(8,128)(2,1)S(1)}) custom-call(s32[8]{0:T(128)S(1)} %pad_add_fusion.1.place_ref, bf16[2,2048,256]{2,1,0:T(8,128)(2,1)S(1)} %copy-done), custom_call_target="tpu_custom_call" | custom-call | tf_op jit(solution)/shard_map/pack_inputs/pallas_call | solution.py:94
  4.8 3.0 %collective-permute-start = (bf16[2,64,2048]{2,1,0:T(8,128)(2,1)}, bf16[2,64,2048]{2,1,0:T(8,128)(2,1)S(1)}, u32[]{:S(2)}, u32[]{:S(2)}) collective-permute-start(bf16[2,64,2048]{2,1,0:T(8,128)(2,1)} %get-tuple-element.50), channel_id=1, source_target_pairs={{0,4},{4,8},{8,12},{12,0},{1,5},{5,9},{9,13},{13,1},{2,6},{6,10},{... | collective-permute-start | bytes 1572872 | tf_op jit(solution)/shard_map/ppermute | solution.py:394
  7.8 2.6 %collective-permute-start.1 = (bf16[2,64,2048]{2,1,0:T(8,128)(2,1)S(1)}, bf16[2,64,2048]{2,1,0:T(8,128)(2,1)S(1)}, u32[]{:S(2)}, u32[]{:S(2)}) collective-permute-start(bf16[2,64,2048]{2,1,0:T(8,128)(2,1)S(1)} %get-tuple-element.51), channel_id=1, source_target_pairs={{0,8},{4,12},{8,0},{12,4},{1,9},{5,13},{9,1},{13,5},{2,10},{6,14},... | collective-permute-start | bytes 1572872 | tf_op jit(solution)/shard_map/ppermute | solution.py:394
  10.4 1.3 collective-permute-start.2
  11.8 0.8 fusion.1
  12.5 2.4 %reshape.11 = f32[8,256,8]{2,1,0:T(8,128)} reshape(f32[8,2048]{1,0:T(8,128)} %param.14) | data formatting | bytes 131072 | tf_op jit(solution)/shard_map/reshape | solution.py:477
  14.9 1.5 %copy.18 = f32[8,256,8]{1,2,0:T(8,128)S(1)} copy(f32[8,256,8]{2,1,0:T(8,128)} %reshape.11) | data formatting | bytes 131072 | tf_op jit(solution)/shard_map/reshape | solution.py:477
  16.5 0.7 broadcast_compare_fusion
  17.1 0.6 reduce_sum.69
  17.8 0.8 select_reduce_fusion.3
  18.5 1.4 copy-done.1
  19.9 0.7 copy-done.2
  20.6 0.1 stage_tables.1
  20.8 0.8 multiply_reduce_fusion
  21.6 0.2 select_reduce_fusion.1
  21.7 0.7 pad_add_fusion.rest_7_.rest_4_.rest_6_.table_ref
  22.5 0.5 collective-permute-done.rest_1_
  23.0 21.6 %collective-permute-done.1.rest_2_ = bf16[2,64,2048]{2,1,0:T(8,128)(2,1)S(1)} collective-permute-done((bf16[2,64,2048]{2,1,0:T(8,128)(2,1)S(1)}, bf16[2,64,2048]{2,1,0:T(8,128)(2,1)S(1)}, u32[]{:S(2)}, u32[]{:S(2)}) %collective-permute-start.1) | collective-permute-done | bytes 524320 | tf_op jit(solution)/shard_map/ppermute | solution.py:394
  44.6 7.0 %filter_transform.1 = (bf16[2,4,64,128]{3,2,1,0:T(8,128)(2,1)S(1)}, bf16[2,4,64,128]{3,2,1,0:T(8,128)(2,1)S(1)}, bf16[2,4,64,128]{3,2,1,0:T(8,128)(2,1)S(1)}, bf...) custom-call(s32[8]{0:T(128)S(1)} %pad_add_fusion.1.place_ref, ...), custom_call_target="tpu_custom_call" | custom-call | flops 3221225472 | bytes 6291456 | tf_op jit(solution)/shard_map/filter_transform/pallas_call | solution.py:212
  51.6 11.8 %collective-permute-start.12 = (bf16[2,4,64,128]{3,2,1,0:T(8,128)(2,1)S(1)}, bf16[2,4,64,128]{3,2,1,0:T(8,128)(2,1)S(1)}, u32[]{:S(2)}, u32[]{:S(2)}) collective-permute-start(bf16[2,4,64,128]{3,2,1,0:T(8,128)(2,1)S(1)} %get-tuple-element.77), channel_id=1, source_target_pairs={{0,4},{4,8},{8,12},{12,0},{1,5},{5,9},{9,13},{13,1},{2,6},{6,10},{... | collective-permute-start | bytes 393224 | tf_op jit(solution)/shard_map/ppermute | solution.py:394
  63.4 1.6 %collective-permute-start.13 = (bf16[2,4,64,128]{3,2,1,0:T(8,128)(2,1)S(1)}, bf16[2,4,64,128]{3,2,1,0:T(8,128)(2,1)S(1)}, u32[]{:S(2)}, u32[]{:S(2)}) collective-permute-start(bf16[2,4,64,128]{3,2,1,0:T(8,128)(2,1)S(1)} %get-tuple-element.78), channel_id=1, source_target_pairs={{0,8},{4,12},{8,0},{12,4},{1,9},{5,13},{9,1},{13,5},{2,10},{6,14},... | collective-permute-start | bytes 393224 | tf_op jit(solution)/shard_map/ppermute | solution.py:394
  65.0 0.8 collective-permute-start.14
  65.8 2.7 %collective-permute-done.12.rest_1_ = bf16[2,4,64,128]{3,2,1,0:T(8,128)(2,1)S(1)} collective-permute-done((bf16[2,4,64,128]{3,2,1,0:T(8,128)(2,1)S(1)}, bf16[2,4,64,128]{3,2,1,0:T(8,128)(2,1)S(1)}, u32[]{:S(2)}, u32[]{:S(2)}) %collective-permute-start.12) | collective-permute-done | bytes 131104 | tf_op jit(solution)/shard_map/ppermute | solution.py:394
  68.5 4.6 %collective-permute-done.13.rest_2_ = bf16[2,4,64,128]{3,2,1,0:T(8,128)(2,1)S(1)} collective-permute-done((bf16[2,4,64,128]{3,2,1,0:T(8,128)(2,1)S(1)}, bf16[2,4,64,128]{3,2,1,0:T(8,128)(2,1)S(1)}, u32[]{:S(2)}, u32[]{:S(2)}) %collective-permute-start.13) | collective-permute-done | bytes 131104 | tf_op jit(solution)/shard_map/ppermute | solution.py:394
  73.1 0.6 join_pieces.4.rest_4_
  73.6 1.6 %collective-permute-start.15 = (bf16[4,2,4,64,128]{4,3,2,1,0:T(8,128)(2,1)S(1)}, bf16[4,2,4,64,128]{4,3,2,1,0:T(8,128)(2,1)S(1)}, u32[]{:S(2)}, u32[]{:S(2)}) collective-permute-start(bf16[4,2,4,64,128]{4,3,2,1,0:T(8,128)(2,1)S(1)} %join_pieces.4.rest_4_), channel_id=1, source_target_pairs={{0,2},{1,3},{2,0},{3,1},{4,6},{5,7},{6,4},{7,5},{8,10},{9,11},{10,... | collective-permute-start | bytes 1572872 | tf_op jit(solution)/shard_map/ppermute | solution.py:401
  75.2 3.3 %collective-permute-start.3 = (bf16[2,4,64,128]{3,2,1,0:T(8,128)(2,1)S(1)}, bf16[2,4,64,128]{3,2,1,0:T(8,128)(2,1)S(1)}, u32[]{:S(2)}, u32[]{:S(2)}) collective-permute-start(bf16[2,4,64,128]{3,2,1,0:T(8,128)(2,1)S(1)} %get-tuple-element.65), channel_id=1, source_target_pairs={{0,4},{4,8},{8,12},{12,0},{1,5},{5,9},{9,13},{13,1},{2,6},{6,10},{... | collective-permute-start | bytes 393224 | tf_op jit(solution)/shard_map/ppermute | solution.py:394
  78.5 2.1 %collective-permute-start.4 = (bf16[2,4,64,128]{3,2,1,0:T(8,128)(2,1)S(1)}, bf16[2,4,64,128]{3,2,1,0:T(8,128)(2,1)S(1)}, u32[]{:S(2)}, u32[]{:S(2)}) collective-permute-start(bf16[2,4,64,128]{3,2,1,0:T(8,128)(2,1)S(1)} %get-tuple-element.66), channel_id=1, source_target_pairs={{0,8},{4,12},{8,0},{12,4},{1,9},{5,13},{9,1},{13,5},{2,10},{6,14},... | collective-permute-start | bytes 393224 | tf_op jit(solution)/shard_map/ppermute | solution.py:394
  80.5 0.3 collective-permute-start.5
  80.8 3.6 %collective-permute-done.3.rest_1_ = bf16[2,4,64,128]{3,2,1,0:T(8,128)(2,1)S(1)} collective-permute-done((bf16[2,4,64,128]{3,2,1,0:T(8,128)(2,1)S(1)}, bf16[2,4,64,128]{3,2,1,0:T(8,128)(2,1)S(1)}, u32[]{:S(2)}, u32[]{:S(2)}) %collective-permute-start.3) | collective-permute-done | bytes 131104 | tf_op jit(solution)/shard_map/ppermute | solution.py:394
  84.5 4.1 %collective-permute-done.4.rest_2_ = bf16[2,4,64,128]{3,2,1,0:T(8,128)(2,1)S(1)} collective-permute-done((bf16[2,4,64,128]{3,2,1,0:T(8,128)(2,1)S(1)}, bf16[2,4,64,128]{3,2,1,0:T(8,128)(2,1)S(1)}, u32[]{:S(2)}, u32[]{:S(2)}) %collective-permute-start.4) | collective-permute-done | bytes 131104 | tf_op jit(solution)/shard_map/ppermute | solution.py:394
  88.6 0.1 collective-permute-done.5.rest_3_
  88.7 0.6 join_pieces.5
  89.3 0.1 collective-permute-start.17
  89.4 0.6 collective-permute-start.16
  90.0 3.1 %collective-permute-start.6 = (bf16[2,4,64,128]{3,2,1,0:T(8,128)(2,1)S(1)}, bf16[2,4,64,128]{3,2,1,0:T(8,128)(2,1)S(1)}, u32[]{:S(2)}, u32[]{:S(2)}) collective-permute-start(bf16[2,4,64,128]{3,2,1,0:T(8,128)(2,1)S(1)} %get-tuple-element.69), channel_id=1, source_target_pairs={{0,4},{4,8},{8,12},{12,0},{1,5},{5,9},{9,13},{13,1},{2,6},{6,10},{... | collective-permute-start | bytes 393224 | tf_op jit(solution)/shard_map/ppermute | solution.py:394
  93.2 1.5 %collective-permute-start.7 = (bf16[2,4,64,128]{3,2,1,0:T(8,128)(2,1)S(1)}, bf16[2,4,64,128]{3,2,1,0:T(8,128)(2,1)S(1)}, u32[]{:S(2)}, u32[]{:S(2)}) collective-permute-start(bf16[2,4,64,128]{3,2,1,0:T(8,128)(2,1)S(1)} %get-tuple-element.70), channel_id=1, source_target_pairs={{0,8},{4,12},{8,0},{12,4},{1,9},{5,13},{9,1},{13,5},{2,10},{6,14},... | collective-permute-start | bytes 393224 | tf_op jit(solution)/shard_map/ppermute | solution.py:394
  94.7 0.9 collective-permute-start.8
  95.5 0.0 collective-permute-done.17.high_ref
  95.5 4.3 %correlate_tiles.4 = (f32[2,8,5,256,256]{4,3,2,1,0:T(8,128)}, f32[8,128]{1,0:T(8,128)S(1)}) custom-call(s32[11]{0:T(128)S(1)} %pad_add_fusion.rest_7_.rest_4_.rest_6_.table_ref, bf16[2,4,2,4,64,128]{5,4,3,2,1,0:T(8,128)(2,1)S(1)} %get-tuple-element.81.low_ref, bf16[2,4,2,4,64,128]{5,4,3,2,1,0:T(8,128)(2,1)S(1)} %collective-permute-done.17.high_ref), custom_call_target="tpu_custom_call" | custom-call | tf_op jit(solution)/shard_map/correlate_tiles/pallas_call | solution.py:360
  99.8 0.0 collective-permute-done.6.rest_1_
  99.8 3.8 %collective-permute-done.7.rest_2_ = bf16[2,4,64,128]{3,2,1,0:T(8,128)(2,1)S(1)} collective-permute-done((bf16[2,4,64,128]{3,2,1,0:T(8,128)(2,1)S(1)}, bf16[2,4,64,128]{3,2,1,0:T(8,128)(2,1)S(1)}, u32[]{:S(2)}, u32[]{:S(2)}) %collective-permute-start.7) | collective-permute-done | bytes 131104 | tf_op jit(solution)/shard_map/ppermute | solution.py:394
  103.6 0.1 collective-permute-done.16.rest_5_
  103.8 0.6 join_pieces.6
  104.4 0.1 collective-permute-start.19
  104.5 1.3 collective-permute-start.18
  105.8 3.3 %collective-permute-start.9 = (bf16[2,4,64,128]{3,2,1,0:T(8,128)(2,1)S(1)}, bf16[2,4,64,128]{3,2,1,0:T(8,128)(2,1)S(1)}, u32[]{:S(2)}, u32[]{:S(2)}) collective-permute-start(bf16[2,4,64,128]{3,2,1,0:T(8,128)(2,1)S(1)} %get-tuple-element.73), channel_id=1, source_target_pairs={{0,4},{4,8},{8,12},{12,0},{1,5},{5,9},{9,13},{13,1},{2,6},{6,10},{... | collective-permute-start | bytes 393224 | tf_op jit(solution)/shard_map/ppermute | solution.py:394
  109.1 1.5 %collective-permute-start.10 = (bf16[2,4,64,128]{3,2,1,0:T(8,128)(2,1)S(1)}, bf16[2,4,64,128]{3,2,1,0:T(8,128)(2,1)S(1)}, u32[]{:S(2)}, u32[]{:S(2)}) collective-permute-start(bf16[2,4,64,128]{3,2,1,0:T(8,128)(2,1)S(1)} %get-tuple-element.74), channel_id=1, source_target_pairs={{0,8},{4,12},{8,0},{12,4},{1,9},{5,13},{9,1},{13,5},{2,10},{6,14},... | collective-permute-start | bytes 393224 | tf_op jit(solution)/shard_map/ppermute | solution.py:394
  110.6 0.8 collective-permute-start.11
  111.5 0.0 collective-permute-done.19.high_ref
  111.5 4.3 %correlate_tiles.5 = (f32[2,8,5,256,256]{4,3,2,1,0:T(8,128)}, f32[8,128]{1,0:T(8,128)S(1)}) custom-call(s32[11]{0:T(128)S(1)} %pad_add_fusion.rest_7_.rest_4_.rest_6_.table_ref, bf16[2,4,2,4,64,128]{5,4,3,2,1,0:T(8,128)(2,1)S(1)} %get-tuple-element.84.low_ref, ...), custom_call_target="tpu_custom_call", output_to_operand_aliasing={{0}: (3, {})} | custom-call | tf_op jit(solution)/shard_map/correlate_tiles/pallas_call | solution.py:360
  115.8 3.9 %collective-permute-done.10.rest_2_ = bf16[2,4,64,128]{3,2,1,0:T(8,128)(2,1)S(1)} collective-permute-done((bf16[2,4,64,128]{3,2,1,0:T(8,128)(2,1)S(1)}, bf16[2,4,64,128]{3,2,1,0:T(8,128)(2,1)S(1)}, u32[]{:S(2)}, u32[]{:S(2)}) %collective-permute-start.10) | collective-permute-done | bytes 131104 | tf_op jit(solution)/shard_map/ppermute | solution.py:394
  119.6 0.6 join_pieces.7
  120.3 0.1 collective-permute-start.21
  120.4 0.6 collective-permute-start.20
  121.0 2.0 %collective-permute-done.21.high_ref = bf16[2,4,2,4,64,128]{5,4,3,2,1,0:T(8,128)(2,1)S(1)} collective-permute-done((bf16[2,4,2,4,64,128]{5,4,3,2,1,0:T(8,128)(2,1)S(1)}, bf16[2,4,2,4,64,128]{5,4,3,2,1,0:T(8,128)(2,1)S(1)}, u32[]{:S(2)}, u32[]{:S(2)}) %collective-permute-start.21) | collective-permute-done | bytes 1048608 | tf_op jit(solution)/shard_map/ppermute | solution.py:401
  123.0 4.3 %correlate_tiles.6 = (f32[2,8,5,256,256]{4,3,2,1,0:T(8,128)}, f32[8,128]{1,0:T(8,128)S(1)}) custom-call(s32[11]{0:T(128)S(1)} %pad_add_fusion.rest_7_.rest_4_.rest_6_.table_ref, bf16[2,4,2,4,64,128]{5,4,3,2,1,0:T(8,128)(2,1)S(1)} %get-tuple-element.88.low_ref, ...), custom_call_target="tpu_custom_call", output_to_operand_aliasing={{0}: (3, {})} | custom-call | tf_op jit(solution)/shard_map/correlate_tiles/pallas_call | solution.py:360
  127.3 7.4 %collective-permute-done.20.other_ref = bf16[4,2,4,64,128]{4,3,2,1,0:T(8,128)(2,1)S(1)} collective-permute-done((bf16[4,2,4,64,128]{4,3,2,1,0:T(8,128)(2,1)S(1)}, bf16[4,2,4,64,128]{4,3,2,1,0:T(8,128)(2,1)S(1)}, u32[]{:S(2)}, u32[]{:S(2)}) %collective-permute-start.20) | collective-permute-done | bytes 524320 | tf_op jit(solution)/shard_map/ppermute | solution.py:401
  134.7 0.1 pair_blocks.1.low_ref
  134.8 0.1 collective-permute-start.22
  134.8 2.6 %collective-permute-done.22.high_ref = bf16[2,4,2,4,64,128]{5,4,3,2,1,0:T(8,128)(2,1)S(1)} collective-permute-done((bf16[2,4,2,4,64,128]{5,4,3,2,1,0:T(8,128)(2,1)S(1)}, bf16[2,4,2,4,64,128]{5,4,3,2,1,0:T(8,128)(2,1)S(1)}, u32[]{:S(2)}, u32[]{:S(2)}) %collective-permute-start.22) | collective-permute-done | bytes 1048608 | tf_op jit(solution)/shard_map/ppermute | solution.py:401
  137.5 4.9 %correlate_tiles.7 = (f32[2,8,5,256,256]{4,3,2,1,0:T(8,128)}, f32[8,128]{1,0:T(8,128)}) custom-call(s32[11]{0:T(128)S(1)} %pad_add_fusion.rest_7_.rest_4_.rest_6_.table_ref, bf16[2,4,2,4,64,128]{5,4,3,2,1,0:T(8,128)(2,1)S(1)} %pair_blocks.1.low_ref, ...), custom_call_target="tpu_custom_call", output_to_operand_aliasing={{0}: (3, {})} | custom-call | tf_op jit(solution)/shard_map/correlate_tiles/pallas_call | solution.py:360
  (12 shorter events, 0.0 us)
Async XLA Ops:
  0.1 1.6 %copy-start = (bf16[2,2048,256]{2,1,0:T(8,128)(2,1)S(1)}, bf16[2,2048,256]{2,1,0:T(8,128)(2,1)}, u32[]{:S(2)}) copy-start(bf16[2,2048,256]{2,1,0:T(8,128)(2,1)} %v_ref.1) | copy-start | bytes 6291460
  4.8 18.2 %collective-permute-start = (bf16[2,64,2048]{2,1,0:T(8,128)(2,1)}, bf16[2,64,2048]{2,1,0:T(8,128)(2,1)S(1)}, u32[]{:S(2)}, u32[]{:S(2)}) collective-permute-start(bf16[2,64,2048]{2,1,0:T(8,128)(2,1)} %get-tuple-element.50), channel_id=1, source_target_pairs={{0,4},{4,8},{8,12},{12,0},{1,5},{5,9},{9,13},{13,1},{2,6},{6,10},{... | collective-permute-start | bytes 1572872 | tf_op jit(solution)/shard_map/ppermute | solution.py:394
  7.8 36.8 %collective-permute-start.1 = (bf16[2,64,2048]{2,1,0:T(8,128)(2,1)S(1)}, bf16[2,64,2048]{2,1,0:T(8,128)(2,1)S(1)}, u32[]{:S(2)}, u32[]{:S(2)}) collective-permute-start(bf16[2,64,2048]{2,1,0:T(8,128)(2,1)S(1)} %get-tuple-element.51), channel_id=1, source_target_pairs={{0,8},{4,12},{8,0},{12,4},{1,9},{5,13},{9,1},{13,5},{2,10},{6,14},... | collective-permute-start | bytes 1572872 | tf_op jit(solution)/shard_map/ppermute | solution.py:394
  10.4 34.2 %collective-permute-start.2 = (bf16[2,64,2048]{2,1,0:T(8,128)(2,1)S(1)}, bf16[2,64,2048]{2,1,0:T(8,128)(2,1)S(1)}, u32[]{:S(2)}, u32[]{:S(2)}) collective-permute-start(bf16[2,64,2048]{2,1,0:T(8,128)(2,1)S(1)} %get-tuple-element.52), channel_id=1, source_target_pairs={{0,12},{4,0},{8,4},{12,8},{1,13},{5,1},{9,5},{13,9},{2,14},{6,2},{... | collective-permute-start | bytes 1572872 | tf_op jit(solution)/shard_map/ppermute | solution.py:394
  18.5 1.4 copy-start.1
  19.9 0.7 copy-start.2
  51.6 16.9 %collective-permute-start.12 = (bf16[2,4,64,128]{3,2,1,0:T(8,128)(2,1)S(1)}, bf16[2,4,64,128]{3,2,1,0:T(8,128)(2,1)S(1)}, u32[]{:S(2)}, u32[]{:S(2)}) collective-permute-start(bf16[2,4,64,128]{3,2,1,0:T(8,128)(2,1)S(1)} %get-tuple-element.77), channel_id=1, source_target_pairs={{0,4},{4,8},{8,12},{12,0},{1,5},{5,9},{9,13},{13,1},{2,6},{6,10},{... | collective-permute-start | bytes 393224 | tf_op jit(solution)/shard_map/ppermute | solution.py:394
  63.4 9.7 %collective-permute-start.13 = (bf16[2,4,64,128]{3,2,1,0:T(8,128)(2,1)S(1)}, bf16[2,4,64,128]{3,2,1,0:T(8,128)(2,1)S(1)}, u32[]{:S(2)}, u32[]{:S(2)}) collective-permute-start(bf16[2,4,64,128]{3,2,1,0:T(8,128)(2,1)S(1)} %get-tuple-element.78), channel_id=1, source_target_pairs={{0,8},{4,12},{8,0},{12,4},{1,9},{5,13},{9,1},{13,5},{2,10},{6,14},... | collective-permute-start | bytes 393224 | tf_op jit(solution)/shard_map/ppermute | solution.py:394
  65.0 8.1 %collective-permute-start.14 = (bf16[2,4,64,128]{3,2,1,0:T(8,128)(2,1)S(1)}, bf16[2,4,64,128]{3,2,1,0:T(8,128)(2,1)S(1)}, u32[]{:S(2)}, u32[]{:S(2)}) collective-permute-start(bf16[2,4,64,128]{3,2,1,0:T(8,128)(2,1)S(1)} %get-tuple-element.79), channel_id=1, source_target_pairs={{0,12},{4,0},{8,4},{12,8},{1,13},{5,1},{9,5},{13,9},{2,14},{6,2},{... | collective-permute-start | bytes 393224 | tf_op jit(solution)/shard_map/ppermute | solution.py:394
  73.6 15.1 %collective-permute-start.15 = (bf16[4,2,4,64,128]{4,3,2,1,0:T(8,128)(2,1)S(1)}, bf16[4,2,4,64,128]{4,3,2,1,0:T(8,128)(2,1)S(1)}, u32[]{:S(2)}, u32[]{:S(2)}) collective-permute-start(bf16[4,2,4,64,128]{4,3,2,1,0:T(8,128)(2,1)S(1)} %join_pieces.4.rest_4_), channel_id=1, source_target_pairs={{0,2},{1,3},{2,0},{3,1},{4,6},{5,7},{6,4},{7,5},{8,10},{9,11},{10,... | collective-permute-start | bytes 1572872 | tf_op jit(solution)/shard_map/ppermute | solution.py:401
  75.2 9.3 %collective-permute-start.3 = (bf16[2,4,64,128]{3,2,1,0:T(8,128)(2,1)S(1)}, bf16[2,4,64,128]{3,2,1,0:T(8,128)(2,1)S(1)}, u32[]{:S(2)}, u32[]{:S(2)}) collective-permute-start(bf16[2,4,64,128]{3,2,1,0:T(8,128)(2,1)S(1)} %get-tuple-element.65), channel_id=1, source_target_pairs={{0,4},{4,8},{8,12},{12,0},{1,5},{5,9},{9,13},{13,1},{2,6},{6,10},{... | collective-permute-start | bytes 393224 | tf_op jit(solution)/shard_map/ppermute | solution.py:394
  78.5 10.1 %collective-permute-start.4 = (bf16[2,4,64,128]{3,2,1,0:T(8,128)(2,1)S(1)}, bf16[2,4,64,128]{3,2,1,0:T(8,128)(2,1)S(1)}, u32[]{:S(2)}, u32[]{:S(2)}) collective-permute-start(bf16[2,4,64,128]{3,2,1,0:T(8,128)(2,1)S(1)} %get-tuple-element.66), channel_id=1, source_target_pairs={{0,8},{4,12},{8,0},{12,4},{1,9},{5,13},{9,1},{13,5},{2,10},{6,14},... | collective-permute-start | bytes 393224 | tf_op jit(solution)/shard_map/ppermute | solution.py:394
  80.5 8.1 %collective-permute-start.5 = (bf16[2,4,64,128]{3,2,1,0:T(8,128)(2,1)S(1)}, bf16[2,4,64,128]{3,2,1,0:T(8,128)(2,1)S(1)}, u32[]{:S(2)}, u32[]{:S(2)}) collective-permute-start(bf16[2,4,64,128]{3,2,1,0:T(8,128)(2,1)S(1)} %get-tuple-element.67), channel_id=1, source_target_pairs={{0,12},{4,0},{8,4},{12,8},{1,13},{5,1},{9,5},{13,9},{2,14},{6,2},{... | collective-permute-start | bytes 393224 | tf_op jit(solution)/shard_map/ppermute | solution.py:394
  89.3 6.2 %collective-permute-start.17 = (bf16[2,4,2,4,64,128]{5,4,3,2,1,0:T(8,128)(2,1)S(1)}, bf16[2,4,2,4,64,128]{5,4,3,2,1,0:T(8,128)(2,1)S(1)}, u32[]{:S(2)}, u32[]{:S(2)}) collective-permute-start(bf16[2,4,2,4,64,128]{5,4,3,2,1,0:T(8,128)(2,1)S(1)} %get-tuple-element.81.low_ref), channel_id=1, source_target_pairs={{0,1},{1,0},{2,3},{3,2},{4,5},{5,4},{6,7},{7,6},{8,9},{9,8},{10,11... | collective-permute-start | bytes 3145736 | tf_op jit(solution)/shard_map/ppermute | solution.py:401
  89.4 14.3 %collective-permute-start.16 = (bf16[4,2,4,64,128]{4,3,2,1,0:T(8,128)(2,1)S(1)}, bf16[4,2,4,64,128]{4,3,2,1,0:T(8,128)(2,1)S(1)}, u32[]{:S(2)}, u32[]{:S(2)}) collective-permute-start(bf16[4,2,4,64,128]{4,3,2,1,0:T(8,128)(2,1)S(1)} %get-tuple-element.80.rest_4_), channel_id=1, source_target_pairs={{0,2},{1,3},{2,0},{3,1},{4,6},{5,7},{6,4},{7,5},{8,10},{9,11},{10,... | collective-permute-start | bytes 1572872 | tf_op jit(solution)/shard_map/ppermute | solution.py:401
  90.0 9.8 %collective-permute-start.6 = (bf16[2,4,64,128]{3,2,1,0:T(8,128)(2,1)S(1)}, bf16[2,4,64,128]{3,2,1,0:T(8,128)(2,1)S(1)}, u32[]{:S(2)}, u32[]{:S(2)}) collective-permute-start(bf16[2,4,64,128]{3,2,1,0:T(8,128)(2,1)S(1)} %get-tuple-element.69), channel_id=1, source_target_pairs={{0,4},{4,8},{8,12},{12,0},{1,5},{5,9},{9,13},{13,1},{2,6},{6,10},{... | collective-permute-start | bytes 393224 | tf_op jit(solution)/shard_map/ppermute | solution.py:394
  93.2 10.5 %collective-permute-start.7 = (bf16[2,4,64,128]{3,2,1,0:T(8,128)(2,1)S(1)}, bf16[2,4,64,128]{3,2,1,0:T(8,128)(2,1)S(1)}, u32[]{:S(2)}, u32[]{:S(2)}) collective-permute-start(bf16[2,4,64,128]{3,2,1,0:T(8,128)(2,1)S(1)} %get-tuple-element.70), channel_id=1, source_target_pairs={{0,8},{4,12},{8,0},{12,4},{1,9},{5,13},{9,1},{13,5},{2,10},{6,14},... | collective-permute-start | bytes 393224 | tf_op jit(solution)/shard_map/ppermute | solution.py:394
  94.7 9.0 %collective-permute-start.8 = (bf16[2,4,64,128]{3,2,1,0:T(8,128)(2,1)S(1)}, bf16[2,4,64,128]{3,2,1,0:T(8,128)(2,1)S(1)}, u32[]{:S(2)}, u32[]{:S(2)}) collective-permute-start(bf16[2,4,64,128]{3,2,1,0:T(8,128)(2,1)S(1)} %get-tuple-element.71), channel_id=1, source_target_pairs={{0,12},{4,0},{8,4},{12,8},{1,13},{5,1},{9,5},{13,9},{2,14},{6,2},{... | collective-permute-start | bytes 393224 | tf_op jit(solution)/shard_map/ppermute | solution.py:394
  104.4 7.1 %collective-permute-start.19 = (bf16[2,4,2,4,64,128]{5,4,3,2,1,0:T(8,128)(2,1)S(1)}, bf16[2,4,2,4,64,128]{5,4,3,2,1,0:T(8,128)(2,1)S(1)}, u32[]{:S(2)}, u32[]{:S(2)}) collective-permute-start(bf16[2,4,2,4,64,128]{5,4,3,2,1,0:T(8,128)(2,1)S(1)} %get-tuple-element.84.low_ref), channel_id=1, source_target_pairs={{0,1},{1,0},{2,3},{3,2},{4,5},{5,4},{6,7},{7,6},{8,9},{9,8},{10,11... | collective-permute-start | bytes 3145736 | tf_op jit(solution)/shard_map/ppermute | solution.py:401
  104.5 15.1 %collective-permute-start.18 = (bf16[4,2,4,64,128]{4,3,2,1,0:T(8,128)(2,1)S(1)}, bf16[4,2,4,64,128]{4,3,2,1,0:T(8,128)(2,1)S(1)}, u32[]{:S(2)}, u32[]{:S(2)}) collective-permute-start(bf16[4,2,4,64,128]{4,3,2,1,0:T(8,128)(2,1)S(1)} %get-tuple-element.83.rest_4_), channel_id=1, source_target_pairs={{0,2},{1,3},{2,0},{3,1},{4,6},{5,7},{6,4},{7,5},{8,10},{9,11},{10,... | collective-permute-start | bytes 1572872 | tf_op jit(solution)/shard_map/ppermute | solution.py:401
  105.8 9.9 %collective-permute-start.9 = (bf16[2,4,64,128]{3,2,1,0:T(8,128)(2,1)S(1)}, bf16[2,4,64,128]{3,2,1,0:T(8,128)(2,1)S(1)}, u32[]{:S(2)}, u32[]{:S(2)}) collective-permute-start(bf16[2,4,64,128]{3,2,1,0:T(8,128)(2,1)S(1)} %get-tuple-element.73), channel_id=1, source_target_pairs={{0,4},{4,8},{8,12},{12,0},{1,5},{5,9},{9,13},{13,1},{2,6},{6,10},{... | collective-permute-start | bytes 393224 | tf_op jit(solution)/shard_map/ppermute | solution.py:394
  109.1 10.5 %collective-permute-start.10 = (bf16[2,4,64,128]{3,2,1,0:T(8,128)(2,1)S(1)}, bf16[2,4,64,128]{3,2,1,0:T(8,128)(2,1)S(1)}, u32[]{:S(2)}, u32[]{:S(2)}) collective-permute-start(bf16[2,4,64,128]{3,2,1,0:T(8,128)(2,1)S(1)} %get-tuple-element.74), channel_id=1, source_target_pairs={{0,8},{4,12},{8,0},{12,4},{1,9},{5,13},{9,1},{13,5},{2,10},{6,14},... | collective-permute-start | bytes 393224 | tf_op jit(solution)/shard_map/ppermute | solution.py:394
  110.6 9.0 %collective-permute-start.11 = (bf16[2,4,64,128]{3,2,1,0:T(8,128)(2,1)S(1)}, bf16[2,4,64,128]{3,2,1,0:T(8,128)(2,1)S(1)}, u32[]{:S(2)}, u32[]{:S(2)}) collective-permute-start(bf16[2,4,64,128]{3,2,1,0:T(8,128)(2,1)S(1)} %get-tuple-element.75), channel_id=1, source_target_pairs={{0,12},{4,0},{8,4},{12,8},{1,13},{5,1},{9,5},{13,9},{2,14},{6,2},{... | collective-permute-start | bytes 393224 | tf_op jit(solution)/shard_map/ppermute | solution.py:394
  120.3 2.7 %collective-permute-start.21 = (bf16[2,4,2,4,64,128]{5,4,3,2,1,0:T(8,128)(2,1)S(1)}, bf16[2,4,2,4,64,128]{5,4,3,2,1,0:T(8,128)(2,1)S(1)}, u32[]{:S(2)}, u32[]{:S(2)}) collective-permute-start(bf16[2,4,2,4,64,128]{5,4,3,2,1,0:T(8,128)(2,1)S(1)} %get-tuple-element.88.low_ref), channel_id=1, source_target_pairs={{0,1},{1,0},{2,3},{3,2},{4,5},{5,4},{6,7},{7,6},{8,9},{9,8},{10,11... | collective-permute-start | bytes 3145736 | tf_op jit(solution)/shard_map/ppermute | solution.py:401
  120.4 14.3 %collective-permute-start.20 = (bf16[4,2,4,64,128]{4,3,2,1,0:T(8,128)(2,1)S(1)}, bf16[4,2,4,64,128]{4,3,2,1,0:T(8,128)(2,1)S(1)}, u32[]{:S(2)}, u32[]{:S(2)}) collective-permute-start(bf16[4,2,4,64,128]{4,3,2,1,0:T(8,128)(2,1)S(1)} %get-tuple-element.87.own_ref), channel_id=1, source_target_pairs={{0,2},{1,3},{2,0},{3,1},{4,6},{5,7},{6,4},{7,5},{8,10},{9,11},{10,... | collective-permute-start | bytes 1572872 | tf_op jit(solution)/shard_map/ppermute | solution.py:401
  134.8 2.7 %collective-permute-start.22 = (bf16[2,4,2,4,64,128]{5,4,3,2,1,0:T(8,128)(2,1)S(1)}, bf16[2,4,2,4,64,128]{5,4,3,2,1,0:T(8,128)(2,1)S(1)}, u32[]{:S(2)}, u32[]{:S(2)}) collective-permute-start(bf16[2,4,2,4,64,128]{5,4,3,2,1,0:T(8,128)(2,1)S(1)} %pair_blocks.1.low_ref), channel_id=1, source_target_pairs={{0,1},{1,0},{2,3},{3,2},{4,5},{5,4},{6,7},{7,6},{8,9},{9,8},{10,11... | collective-permute-start | bytes 3145736 | tf_op jit(solution)/shard_map/ppermute | solution.py:401
where the time goes:
time: 144 us; the launch traced here: 143 us
  waiting for transfers between devices  57.1 us (40%)
  starting transfers between devices  42.3 us (29%)
  Pallas kernels  30.5 us (21%)
  local copies, waits for them, and re-layouts  7.63 us (5%)
  other arithmetic  4.61 us (3%)
    ppermute x15, waiting for transfers between devices, spread(): lax.ppermute(pieces[d], 'ft', [(i, (i + d) % count) for i in range(count)])  44.9 us
    ppermute x15, starting transfers between devices, spread(): lax.ppermute(pieces[d], 'ft', [(i, (i + d) % count) for i in range(count)])  37.9 us
    pallas_call x4, Pallas kernels, correlate(): pl.pallas_call(functools.partial(correlate_kernel, chunks, 1.0 / (AVG * s...  17.7 us
    ppermute x8, waiting for transfers between devices, exchange(): return lax.ppermute(own, 'bl', [(i, i ^ bit) for i in range(count)])  12.3 us
    pallas_call x1, Pallas kernels, transform_all(): pl.pallas_call(functools.partial(transform_kernel, radix, dests, units),...  7.01 us
    ppermute x8, starting transfers between devices, exchange(): return lax.ppermute(own, 'bl', [(i, i ^ bit) for i in range(count)])  4.37 us
    reshape x2, local copies, waits for them, and re-layouts, per_device_kernels(): coef_table = coefs.reshape(taps, MXU, radix).transpose(0, 2, 1)  3.92 us
    unnamed x6, local copies, waits for them, and re-layouts  3.71 us
  transfers between devices with their start and end apart: 23, of which 13 were waited for; matrix products, arithmetic and copies ran while one was open for 6% of the time, Pallas kernels for 9%

commit v1 on v0

--- a/solution.py
+++ b/solution.py
@@ -76,35 +76,38 @@
     o_refs, (wide, turned) = rest[:-2], rest[-2:]
     dests, rows, samples = turned.shape
     inner = samples // radix
-    wide[...] = v_ref[0].astype(jnp.float32)
-    for phase in range(radix):
-        part = wide[pl.ds(phase, inner, stride=radix), :].T.astype(jnp.bfloat16)
-        for dest in range(dests):
-            turned[dest, :, phase * inner : (phase + 1) * inner] = part[
-                dest * rows : (dest + 1) * rows
-            ]
-    for shift in range(dests):
-        o_refs[shift][0] = turned[place_ref[shift]]
+    for part in range(2):
+        for chunk in range(v_ref.shape[2] // LANES):
+            wide[...] = v_ref[part, :, chunk * LANES : (chunk + 1) * LANES].astype(jnp.float32)
+            for phase in range(radix):
+                here = wide[pl.ds(phase, inner, stride=radix), :].T.astype(jnp.bfloat16)
+                for dest in range(dests):
+                    turned[dest, :, phase * inner : (phase + 1) * inner] = here[
+                        dest * rows : (dest + 1) * rows
+                    ]
+            for shift in range(dests):
+                o_refs[shift][part, chunk * rows : (chunk + 1) * rows] = turned[place_ref[shift]]
 
 
 def pack(voltages, place, dests, radix):
     _, samples, inputs = voltages.shape
     chunks = inputs // LANES
     rows = LANES // dests
+    vmem = pl.BlockSpec(memory_space=pltpu.VMEM)
     return pl.pallas_call(
         functools.partial(pack_kernel, radix),
         grid_spec=pltpu.PrefetchScalarGridSpec(
             num_scalar_prefetch=1,
-            grid=(2, chunks),
-            in_specs=[pl.BlockSpec((1, samples, LANES), lambda p, h, t: (p, 0, h))],
-            out_specs=[pl.BlockSpec((1, rows, samples), lambda p, h, t: (p, h, 0))] * dests,
+            grid=(),
+            in_specs=[vmem],
+            out_specs=[vmem] * dests,
             scratch_shapes=[
                 pltpu.VMEM((samples, LANES), jnp.float32),
                 pltpu.VMEM((dests, rows, samples), jnp.bfloat16),
             ],
         ),
         out_shape=[jax.ShapeDtypeStruct((2, chunks * rows, samples), jnp.bfloat16)] * dests,
-        compiler_params=pltpu.CompilerParams(vmem_limit_bytes=VMEM_BYTES),
+        compiler_params=pltpu.CompilerParams(vmem_limit_bytes=VMEM_BYTES // 2),
         name="pack_inputs",
     )(place, voltages)
 
@@ -127,22 +130,16 @@
     )(*tables)
 
 
-def transform_kernel(radix, dests, units, place_ref, *rest):
-    v_refs = rest[:dests]
-    c_ref, tw_ref, g_ref = rest[dests : dests + 3]
-    out_refs = rest[dests + 4 : -4]
-    held, split, prod, made = rest[-4:]
+def filter_blocks(place_ref, v_refs, c_ref, held, split):
     spectra, _, rows, samples = held.shape
-    taps = c_ref.shape[0]
-    inner = samples // radix
-    group = spectra * rows
-    for shift in range(dests):
-        held[place_ref[dests + shift]] = v_refs[shift][...]
+    taps, radix, inner = c_ref.shape
+    for shift in range(len(v_refs)):
+        held[place_ref[len(v_refs) + shift]] = v_refs[shift][...]
 
     @pl.loop(0, radix)
     def _(phase):
         lane0 = pl.multiple_of(phase * inner, inner)
-        row0 = pl.multiple_of(phase * group, group)
+        row0 = pl.multiple_of(phase * spectra * rows, spectra * rows)
         for part in range(2):
             for sub in range(0, rows, ROWS16):
                 blocks = [
@@ -160,83 +157,90 @@
                     split[at, part * inner : (part + 1) * inner] = high
                     split[at, (2 + part) * inner : (3 + part) * inner] = low
 
+
+def transform_lanes(place_ref, split, tw_ref, g_ref, prod, made, out_refs):
+    dests, halves, _, spectra, rows, _ = made.shape
+    radix = tw_ref.shape[1]
+    group = spectra * rows
+    depth = split.shape[1] // 2
+
     @pl.loop(0, radix // 2)
     def _(pair):
         at = pl.ds(pl.multiple_of(pair * 2 * group, 2 * group), 2 * group)
-        high = split[at, : 2 * inner]
-        line = jnp.concatenate([high, split[at, 2 * inner :], high], axis=1)
+        high = split[at, :depth]
+        line = jnp.concatenate([high, split[at, depth:], high], axis=1)
         prod[at, :] = jnp.dot(line, g_ref[...], preferred_element_type=jnp.float32)
-
-    halves = radix // dests
-    lane_cuts = inner // LANES
 
     @pl.loop(0, spectra)
     def _(s):
         for sub in range(0, rows, ROWS16):
-            for cut in range(lane_cuts):
-                lane = cut * LANES
-                parts = []
-                for phase in range(radix):
-                    at = pl.ds(pl.multiple_of(phase * group + s * rows + sub, ROWS16), ROWS16)
-                    yr = prod[at, lane : lane + LANES]
-                    yi = prod[at, inner + lane : inner + lane + LANES]
-                    cos_here = tw_ref[0, phase : phase + 1, lane : lane + LANES]
-                    sin_here = tw_ref[1, phase : phase + 1, lane : lane + LANES]
-                    if phase == 0:
-                        parts.append((yr * cos_here, yi * cos_here))
-                    else:
-                        parts.append(
-                            (yr * cos_here + yi * sin_here, yi * cos_here - yr * sin_here)
-                        )
-                for step, pair in enumerate(butterflies(parts)):
-                    unit = step % halves * lane_cuts + cut
-                    for part in range(2):
-                        made[step // halves, unit, part, s, sub : sub + ROWS16, :] = pair[
-                            part
-                        ].astype(jnp.bfloat16)
+            parts = []
+            for phase in range(radix):
+                at = pl.ds(pl.multiple_of(phase * group + s * rows + sub, ROWS16), ROWS16)
+                yr, yi = prod[at, :LANES], prod[at, LANES:]
+                cos_here = tw_ref[0, phase : phase + 1, :]
+                sin_here = tw_ref[1, phase : phase + 1, :]
+                if phase == 0:
+                    parts.append((yr * cos_here, yi * cos_here))
+                else:
+                    parts.append((yr * cos_here + yi * sin_here, yi * cos_here - yr * sin_here))
+            for step, pair in enumerate(butterflies(parts)):
+                for part in range(2):
+                    made[step // halves, step % halves, part, s, sub : sub + ROWS16, :] = pair[
+                        part
+                    ].astype(jnp.bfloat16)
 
     for shift in range(dests):
-        for unit in range(units):
-            out_refs[unit * dests + shift][...] = made[place_ref[shift], unit]
-
-
-def transform_all(blocks, place, tables, radix, after):
-    dests = len(blocks)
-    _, rows, samples = blocks[0].shape
-    spectra = dests
+        for half in range(halves):
+            out_refs[half * dests + shift][...] = made[place_ref[shift], half]
+
+
+def transform_cut(source, place, coef_table, tables, cut, sizes, after):
+    dests, spectra, rows, samples, radix = sizes
     inner = samples // radix
-    units = samples // dests // LANES
-    anywhere = pl.BlockSpec(memory_space=pl.ANY)
+    halves = radix // dests
+    total = radix * spectra * rows
+    begins = coef_table is not None
     vmem = pl.BlockSpec(memory_space=pltpu.VMEM)
-    total = radix * spectra * rows
+
+    def kernel(place_ref, *rest):
+        if begins:
+            v_refs, (c_ref, tw_ref, g_ref) = rest[:dests], rest[dests : dests + 3]
+            out_refs, (split, held, prod, made) = rest[dests + 4 : -4], rest[-4:]
+            filter_blocks(place_ref, v_refs, c_ref, held, split)
+        else:
+            split, tw_ref, g_ref = rest[:3]
+            out_refs, (prod, made) = rest[4:-2], rest[-2:]
+        transform_lanes(place_ref, split, tw_ref, g_ref, prod, made, out_refs)
+
+    scratch = [
+        pltpu.VMEM((total, 2 * LANES), jnp.float32),
+        pltpu.VMEM((dests, halves, 2, spectra, rows, LANES), jnp.bfloat16),
+    ]
+    shapes = [jax.ShapeDtypeStruct((2, spectra, rows, LANES), jnp.bfloat16)] * (halves * dests)
+    if begins:
+        scratch = [pltpu.VMEM((spectra, 2, rows, samples), jnp.bfloat16)] + scratch
+        shapes = shapes + [jax.ShapeDtypeStruct((total, 4 * inner), jnp.bfloat16)]
+    args = [*source, coef_table] if begins else [source]
+    args += [tables[2 * cut], tables[2 * cut + 1]]
     made = pl.pallas_call(
-        functools.partial(transform_kernel, radix, dests, units),
+        kernel,
         grid_spec=pltpu.PrefetchScalarGridSpec(
             num_scalar_prefetch=1,
             grid=(),
-            in_specs=[vmem] * (dests + 3) + [anywhere],
-            out_specs=[vmem] * (units * dests),
-            scratch_shapes=[
-                pltpu.VMEM((spectra, 2, rows, samples), jnp.bfloat16),
-                pltpu.VMEM((total, 4 * inner), jnp.bfloat16),
-                pltpu.VMEM((total, 2 * inner), jnp.float32),
-                pltpu.VMEM((dests, units, 2, spectra, rows, LANES), jnp.bfloat16),
-            ],
+            in_specs=[vmem] * len(args) + [pl.BlockSpec(memory_space=pl.ANY)],
+            out_specs=[vmem] * len(shapes),
+            scratch_shapes=scratch,
         ),
-        out_shape=[jax.ShapeDtypeStruct((2, spectra, rows, LANES), jnp.bfloat16)]
-        * (units * dests),
+        out_shape=shapes,
         cost_estimate=pl.CostEstimate(
-            flops=3 * 2 * total * 4 * inner * inner, bytes_accessed=6 << 20, transcendentals=0
+            flops=3 * 2 * total * 4 * inner * LANES, bytes_accessed=6 << 20, transcendentals=0
         ),
-        compiler_params=pltpu.CompilerParams(vmem_limit_bytes=VMEM_BYTES),
-        name="filter_transform",
-    )(
-        place,
-        *blocks,
-        *tables,
-        after,
-    )
-    return [made[unit * dests : (unit + 1) * dests] for unit in range(units)]
+        compiler_params=pltpu.CompilerParams(vmem_limit_bytes=VMEM_BYTES // 2),
+        name="filter_transform" if begins else "transform_rest",
+    )(place, *args, after)
+    units = [made[half * dests : (half + 1) * dests] for half in range(halves)]
+    return units, made[-1]
 
 
 def join(pieces, place, before, after):
@@ -346,7 +350,7 @@
             copy_out(empty, c, slot).wait()
 
 
-def correlate(table, gathered, unit, units, chunks, slots, vis):
+def correlate(table, gathered, first, channels, chunks, slots, vis):
     half, senders, _, spectra, rows, lanes = gathered[0].shape
     coarse = lanes // AVG
     side = senders * rows
@@ -358,7 +362,7 @@
         args.append(vis)
         aliases = {len(args) - 1: 0}
     return pl.pallas_call(
-        functools.partial(correlate_kernel, chunks, 1.0 / (AVG * spectra), unit * coarse),
+        functools.partial(correlate_kernel, chunks, 1.0 / (AVG * spectra), first),
         grid_spec=pltpu.PrefetchScalarGridSpec(
             num_scalar_prefetch=1,
             grid=(),
@@ -372,7 +376,7 @@
             ],
         ),
         out_shape=[
-            jax.ShapeDtypeStruct((2, units * coarse, slots, side, side), jnp.float32),
+            jax.ShapeDtypeStruct((2, channels, slots, side, side), jnp.float32),
             jax.ShapeDtypeStruct((8, LANES), jnp.float32),
         ],
         input_output_aliases=aliases,
@@ -477,9 +481,23 @@
     coef_table = coefs.reshape(taps, MXU, radix).transpose(0, 2, 1)
     place = places(dests)
     table, slot_cap = tile_tables(block_ids, tile_owner)
-    tables = stage(coef_table, twiddle_tables(radix, MXU), matrix_tables(MXU))
+    matrix, twiddle = matrix_tables(MXU), twiddle_tables(radix, MXU)
+    cuts = MXU // LANES
+    tables = []
+    for cut in range(cuts):
+        at = slice(cut * LANES, (cut + 1) * LANES)
+        tables.append(np.ascontiguousarray(twiddle[:, :, at]))
+        tables.append(np.concatenate([matrix[:, :MXU][:, at], matrix[:, MXU:][:, at]], axis=1))
+    coef_table, *tables = stage(coef_table, *tables)
     arrived = spread(pack(voltages, place, dests, radix))
-    made = transform_all(arrived, place, tables, radix, table)
+    _, rows, samples = arrived[0].shape
+    sizes = (dests, dests, rows, samples, radix)
+    made, split = transform_cut(arrived, place, coef_table, tables, 0, sizes, table)
+    firsts = [table]
+    for cut in range(1, cuts):
+        more, _ = transform_cut(split, place, None, tables, cut, sizes, table)
+        made = made + more
+        firsts.append(more[0][0])
     half = lax.axis_size("bl") // 2
     units = len(made)
     own, other, arrived, tokens, vis = None, None, None, [], None
@@ -494,13 +512,17 @@
             if unit > 0:
                 own, held = join(arrived, place, (own, other), after)
             else:
-                (own,) = join(arrived, place, (), after)
+                (own,) = join(arrived, place, (), firsts[-1])
             other = exchange(own, half)
         else:
             held = pair(own, other, tokens[-1])
         if unit > 0:
             gathered = gather_blocks(held, table)
-            vis, token = correlate(table, gathered, unit - 1, units, chunks, slot_cap, vis)
+            cut, part = divmod(unit - 1, radix // dests)
+            first = (part * MXU + cut * LANES) // AVG
+            vis, token = correlate(
+                table, gathered, first, units * LANES // AVG, chunks, slot_cap, vis
+            )
             tokens.append(token)
     return vis
 

time: 144 us -> 142 us (0.986)
  waiting for transfers between devices: 57.1 us -> 47.4 us
  Pallas kernels: 30.5 us -> 37.5 us
  local copies, waits for them, and re-layouts: 7.63 us -> 9.17 us
    ppermute x15, waiting for transfers between devices: 44.9 us -> 36.9 us  [spread(): lax.ppermute(pieces[d], 'ft', [(i, (i + d) % count) for i in range(count)])]
    pallas_call x4, Pallas kernels: 17.7 us -> 23.9 us  [correlate(): pl.pallas_call(functools.partial(correlate_kernel, chunks, 1.0 / (AVG * s...]
    ppermute x8, waiting for transfers between devices: 12.3 us -> 10.5 us  [exchange(): return lax.ppermute(own, 'bl', [(i, i ^ bit) for i in range(count)])]
    unnamed x6 -> x10, local copies, waits for them, and re-layouts: 3.71 us -> 5.25 us
    pallas_call x1 -> x2, Pallas kernels: 7.01 us -> 8.24 us  [transform_cut(): pl.pallas_call(kernel, grid_spec=pltpu.PrefetchScalarGridSpec(num_scalar_...]
  transfers between devices with their start and end apart: 23 -> 23, of which waited for: 13 -> 11; matrix products, arithmetic and copies ran while one was open for 6% -> 6% of each run, Pallas kernels for 9% -> 15%
where the time goes in v1:
time: 142 us; the launch traced here: 141 us
  waiting for transfers between devices  47.4 us (33%)
  starting transfers between devices  42.3 us (30%)
  Pallas kernels  37.5 us (26%)
  local copies, waits for them, and re-layouts  9.17 us (6%)
  other arithmetic  4.61 us (3%)
    ppermute x15, starting transfers between devices, spread(): lax.ppermute(pieces[d], 'ft', [(i, (i + d) % count) for i in range(count)])  37.9 us
    ppermute x15, waiting for transfers between devices, spread(): lax.ppermute(pieces[d], 'ft', [(i, (i + d) % count) for i in range(count)])  36.9 us
    pallas_call x4, Pallas kernels, correlate(): pl.pallas_call(functools.partial(correlate_kernel, chunks, 1.0 / (AVG * s...  23.9 us
    ppermute x8, waiting for transfers between devices, exchange(): return lax.ppermute(own, 'bl', [(i, i ^ bit) for i in range(count)])  10.5 us
    pallas_call x2, Pallas kernels, transform_cut(): pl.pallas_call(kernel, grid_spec=pltpu.PrefetchScalarGridSpec(num_scalar_...  8.24 us
    unnamed x10, local copies, waits for them, and re-layouts  5.25 us
    ppermute x8, starting transfers between devices, exchange(): return lax.ppermute(own, 'bl', [(i, i ^ bit) for i in range(count)])  4.38 us
    reshape x2, local copies, waits for them, and re-layouts, per_device_kernels(): coef_table = coefs.reshape(taps, MXU, radix).transpose(0, 2, 1)  3.92 us
  transfers between devices with their start and end apart: 23, of which 11 were waited for; matrix products, arithmetic and copies ran while one was open for 6% of the time, Pallas kernels for 15%

profile of v1, /device:TPU:0, one launch (start us, length us, event | category | flops | bytes accessed | tf_op | source)
XLA Modules:
  0.0 141.4 jit_solution(15082450045990758229)
XLA Ops:
  0.0 0.1 pad_add_fusion.1.place_ref
  0.1 1.6 %copy-done = bf16[2,2048,256]{2,1,0:T(8,128)(2,1)S(1)} copy-done((bf16[2,2048,256]{2,1,0:T(8,128)(2,1)S(1)}, bf16[2,2048,256]{2,1,0:T(8,128)(2,1)}, u32[]{:S(2)}) %copy-start) | copy-done | bytes 2097176
  1.7 2.7 %pack_inputs.1 = (bf16[2,64,2048]{2,1,0:T(8,128)(2,1)S(1)}, bf16[2,64,2048]{2,1,0:T(8,128)(2,1)}, bf16[2,64,2048]{2,1,0:T(8,128)(2,1)S(1)}, bf16[2,64,2048]{2,1,0:T(8,128)(2,1)S(1)}) custom-call(s32[8]{0:T(128)S(1)} %pad_add_fusion.1.place_ref, bf16[2,2048,256]{2,1,0:T(8,128)(2,1)S(1)} %copy-done), custom_call_target="tpu_custom_call" | custom-call | tf_op jit(solution)/shard_map/pack_inputs/pallas_call | solution.py:97
  4.4 3.0 %collective-permute-start = (bf16[2,64,2048]{2,1,0:T(8,128)(2,1)}, bf16[2,64,2048]{2,1,0:T(8,128)(2,1)S(1)}, u32[]{:S(2)}, u32[]{:S(2)}) collective-permute-start(bf16[2,64,2048]{2,1,0:T(8,128)(2,1)} %get-tuple-element.53), channel_id=1, source_target_pairs={{0,4},{4,8},{8,12},{12,0},{1,5},{5,9},{9,13},{13,1},{2,6},{6,10},{... | collective-permute-start | bytes 1572872 | tf_op jit(solution)/shard_map/ppermute | solution.py:398
  7.4 2.6 %collective-permute-start.1 = (bf16[2,64,2048]{2,1,0:T(8,128)(2,1)S(1)}, bf16[2,64,2048]{2,1,0:T(8,128)(2,1)S(1)}, u32[]{:S(2)}, u32[]{:S(2)}) collective-permute-start(bf16[2,64,2048]{2,1,0:T(8,128)(2,1)S(1)} %get-tuple-element.54), channel_id=1, source_target_pairs={{0,8},{4,12},{8,0},{12,4},{1,9},{5,13},{9,1},{13,5},{2,10},{6,14},... | collective-permute-start | bytes 1572872 | tf_op jit(solution)/shard_map/ppermute | solution.py:398
  10.0 1.3 collective-permute-start.2
  11.3 0.8 fusion.1
  12.1 2.4 %reshape.11 = f32[8,256,8]{2,1,0:T(8,128)} reshape(f32[8,2048]{1,0:T(8,128)} %param.16) | data formatting | bytes 131072 | tf_op jit(solution)/shard_map/reshape | solution.py:481
  14.5 1.5 %copy.20 = f32[8,256,8]{1,2,0:T(8,128)S(1)} copy(f32[8,256,8]{2,1,0:T(8,128)} %reshape.11) | data formatting | bytes 131072 | tf_op jit(solution)/shard_map/reshape | solution.py:481
  16.0 0.7 broadcast_compare_fusion
  16.7 0.6 reduce_sum.69
  17.3 0.8 select_reduce_fusion.3
  18.1 1.1 copy-done.1
  19.2 1.1 copy-done.2
  20.4 0.7 copy-done.3
  21.0 0.7 copy-done.4
  21.7 0.1 stage_tables.1
  21.9 0.8 multiply_reduce_fusion
  22.7 0.2 select_reduce_fusion.1
  22.8 0.7 pad_add_fusion.rest_7_.rest_3_.rest_6_.table_ref
  23.6 0.0 collective-permute-done.rest_1_
  23.6 20.6 %collective-permute-done.1.rest_2_ = bf16[2,64,2048]{2,1,0:T(8,128)(2,1)S(1)} collective-permute-done((bf16[2,64,2048]{2,1,0:T(8,128)(2,1)S(1)}, bf16[2,64,2048]{2,1,0:T(8,128)(2,1)S(1)}, u32[]{:S(2)}, u32[]{:S(2)}) %collective-permute-start.1) | collective-permute-done | bytes 524320 | tf_op jit(solution)/shard_map/ppermute | solution.py:398
  44.2 0.0 collective-permute-done.2.rest_3_
  44.2 4.8 %filter_transform.1 = (bf16[2,4,64,128]{3,2,1,0:T(8,128)(2,1)S(1)}, bf16[2,4,64,128]{3,2,1,0:T(8,128)(2,1)S(1)}, bf16[2,4,64,128]{3,2,1,0:T(8,128)(2,1)S(1)}, bf...) custom-call(s32[8]{0:T(128)S(1)} %pad_add_fusion.1.place_ref, ...), custom_call_target="tpu_custom_call" | custom-call | flops 1610612736 | bytes 6291456 | tf_op jit(solution)/shard_map/filter_transform/pallas_call | solution.py:226
  49.0 11.8 %collective-permute-start.12 = (bf16[2,4,64,128]{3,2,1,0:T(8,128)(2,1)S(1)}, bf16[2,4,64,128]{3,2,1,0:T(8,128)(2,1)S(1)}, u32[]{:S(2)}, u32[]{:S(2)}) collective-permute-start(bf16[2,4,64,128]{3,2,1,0:T(8,128)(2,1)S(1)} %get-tuple-element.83), channel_id=1, source_target_pairs={{0,4},{4,8},{8,12},{12,0},{1,5},{5,9},{9,13},{13,1},{2,6},{6,10},{... | collective-permute-start | bytes 393224 | tf_op jit(solution)/shard_map/ppermute | solution.py:398
  60.7 1.6 %collective-permute-start.13 = (bf16[2,4,64,128]{3,2,1,0:T(8,128)(2,1)S(1)}, bf16[2,4,64,128]{3,2,1,0:T(8,128)(2,1)S(1)}, u32[]{:S(2)}, u32[]{:S(2)}) collective-permute-start(bf16[2,4,64,128]{3,2,1,0:T(8,128)(2,1)S(1)} %get-tuple-element.84), channel_id=1, source_target_pairs={{0,8},{4,12},{8,0},{12,4},{1,9},{5,13},{9,1},{13,5},{2,10},{6,14},... | collective-permute-start | bytes 393224 | tf_op jit(solution)/shard_map/ppermute | solution.py:398
  62.3 0.8 collective-permute-start.14
  63.2 3.4 %transform_rest.1 = (bf16[2,4,64,128]{3,2,1,0:T(8,128)(2,1)S(1)}, bf16[2,4,64,128]{3,2,1,0:T(8,128)(2,1)S(1)}, bf16[2,4,64,128]{3,2,1,0:T(8,128)(2,1)S(1)}, bf16...) custom-call(s32[8]{0:T(128)S(1)} %pad_add_fusion.1.place_ref, ...), custom_call_target="tpu_custom_call" | custom-call | flops 1610612736 | bytes 6291456 | tf_op jit(solution)/shard_map/transform_rest/pallas_call | solution.py:226
  66.6 3.8 %collective-permute-done.13.rest_2_ = bf16[2,4,64,128]{3,2,1,0:T(8,128)(2,1)S(1)} collective-permute-done((bf16[2,4,64,128]{3,2,1,0:T(8,128)(2,1)S(1)}, bf16[2,4,64,128]{3,2,1,0:T(8,128)(2,1)S(1)}, u32[]{:S(2)}, u32[]{:S(2)}) %collective-permute-start.13) | collective-permute-done | bytes 131104 | tf_op jit(solution)/shard_map/ppermute | solution.py:398
  70.4 0.6 join_pieces.4.rest_4_
  71.0 1.6 %collective-permute-start.15 = (bf16[4,2,4,64,128]{4,3,2,1,0:T(8,128)(2,1)S(1)}, bf16[4,2,4,64,128]{4,3,2,1,0:T(8,128)(2,1)S(1)}, u32[]{:S(2)}, u32[]{:S(2)}) collective-permute-start(bf16[4,2,4,64,128]{4,3,2,1,0:T(8,128)(2,1)S(1)} %join_pieces.4.rest_4_), channel_id=1, source_target_pairs={{0,2},{1,3},{2,0},{3,1},{4,6},{5,7},{6,4},{7,5},{8,10},{9,11},{10,... | collective-permute-start | bytes 1572872 | tf_op jit(solution)/shard_map/ppermute | solution.py:405
  72.6 3.3 %collective-permute-start.3 = (bf16[2,4,64,128]{3,2,1,0:T(8,128)(2,1)S(1)}, bf16[2,4,64,128]{3,2,1,0:T(8,128)(2,1)S(1)}, u32[]{:S(2)}, u32[]{:S(2)}) collective-permute-start(bf16[2,4,64,128]{3,2,1,0:T(8,128)(2,1)S(1)} %get-tuple-element.71), channel_id=1, source_target_pairs={{0,4},{4,8},{8,12},{12,0},{1,5},{5,9},{9,13},{13,1},{2,6},{6,10},{... | collective-permute-start | bytes 393224 | tf_op jit(solution)/shard_map/ppermute | solution.py:398
  75.8 2.1 %collective-permute-start.4 = (bf16[2,4,64,128]{3,2,1,0:T(8,128)(2,1)S(1)}, bf16[2,4,64,128]{3,2,1,0:T(8,128)(2,1)S(1)}, u32[]{:S(2)}, u32[]{:S(2)}) collective-permute-start(bf16[2,4,64,128]{3,2,1,0:T(8,128)(2,1)S(1)} %get-tuple-element.72), channel_id=1, source_target_pairs={{0,8},{4,12},{8,0},{12,4},{1,9},{5,13},{9,1},{13,5},{2,10},{6,14},... | collective-permute-start | bytes 393224 | tf_op jit(solution)/shard_map/ppermute | solution.py:398
  77.9 0.3 collective-permute-start.5
  78.2 3.6 %collective-permute-done.3.rest_1_ = bf16[2,4,64,128]{3,2,1,0:T(8,128)(2,1)S(1)} collective-permute-done((bf16[2,4,64,128]{3,2,1,0:T(8,128)(2,1)S(1)}, bf16[2,4,64,128]{3,2,1,0:T(8,128)(2,1)S(1)}, u32[]{:S(2)}, u32[]{:S(2)}) %collective-permute-start.3) | collective-permute-done | bytes 131104 | tf_op jit(solution)/shard_map/ppermute | solution.py:398
  81.8 4.1 %collective-permute-done.4.rest_2_ = bf16[2,4,64,128]{3,2,1,0:T(8,128)(2,1)S(1)} collective-permute-done((bf16[2,4,64,128]{3,2,1,0:T(8,128)(2,1)S(1)}, bf16[2,4,64,128]{3,2,1,0:T(8,128)(2,1)S(1)}, u32[]{:S(2)}, u32[]{:S(2)}) %collective-permute-start.4) | collective-permute-done | bytes 131104 | tf_op jit(solution)/shard_map/ppermute | solution.py:398
  85.9 0.1 collective-permute-done.5.rest_3_
  86.1 0.6 join_pieces.5
  86.7 0.1 collective-permute-start.17
  86.8 0.6 collective-permute-start.16
  87.4 3.1 %collective-permute-start.6 = (bf16[2,4,64,128]{3,2,1,0:T(8,128)(2,1)S(1)}, bf16[2,4,64,128]{3,2,1,0:T(8,128)(2,1)S(1)}, u32[]{:S(2)}, u32[]{:S(2)}) collective-permute-start(bf16[2,4,64,128]{3,2,1,0:T(8,128)(2,1)S(1)} %get-tuple-element.75), channel_id=1, source_target_pairs={{0,4},{4,8},{8,12},{12,0},{1,5},{5,9},{9,13},{13,1},{2,6},{6,10},{... | collective-permute-start | bytes 393224 | tf_op jit(solution)/shard_map/ppermute | solution.py:398
  90.5 1.5 %collective-permute-start.7 = (bf16[2,4,64,128]{3,2,1,0:T(8,128)(2,1)S(1)}, bf16[2,4,64,128]{3,2,1,0:T(8,128)(2,1)S(1)}, u32[]{:S(2)}, u32[]{:S(2)}) collective-permute-start(bf16[2,4,64,128]{3,2,1,0:T(8,128)(2,1)S(1)} %get-tuple-element.76), channel_id=1, source_target_pairs={{0,8},{4,12},{8,0},{12,4},{1,9},{5,13},{9,1},{13,5},{2,10},{6,14},... | collective-permute-start | bytes 393224 | tf_op jit(solution)/shard_map/ppermute | solution.py:398
  92.0 0.9 collective-permute-start.8
  92.9 5.8 %correlate_tiles.4 = (f32[2,8,5,256,256]{4,3,2,1,0:T(8,128)}, f32[8,128]{1,0:T(8,128)S(1)}) custom-call(s32[11]{0:T(128)S(1)} %pad_add_fusion.rest_7_.rest_3_.rest_6_.table_ref, bf16[2,4,2,4,64,128]{5,4,3,2,1,0:T(8,128)(2,1)S(1)} %get-tuple-element.87.low_ref, bf16[2,4,2,4,64,128]{5,4,3,2,1,0:T(8,128)(2,1)S(1)} %collective-permute-done.17.high_ref), custom_call_target="tpu_custom_call" | custom-call | tf_op jit(solution)/shard_map/correlate_tiles/pallas_call | solution.py:364
  98.7 2.3 %collective-permute-done.7.rest_2_ = bf16[2,4,64,128]{3,2,1,0:T(8,128)(2,1)S(1)} collective-permute-done((bf16[2,4,64,128]{3,2,1,0:T(8,128)(2,1)S(1)}, bf16[2,4,64,128]{3,2,1,0:T(8,128)(2,1)S(1)}, u32[]{:S(2)}, u32[]{:S(2)}) %collective-permute-start.7) | collective-permute-done | bytes 131104 | tf_op jit(solution)/shard_map/ppermute | solution.py:398
  101.0 0.1 collective-permute-done.16.rest_5_
  101.1 0.6 join_pieces.6
  101.8 0.1 collective-permute-start.19
  101.9 1.3 collective-permute-start.18
  103.2 3.3 %collective-permute-start.9 = (bf16[2,4,64,128]{3,2,1,0:T(8,128)(2,1)S(1)}, bf16[2,4,64,128]{3,2,1,0:T(8,128)(2,1)S(1)}, u32[]{:S(2)}, u32[]{:S(2)}) collective-permute-start(bf16[2,4,64,128]{3,2,1,0:T(8,128)(2,1)S(1)} %get-tuple-element.79), channel_id=1, source_target_pairs={{0,4},{4,8},{8,12},{12,0},{1,5},{5,9},{9,13},{13,1},{2,6},{6,10},{... | collective-permute-start | bytes 393224 | tf_op jit(solution)/shard_map/ppermute | solution.py:398
  106.5 1.5 %collective-permute-start.10 = (bf16[2,4,64,128]{3,2,1,0:T(8,128)(2,1)S(1)}, bf16[2,4,64,128]{3,2,1,0:T(8,128)(2,1)S(1)}, u32[]{:S(2)}, u32[]{:S(2)}) collective-permute-start(bf16[2,4,64,128]{3,2,1,0:T(8,128)(2,1)S(1)} %get-tuple-element.80), channel_id=1, source_target_pairs={{0,8},{4,12},{8,0},{12,4},{1,9},{5,13},{9,1},{13,5},{2,10},{6,14},... | collective-permute-start | bytes 393224 | tf_op jit(solution)/shard_map/ppermute | solution.py:398
  108.0 0.8 collective-permute-start.11
  108.8 5.8 %correlate_tiles.5 = (f32[2,8,5,256,256]{4,3,2,1,0:T(8,128)}, f32[8,128]{1,0:T(8,128)S(1)}) custom-call(s32[11]{0:T(128)S(1)} %pad_add_fusion.rest_7_.rest_3_.rest_6_.table_ref, bf16[2,4,2,4,64,128]{5,4,3,2,1,0:T(8,128)(2,1)S(1)} %get-tuple-element.90.low_ref, ...), custom_call_target="tpu_custom_call", output_to_operand_aliasing={{0}: (3, {})} | custom-call | tf_op jit(solution)/shard_map/correlate_tiles/pallas_call | solution.py:364
  114.6 2.3 %collective-permute-done.10.rest_2_ = bf16[2,4,64,128]{3,2,1,0:T(8,128)(2,1)S(1)} collective-permute-done((bf16[2,4,64,128]{3,2,1,0:T(8,128)(2,1)S(1)}, bf16[2,4,64,128]{3,2,1,0:T(8,128)(2,1)S(1)}, u32[]{:S(2)}, u32[]{:S(2)}) %collective-permute-start.10) | collective-permute-done | bytes 131104 | tf_op jit(solution)/shard_map/ppermute | solution.py:398
  117.0 0.6 join_pieces.7
  117.6 0.1 collective-permute-start.21
  117.7 0.6 collective-permute-start.20
  118.3 2.0 %collective-permute-done.21.high_ref = bf16[2,4,2,4,64,128]{5,4,3,2,1,0:T(8,128)(2,1)S(1)} collective-permute-done((bf16[2,4,2,4,64,128]{5,4,3,2,1,0:T(8,128)(2,1)S(1)}, bf16[2,4,2,4,64,128]{5,4,3,2,1,0:T(8,128)(2,1)S(1)}, u32[]{:S(2)}, u32[]{:S(2)}) %collective-permute-start.21) | collective-permute-done | bytes 1048608 | tf_op jit(solution)/shard_map/ppermute | solution.py:405
  120.4 6.0 %correlate_tiles.6 = (f32[2,8,5,256,256]{4,3,2,1,0:T(8,128)}, f32[8,128]{1,0:T(8,128)S(1)}) custom-call(s32[11]{0:T(128)S(1)} %pad_add_fusion.rest_7_.rest_3_.rest_6_.table_ref, bf16[2,4,2,4,64,128]{5,4,3,2,1,0:T(8,128)(2,1)S(1)} %get-tuple-element.94.low_ref, ...), custom_call_target="tpu_custom_call", output_to_operand_aliasing={{0}: (3, {})} | custom-call | tf_op jit(solution)/shard_map/correlate_tiles/pallas_call | solution.py:364
  126.3 5.7 %collective-permute-done.20.other_ref = bf16[4,2,4,64,128]{4,3,2,1,0:T(8,128)(2,1)S(1)} collective-permute-done((bf16[4,2,4,64,128]{4,3,2,1,0:T(8,128)(2,1)S(1)}, bf16[4,2,4,64,128]{4,3,2,1,0:T(8,128)(2,1)S(1)}, u32[]{:S(2)}, u32[]{:S(2)}) %collective-permute-start.20) | collective-permute-done | bytes 524320 | tf_op jit(solution)/shard_map/ppermute | solution.py:405
  132.1 0.1 pair_blocks.1.low_ref
  132.1 0.1 collective-permute-start.22
  132.2 2.6 %collective-permute-done.22.high_ref = bf16[2,4,2,4,64,128]{5,4,3,2,1,0:T(8,128)(2,1)S(1)} collective-permute-done((bf16[2,4,2,4,64,128]{5,4,3,2,1,0:T(8,128)(2,1)S(1)}, bf16[2,4,2,4,64,128]{5,4,3,2,1,0:T(8,128)(2,1)S(1)}, u32[]{:S(2)}, u32[]{:S(2)}) %collective-permute-start.22) | collective-permute-done | bytes 1048608 | tf_op jit(solution)/shard_map/ppermute | solution.py:405
  134.9 6.4 %correlate_tiles.7 = (f32[2,8,5,256,256]{4,3,2,1,0:T(8,128)}, f32[8,128]{1,0:T(8,128)}) custom-call(s32[11]{0:T(128)S(1)} %pad_add_fusion.rest_7_.rest_3_.rest_6_.table_ref, bf16[2,4,2,4,64,128]{5,4,3,2,1,0:T(8,128)(2,1)S(1)} %pair_blocks.1.low_ref, ...), custom_call_target="tpu_custom_call", output_to_operand_aliasing={{0}: (3, {})} | custom-call | tf_op jit(solution)/shard_map/correlate_tiles/pallas_call | solution.py:364
  (17 shorter events, 0.1 us)
Async XLA Ops:
  0.1 1.6 %copy-start = (bf16[2,2048,256]{2,1,0:T(8,128)(2,1)S(1)}, bf16[2,2048,256]{2,1,0:T(8,128)(2,1)}, u32[]{:S(2)}) copy-start(bf16[2,2048,256]{2,1,0:T(8,128)(2,1)} %v_ref.1) | copy-start | bytes 6291460
  4.4 19.2 %collective-permute-start = (bf16[2,64,2048]{2,1,0:T(8,128)(2,1)}, bf16[2,64,2048]{2,1,0:T(8,128)(2,1)S(1)}, u32[]{:S(2)}, u32[]{:S(2)}) collective-permute-start(bf16[2,64,2048]{2,1,0:T(8,128)(2,1)} %get-tuple-element.53), channel_id=1, source_target_pairs={{0,4},{4,8},{8,12},{12,0},{1,5},{5,9},{9,13},{13,1},{2,6},{6,10},{... | collective-permute-start | bytes 1572872 | tf_op jit(solution)/shard_map/ppermute | solution.py:398
  7.4 36.8 %collective-permute-start.1 = (bf16[2,64,2048]{2,1,0:T(8,128)(2,1)S(1)}, bf16[2,64,2048]{2,1,0:T(8,128)(2,1)S(1)}, u32[]{:S(2)}, u32[]{:S(2)}) collective-permute-start(bf16[2,64,2048]{2,1,0:T(8,128)(2,1)S(1)} %get-tuple-element.54), channel_id=1, source_target_pairs={{0,8},{4,12},{8,0},{12,4},{1,9},{5,13},{9,1},{13,5},{2,10},{6,14},... | collective-permute-start | bytes 1572872 | tf_op jit(solution)/shard_map/ppermute | solution.py:398
  10.0 34.2 %collective-permute-start.2 = (bf16[2,64,2048]{2,1,0:T(8,128)(2,1)S(1)}, bf16[2,64,2048]{2,1,0:T(8,128)(2,1)S(1)}, u32[]{:S(2)}, u32[]{:S(2)}) collective-permute-start(bf16[2,64,2048]{2,1,0:T(8,128)(2,1)S(1)} %get-tuple-element.55), channel_id=1, source_target_pairs={{0,12},{4,0},{8,4},{12,8},{1,13},{5,1},{9,5},{13,9},{2,14},{6,2},{... | collective-permute-start | bytes 1572872 | tf_op jit(solution)/shard_map/ppermute | solution.py:398
  18.1 1.1 copy-start.1
  19.2 1.1 copy-start.2
  20.3 0.7 copy-start.3
  21.0 0.7 copy-start.4
  49.0 17.6 %collective-permute-start.12 = (bf16[2,4,64,128]{3,2,1,0:T(8,128)(2,1)S(1)}, bf16[2,4,64,128]{3,2,1,0:T(8,128)(2,1)S(1)}, u32[]{:S(2)}, u32[]{:S(2)}) collective-permute-start(bf16[2,4,64,128]{3,2,1,0:T(8,128)(2,1)S(1)} %get-tuple-element.83), channel_id=1, source_target_pairs={{0,4},{4,8},{8,12},{12,0},{1,5},{5,9},{9,13},{13,1},{2,6},{6,10},{... | collective-permute-start | bytes 393224 | tf_op jit(solution)/shard_map/ppermute | solution.py:398
  60.7 9.7 %collective-permute-start.13 = (bf16[2,4,64,128]{3,2,1,0:T(8,128)(2,1)S(1)}, bf16[2,4,64,128]{3,2,1,0:T(8,128)(2,1)S(1)}, u32[]{:S(2)}, u32[]{:S(2)}) collective-permute-start(bf16[2,4,64,128]{3,2,1,0:T(8,128)(2,1)S(1)} %get-tuple-element.84), channel_id=1, source_target_pairs={{0,8},{4,12},{8,0},{12,4},{1,9},{5,13},{9,1},{13,5},{2,10},{6,14},... | collective-permute-start | bytes 393224 | tf_op jit(solution)/shard_map/ppermute | solution.py:398
  62.3 8.1 %collective-permute-start.14 = (bf16[2,4,64,128]{3,2,1,0:T(8,128)(2,1)S(1)}, bf16[2,4,64,128]{3,2,1,0:T(8,128)(2,1)S(1)}, u32[]{:S(2)}, u32[]{:S(2)}) collective-permute-start(bf16[2,4,64,128]{3,2,1,0:T(8,128)(2,1)S(1)} %get-tuple-element.85), channel_id=1, source_target_pairs={{0,12},{4,0},{8,4},{12,8},{1,13},{5,1},{9,5},{13,9},{2,14},{6,2},{... | collective-permute-start | bytes 393224 | tf_op jit(solution)/shard_map/ppermute | solution.py:398
  71.0 15.1 %collective-permute-start.15 = (bf16[4,2,4,64,128]{4,3,2,1,0:T(8,128)(2,1)S(1)}, bf16[4,2,4,64,128]{4,3,2,1,0:T(8,128)(2,1)S(1)}, u32[]{:S(2)}, u32[]{:S(2)}) collective-permute-start(bf16[4,2,4,64,128]{4,3,2,1,0:T(8,128)(2,1)S(1)} %join_pieces.4.rest_4_), channel_id=1, source_target_pairs={{0,2},{1,3},{2,0},{3,1},{4,6},{5,7},{6,4},{7,5},{8,10},{9,11},{10,... | collective-permute-start | bytes 1572872 | tf_op jit(solution)/shard_map/ppermute | solution.py:405
  72.6 9.3 %collective-permute-start.3 = (bf16[2,4,64,128]{3,2,1,0:T(8,128)(2,1)S(1)}, bf16[2,4,64,128]{3,2,1,0:T(8,128)(2,1)S(1)}, u32[]{:S(2)}, u32[]{:S(2)}) collective-permute-start(bf16[2,4,64,128]{3,2,1,0:T(8,128)(2,1)S(1)} %get-tuple-element.71), channel_id=1, source_target_pairs={{0,4},{4,8},{8,12},{12,0},{1,5},{5,9},{9,13},{13,1},{2,6},{6,10},{... | collective-permute-start | bytes 393224 | tf_op jit(solution)/shard_map/ppermute | solution.py:398
  75.8 10.1 %collective-permute-start.4 = (bf16[2,4,64,128]{3,2,1,0:T(8,128)(2,1)S(1)}, bf16[2,4,64,128]{3,2,1,0:T(8,128)(2,1)S(1)}, u32[]{:S(2)}, u32[]{:S(2)}) collective-permute-start(bf16[2,4,64,128]{3,2,1,0:T(8,128)(2,1)S(1)} %get-tuple-element.72), channel_id=1, source_target_pairs={{0,8},{4,12},{8,0},{12,4},{1,9},{5,13},{9,1},{13,5},{2,10},{6,14},... | collective-permute-start | bytes 393224 | tf_op jit(solution)/shard_map/ppermute | solution.py:398
  77.9 8.1 %collective-permute-start.5 = (bf16[2,4,64,128]{3,2,1,0:T(8,128)(2,1)S(1)}, bf16[2,4,64,128]{3,2,1,0:T(8,128)(2,1)S(1)}, u32[]{:S(2)}, u32[]{:S(2)}) collective-permute-start(bf16[2,4,64,128]{3,2,1,0:T(8,128)(2,1)S(1)} %get-tuple-element.73), channel_id=1, source_target_pairs={{0,12},{4,0},{8,4},{12,8},{1,13},{5,1},{9,5},{13,9},{2,14},{6,2},{... | collective-permute-start | bytes 393224 | tf_op jit(solution)/shard_map/ppermute | solution.py:398
  86.7 6.2 %collective-permute-start.17 = (bf16[2,4,2,4,64,128]{5,4,3,2,1,0:T(8,128)(2,1)S(1)}, bf16[2,4,2,4,64,128]{5,4,3,2,1,0:T(8,128)(2,1)S(1)}, u32[]{:S(2)}, u32[]{:S(2)}) collective-permute-start(bf16[2,4,2,4,64,128]{5,4,3,2,1,0:T(8,128)(2,1)S(1)} %get-tuple-element.87.low_ref), channel_id=1, source_target_pairs={{0,1},{1,0},{2,3},{3,2},{4,5},{5,4},{6,7},{7,6},{8,9},{9,8},{10,11... | collective-permute-start | bytes 3145736 | tf_op jit(solution)/shard_map/ppermute | solution.py:405
  86.8 14.3 %collective-permute-start.16 = (bf16[4,2,4,64,128]{4,3,2,1,0:T(8,128)(2,1)S(1)}, bf16[4,2,4,64,128]{4,3,2,1,0:T(8,128)(2,1)S(1)}, u32[]{:S(2)}, u32[]{:S(2)}) collective-permute-start(bf16[4,2,4,64,128]{4,3,2,1,0:T(8,128)(2,1)S(1)} %get-tuple-element.86.rest_4_), channel_id=1, source_target_pairs={{0,2},{1,3},{2,0},{3,1},{4,6},{5,7},{6,4},{7,5},{8,10},{9,11},{10,... | collective-permute-start | bytes 1572872 | tf_op jit(solution)/shard_map/ppermute | solution.py:405
  87.4 11.3 %collective-permute-start.6 = (bf16[2,4,64,128]{3,2,1,0:T(8,128)(2,1)S(1)}, bf16[2,4,64,128]{3,2,1,0:T(8,128)(2,1)S(1)}, u32[]{:S(2)}, u32[]{:S(2)}) collective-permute-start(bf16[2,4,64,128]{3,2,1,0:T(8,128)(2,1)S(1)} %get-tuple-element.75), channel_id=1, source_target_pairs={{0,4},{4,8},{8,12},{12,0},{1,5},{5,9},{9,13},{13,1},{2,6},{6,10},{... | collective-permute-start | bytes 393224 | tf_op jit(solution)/shard_map/ppermute | solution.py:398
  90.5 10.5 %collective-permute-start.7 = (bf16[2,4,64,128]{3,2,1,0:T(8,128)(2,1)S(1)}, bf16[2,4,64,128]{3,2,1,0:T(8,128)(2,1)S(1)}, u32[]{:S(2)}, u32[]{:S(2)}) collective-permute-start(bf16[2,4,64,128]{3,2,1,0:T(8,128)(2,1)S(1)} %get-tuple-element.76), channel_id=1, source_target_pairs={{0,8},{4,12},{8,0},{12,4},{1,9},{5,13},{9,1},{13,5},{2,10},{6,14},... | collective-permute-start | bytes 393224 | tf_op jit(solution)/shard_map/ppermute | solution.py:398
  92.0 9.0 %collective-permute-start.8 = (bf16[2,4,64,128]{3,2,1,0:T(8,128)(2,1)S(1)}, bf16[2,4,64,128]{3,2,1,0:T(8,128)(2,1)S(1)}, u32[]{:S(2)}, u32[]{:S(2)}) collective-permute-start(bf16[2,4,64,128]{3,2,1,0:T(8,128)(2,1)S(1)} %get-tuple-element.77), channel_id=1, source_target_pairs={{0,12},{4,0},{8,4},{12,8},{1,13},{5,1},{9,5},{13,9},{2,14},{6,2},{... | collective-permute-start | bytes 393224 | tf_op jit(solution)/shard_map/ppermute | solution.py:398
  101.8 7.1 %collective-permute-start.19 = (bf16[2,4,2,4,64,128]{5,4,3,2,1,0:T(8,128)(2,1)S(1)}, bf16[2,4,2,4,64,128]{5,4,3,2,1,0:T(8,128)(2,1)S(1)}, u32[]{:S(2)}, u32[]{:S(2)}) collective-permute-start(bf16[2,4,2,4,64,128]{5,4,3,2,1,0:T(8,128)(2,1)S(1)} %get-tuple-element.90.low_ref), channel_id=1, source_target_pairs={{0,1},{1,0},{2,3},{3,2},{4,5},{5,4},{6,7},{7,6},{8,9},{9,8},{10,11... | collective-permute-start | bytes 3145736 | tf_op jit(solution)/shard_map/ppermute | solution.py:405
  101.9 15.1 %collective-permute-start.18 = (bf16[4,2,4,64,128]{4,3,2,1,0:T(8,128)(2,1)S(1)}, bf16[4,2,4,64,128]{4,3,2,1,0:T(8,128)(2,1)S(1)}, u32[]{:S(2)}, u32[]{:S(2)}) collective-permute-start(bf16[4,2,4,64,128]{4,3,2,1,0:T(8,128)(2,1)S(1)} %get-tuple-element.89.rest_4_), channel_id=1, source_target_pairs={{0,2},{1,3},{2,0},{3,1},{4,6},{5,7},{6,4},{7,5},{8,10},{9,11},{10,... | collective-permute-start | bytes 1572872 | tf_op jit(solution)/shard_map/ppermute | solution.py:405
  103.2 11.4 %collective-permute-start.9 = (bf16[2,4,64,128]{3,2,1,0:T(8,128)(2,1)S(1)}, bf16[2,4,64,128]{3,2,1,0:T(8,128)(2,1)S(1)}, u32[]{:S(2)}, u32[]{:S(2)}) collective-permute-start(bf16[2,4,64,128]{3,2,1,0:T(8,128)(2,1)S(1)} %get-tuple-element.79), channel_id=1, source_target_pairs={{0,4},{4,8},{8,12},{12,0},{1,5},{5,9},{9,13},{13,1},{2,6},{6,10},{... | collective-permute-start | bytes 393224 | tf_op jit(solution)/shard_map/ppermute | solution.py:398
  106.5 10.5 %collective-permute-start.10 = (bf16[2,4,64,128]{3,2,1,0:T(8,128)(2,1)S(1)}, bf16[2,4,64,128]{3,2,1,0:T(8,128)(2,1)S(1)}, u32[]{:S(2)}, u32[]{:S(2)}) collective-permute-start(bf16[2,4,64,128]{3,2,1,0:T(8,128)(2,1)S(1)} %get-tuple-element.80), channel_id=1, source_target_pairs={{0,8},{4,12},{8,0},{12,4},{1,9},{5,13},{9,1},{13,5},{2,10},{6,14},... | collective-permute-start | bytes 393224 | tf_op jit(solution)/shard_map/ppermute | solution.py:398
  108.0 9.0 %collective-permute-start.11 = (bf16[2,4,64,128]{3,2,1,0:T(8,128)(2,1)S(1)}, bf16[2,4,64,128]{3,2,1,0:T(8,128)(2,1)S(1)}, u32[]{:S(2)}, u32[]{:S(2)}) collective-permute-start(bf16[2,4,64,128]{3,2,1,0:T(8,128)(2,1)S(1)} %get-tuple-element.81), channel_id=1, source_target_pairs={{0,12},{4,0},{8,4},{12,8},{1,13},{5,1},{9,5},{13,9},{2,14},{6,2},{... | collective-permute-start | bytes 393224 | tf_op jit(solution)/shard_map/ppermute | solution.py:398
  117.6 2.7 %collective-permute-start.21 = (bf16[2,4,2,4,64,128]{5,4,3,2,1,0:T(8,128)(2,1)S(1)}, bf16[2,4,2,4,64,128]{5,4,3,2,1,0:T(8,128)(2,1)S(1)}, u32[]{:S(2)}, u32[]{:S(2)}) collective-permute-start(bf16[2,4,2,4,64,128]{5,4,3,2,1,0:T(8,128)(2,1)S(1)} %get-tuple-element.94.low_ref), channel_id=1, source_target_pairs={{0,1},{1,0},{2,3},{3,2},{4,5},{5,4},{6,7},{7,6},{8,9},{9,8},{10,11... | collective-permute-start | bytes 3145736 | tf_op jit(solution)/shard_map/ppermute | solution.py:405
  117.7 14.3 %collective-permute-start.20 = (bf16[4,2,4,64,128]{4,3,2,1,0:T(8,128)(2,1)S(1)}, bf16[4,2,4,64,128]{4,3,2,1,0:T(8,128)(2,1)S(1)}, u32[]{:S(2)}, u32[]{:S(2)}) collective-permute-start(bf16[4,2,4,64,128]{4,3,2,1,0:T(8,128)(2,1)S(1)} %get-tuple-element.93.own_ref), channel_id=1, source_target_pairs={{0,2},{1,3},{2,0},{3,1},{4,6},{5,7},{6,4},{7,5},{8,10},{9,11},{10,... | collective-permute-start | bytes 1572872 | tf_op jit(solution)/shard_map/ppermute | solution.py:405
  132.1 2.7 %collective-permute-start.22 = (bf16[2,4,2,4,64,128]{5,4,3,2,1,0:T(8,128)(2,1)S(1)}, bf16[2,4,2,4,64,128]{5,4,3,2,1,0:T(8,128)(2,1)S(1)}, u32[]{:S(2)}, u32[]{:S(2)}) collective-permute-start(bf16[2,4,2,4,64,128]{5,4,3,2,1,0:T(8,128)(2,1)S(1)} %pair_blocks.1.low_ref), channel_id=1, source_target_pairs={{0,1},{1,0},{2,3},{3,2},{4,5},{5,4},{6,7},{7,6},{8,9},{9,8},{10,11... | collective-permute-start | bytes 3145736 | tf_op jit(solution)/shard_map/ppermute | solution.py:405

commit v2 on v1

--- a/solution.py
+++ b/solution.py
@@ -190,9 +190,20 @@
                         part
                     ].astype(jnp.bfloat16)
 
+    whole = halves if len(out_refs) == halves * dests else halves - 1
     for shift in range(dests):
-        for half in range(halves):
+        for half in range(whole):
             out_refs[half * dests + shift][...] = made[place_ref[shift], half]
+        if whole < halves:
+            run = rows // 2
+            for part in range(2):
+                for s in range(spectra):
+                    both = made[place_ref[shift], whole, part, s]
+                    for c in range(2):
+                        at = slice(c * AVG, (c + 1) * AVG)
+                        out_refs[(whole + c) * dests + shift][part, s] = jnp.concatenate(
+                            [both[:run, at], both[run:, at]], axis=1
+                        )
 
 
 def transform_cut(source, place, coef_table, tables, cut, sizes, after):
@@ -218,6 +229,11 @@
         pltpu.VMEM((dests, halves, 2, spectra, rows, LANES), jnp.bfloat16),
     ]
     shapes = [jax.ShapeDtypeStruct((2, spectra, rows, LANES), jnp.bfloat16)] * (halves * dests)
+    if not begins:
+        shapes[-dests:] = [
+            jax.ShapeDtypeStruct((2, spectra, rows // 2, LANES), jnp.bfloat16)
+        ] * (2 * dests)
+    outs = len(shapes) // dests
     if begins:
         scratch = [pltpu.VMEM((spectra, 2, rows, samples), jnp.bfloat16)] + scratch
         shapes = shapes + [jax.ShapeDtypeStruct((total, 4 * inner), jnp.bfloat16)]
@@ -239,7 +255,7 @@
         compiler_params=pltpu.CompilerParams(vmem_limit_bytes=VMEM_BYTES // 2),
         name="filter_transform" if begins else "transform_rest",
     )(place, *args, after)
-    units = [made[half * dests : (half + 1) * dests] for half in range(halves)]
+    units = [made[unit * dests : (unit + 1) * dests] for unit in range(outs)]
     return units, made[-1]
 
 
@@ -287,14 +303,14 @@
     )(own, other, after)
 
 
-def correlate_kernel(chunks, scale, first, table_ref, low_ref, high_ref, *rest):
+def correlate_kernel(chunks, single, scale, first, table_ref, low_ref, high_ref, *rest):
     o_ref, token_ref, left, tiles, empty, sems = rest[-6:]
     half, senders, _, spectra, rows, lanes = low_ref.shape
     order = block_order(2 * half)
     slots = o_ref.shape[2]
-    coarse = lanes // AVG
-    side = senders * rows
-    run = rows // chunks
+    coarse = 1 if single else lanes // AVG
+    run = rows if single else rows // chunks
+    side = senders * chunks * run
     count = table_ref[2 * slots]
     token_ref[...] = jnp.zeros_like(token_ref)
     empty[...] = jnp.zeros_like(empty)
@@ -317,13 +333,14 @@
             for part in range(2):
                 for chunk in range(chunks):
                     row = pl.multiple_of(part * side + (chunk * senders + sender) * run, run)
+                    top = 0 if single else chunk * run
                     pieces = [
-                        source[sender, part, s, chunk * run : (chunk + 1) * run]
-                        for s in range(spectra)
+                        source[sender, part, s, top : top + run] for s in range(spectra)
                     ]
                     for c in range(coarse):
+                        lane = (chunk if single else c) * AVG
                         left[c, block, pl.ds(row, run), :] = jnp.concatenate(
-                            [piece[:, c * AVG : (c + 1) * AVG] for piece in pieces], axis=1
+                            [piece[:, lane : lane + AVG] for piece in pieces], axis=1
                         )
 
     for slot in range(slots):
@@ -350,10 +367,10 @@
             copy_out(empty, c, slot).wait()
 
 
-def correlate(table, gathered, first, channels, chunks, slots, vis):
+def correlate(table, gathered, first, channels, chunks, single, slots, vis):
     half, senders, _, spectra, rows, lanes = gathered[0].shape
-    coarse = lanes // AVG
-    side = senders * rows
+    coarse = 1 if single else lanes // AVG
+    side = senders * rows * (chunks if single else 1)
     vmem = pl.BlockSpec(memory_space=pltpu.VMEM)
     anywhere = pl.BlockSpec(memory_space=pl.ANY)
     args = [table, *gathered]
@@ -362,7 +379,7 @@
         args.append(vis)
         aliases = {len(args) - 1: 0}
     return pl.pallas_call(
-        functools.partial(correlate_kernel, chunks, 1.0 / (AVG * spectra), first),
+        functools.partial(correlate_kernel, chunks, single, 1.0 / (AVG * spectra), first),
         grid_spec=pltpu.PrefetchScalarGridSpec(
             num_scalar_prefetch=1,
             grid=(),
@@ -466,7 +483,10 @@
         and radix <= 8
         and blocks & (blocks - 1) == 0
         and blocks > 2
-        and inputs % LANES == 0
+        and inputs == 2 * LANES
+        and LANES == 2 * AVG
+        and radix // dests * MXU // LANES > 1
+        and MXU > LANES
         and LANES % dests == 0
         and (LANES // dests) % ROWS16 == 0
         and (dests * AVG) % LANES == 0
@@ -518,10 +538,11 @@
             held = pair(own, other, tokens[-1])
         if unit > 0:
             gathered = gather_blocks(held, table)
-            cut, part = divmod(unit - 1, radix // dests)
-            first = (part * MXU + cut * LANES) // AVG
+            single = unit > units - 2
+            cut, part = divmod(min(unit, units - 1) - 1, radix // dests)
+            first = (part * MXU + cut * LANES) // AVG + (1 if unit == units else 0)
             vis, token = correlate(
-                table, gathered, first, units * LANES // AVG, chunks, slot_cap, vis
+                table, gathered, first, samples // dests // AVG, chunks, single, slot_cap, vis
             )
             tokens.append(token)
     return vis

time: 142 us -> 147 us (1.035)
  starting transfers between devices: 42.3 us -> 48.8 us
  waiting for transfers between devices: 47.4 us -> 42.2 us
  Pallas kernels: 37.5 us -> 41.3 us
    ppermute x15 -> x18, starting transfers between devices: 37.9 us -> 43.6 us  [spread(): lax.ppermute(pieces[d], 'ft', [(i, (i + d) % count) for i in range(count)])]
    pallas_call x4 -> x5, Pallas kernels: 23.9 us -> 27 us  [correlate(): pl.pallas_call(functools.partial(correlate_kernel, chunks, single, 1.0 /...]
    ppermute x8 -> x10, waiting for transfers between devices: 10.5 us -> 7.79 us  [exchange(): return lax.ppermute(own, 'bl', [(i, i ^ bit) for i in range(count)])]
    ppermute x15 -> x18, waiting for transfers between devices: 36.9 us -> 34.4 us  [spread(): lax.ppermute(pieces[d], 'ft', [(i, (i + d) % count) for i in range(count)])]
    ppermute x8 -> x10, starting transfers between devices: 4.38 us -> 5.25 us  [exchange(): return lax.ppermute(own, 'bl', [(i, i ^ bit) for i in range(count)])]
    pallas_call x4 -> x5, Pallas kernels: 2.51 us -> 3.09 us  [join(): pl.pallas_call(kernel, grid_spec=pltpu.PrefetchScalarGridSpec(num_scalar_...]
  transfers between devices with their start and end apart: 23 -> 28, of which waited for: 11 -> 11; matrix products, arithmetic and copies ran while one was open for 6% -> 6% of each run, Pallas kernels for 15% -> 18%
where the time goes in v2:
time: 147 us
  starting transfers between devices  48.8 us (33%)
  waiting for transfers between devices  42.2 us (29%)
  Pallas kernels  41.3 us (28%)
  local copies, waits for them, and re-layouts  9.17 us (6%)
  other arithmetic  4.61 us (3%)
    ppermute x18, starting transfers between devices, spread(): lax.ppermute(pieces[d], 'ft', [(i, (i + d) % count) for i in range(count)])  43.6 us
    ppermute x18, waiting for transfers between devices, spread(): lax.ppermute(pieces[d], 'ft', [(i, (i + d) % count) for i in range(count)])  34.4 us
    pallas_call x5, Pallas kernels, correlate(): pl.pallas_call(functools.partial(correlate_kernel, chunks, single, 1.0 /...  27 us
    pallas_call x2, Pallas kernels, transform_cut(): pl.pallas_call(kernel, grid_spec=pltpu.PrefetchScalarGridSpec(num_scalar_...  8.38 us
    ppermute x10, waiting for transfers between devices, exchange(): return lax.ppermute(own, 'bl', [(i, i ^ bit) for i in range(count)])  7.79 us
    unnamed x10, local copies, waits for them, and re-layouts  5.25 us
    ppermute x10, starting transfers between devices, exchange(): return lax.ppermute(own, 'bl', [(i, i ^ bit) for i in range(count)])  5.25 us
    reshape x2, local copies, waits for them, and re-layouts, per_device_kernels(): coef_table = coefs.reshape(taps, MXU, radix).transpose(0, 2, 1)  3.92 us
  transfers between devices with their start and end apart: 28, of which 11 were waited for; matrix products, arithmetic and copies ran while one was open for 6% of the time, Pallas kernels for 18%

profile of v2, /device:TPU:0, one launch (start us, length us, event | category | flops | bytes accessed | tf_op | source)
XLA Modules:
  0.0 146.6 jit_solution(11841076830796238786)
XLA Ops:
  0.0 0.1 pad_add_fusion.1.place_ref
  0.1 1.6 %copy-done = bf16[2,2048,256]{2,1,0:T(8,128)(2,1)S(1)} copy-done((bf16[2,2048,256]{2,1,0:T(8,128)(2,1)S(1)}, bf16[2,2048,256]{2,1,0:T(8,128)(2,1)}, u32[]{:S(2)}) %copy-start) | copy-done | bytes 2097176
  1.7 2.7 %pack_inputs.1 = (bf16[2,64,2048]{2,1,0:T(8,128)(2,1)S(1)}, bf16[2,64,2048]{2,1,0:T(8,128)(2,1)}, bf16[2,64,2048]{2,1,0:T(8,128)(2,1)S(1)}, bf16[2,64,2048]{2,1,0:T(8,128)(2,1)S(1)}) custom-call(s32[8]{0:T(128)S(1)} %pad_add_fusion.1.place_ref, bf16[2,2048,256]{2,1,0:T(8,128)(2,1)S(1)} %copy-done), custom_call_target="tpu_custom_call" | custom-call | tf_op jit(solution)/shard_map/pack_inputs/pallas_call | solution.py:97
  4.4 3.0 %collective-permute-start = (bf16[2,64,2048]{2,1,0:T(8,128)(2,1)}, bf16[2,64,2048]{2,1,0:T(8,128)(2,1)S(1)}, u32[]{:S(2)}, u32[]{:S(2)}) collective-permute-start(bf16[2,64,2048]{2,1,0:T(8,128)(2,1)} %get-tuple-element.65), channel_id=1, source_target_pairs={{0,4},{4,8},{8,12},{12,0},{1,5},{5,9},{9,13},{13,1},{2,6},{6,10},{... | collective-permute-start | bytes 1572872 | tf_op jit(solution)/shard_map/ppermute | solution.py:415
  7.4 2.6 %collective-permute-start.1 = (bf16[2,64,2048]{2,1,0:T(8,128)(2,1)S(1)}, bf16[2,64,2048]{2,1,0:T(8,128)(2,1)S(1)}, u32[]{:S(2)}, u32[]{:S(2)}) collective-permute-start(bf16[2,64,2048]{2,1,0:T(8,128)(2,1)S(1)} %get-tuple-element.66), channel_id=1, source_target_pairs={{0,8},{4,12},{8,0},{12,4},{1,9},{5,13},{9,1},{13,5},{2,10},{6,14},... | collective-permute-start | bytes 1572872 | tf_op jit(solution)/shard_map/ppermute | solution.py:415
  10.0 1.3 collective-permute-start.2
  11.4 0.8 fusion.1
  12.1 2.4 %reshape.11 = f32[8,256,8]{2,1,0:T(8,128)} reshape(f32[8,2048]{1,0:T(8,128)} %param.16) | data formatting | bytes 131072 | tf_op jit(solution)/shard_map/reshape | solution.py:501
  14.5 1.5 %copy.21 = f32[8,256,8]{1,2,0:T(8,128)S(1)} copy(f32[8,256,8]{2,1,0:T(8,128)} %reshape.11) | data formatting | bytes 131072 | tf_op jit(solution)/shard_map/reshape | solution.py:501
  16.0 0.7 broadcast_compare_fusion
  16.7 0.6 reduce_sum.69
  17.3 0.8 select_reduce_fusion.3
  18.1 1.1 copy-done.1
  19.2 1.1 copy-done.2
  20.4 0.7 copy-done.3
  21.1 0.7 copy-done.4
  21.8 0.1 stage_tables.1
  21.9 0.8 multiply_reduce_fusion
  22.7 0.2 select_reduce_fusion.1
  22.9 0.7 pad_add_fusion.rest_7_.rest_3_.rest_6_.table_ref
  23.6 20.6 %collective-permute-done.1.rest_2_ = bf16[2,64,2048]{2,1,0:T(8,128)(2,1)S(1)} collective-permute-done((bf16[2,64,2048]{2,1,0:T(8,128)(2,1)S(1)}, bf16[2,64,2048]{2,1,0:T(8,128)(2,1)S(1)}, u32[]{:S(2)}, u32[]{:S(2)}) %collective-permute-start.1) | collective-permute-done | bytes 524320 | tf_op jit(solution)/shard_map/ppermute | solution.py:415
  44.2 4.8 %filter_transform.1 = (bf16[2,4,64,128]{3,2,1,0:T(8,128)(2,1)S(1)}, bf16[2,4,64,128]{3,2,1,0:T(8,128)(2,1)S(1)}, bf16[2,4,64,128]{3,2,1,0:T(8,128)(2,1)S(1)}, bf...) custom-call(s32[8]{0:T(128)S(1)} %pad_add_fusion.1.place_ref, ...), custom_call_target="tpu_custom_call" | custom-call | flops 1610612736 | bytes 6291456 | tf_op jit(solution)/shard_map/filter_transform/pallas_call | solution.py:242
  49.0 11.8 %collective-permute-start.15 = (bf16[2,4,64,128]{3,2,1,0:T(8,128)(2,1)S(1)}, bf16[2,4,64,128]{3,2,1,0:T(8,128)(2,1)S(1)}, u32[]{:S(2)}, u32[]{:S(2)}) collective-permute-start(bf16[2,4,64,128]{3,2,1,0:T(8,128)(2,1)S(1)} %get-tuple-element.103), channel_id=1, source_target_pairs={{0,4},{4,8},{8,12},{12,0},{1,5},{5,9},{9,13},{13,1},{2,6},{6,10},{... | collective-permute-start | bytes 393224 | tf_op jit(solution)/shard_map/ppermute | solution.py:415
  60.8 1.6 %collective-permute-start.16 = (bf16[2,4,64,128]{3,2,1,0:T(8,128)(2,1)S(1)}, bf16[2,4,64,128]{3,2,1,0:T(8,128)(2,1)S(1)}, u32[]{:S(2)}, u32[]{:S(2)}) collective-permute-start(bf16[2,4,64,128]{3,2,1,0:T(8,128)(2,1)S(1)} %get-tuple-element.104), channel_id=1, source_target_pairs={{0,8},{4,12},{8,0},{12,4},{1,9},{5,13},{9,1},{13,5},{2,10},{6,14},... | collective-permute-start | bytes 393224 | tf_op jit(solution)/shard_map/ppermute | solution.py:415
  62.3 0.9 collective-permute-start.17
  63.2 3.6 %transform_rest.1 = (bf16[2,4,64,128]{3,2,1,0:T(8,128)(2,1)S(1)}, bf16[2,4,64,128]{3,2,1,0:T(8,128)(2,1)S(1)}, bf16[2,4,64,128]{3,2,1,0:T(8,128)(2,1)S(1)}, bf16...) custom-call(s32[8]{0:T(128)S(1)} %pad_add_fusion.1.place_ref, ...), custom_call_target="tpu_custom_call" | custom-call | flops 1610612736 | bytes 6291456 | tf_op jit(solution)/shard_map/transform_rest/pallas_call | solution.py:242
  66.8 3.6 %collective-permute-done.16.rest_2_ = bf16[2,4,64,128]{3,2,1,0:T(8,128)(2,1)S(1)} collective-permute-done((bf16[2,4,64,128]{3,2,1,0:T(8,128)(2,1)S(1)}, bf16[2,4,64,128]{3,2,1,0:T(8,128)(2,1)S(1)}, u32[]{:S(2)}, u32[]{:S(2)}) %collective-permute-start.16) | collective-permute-done | bytes 131104 | tf_op jit(solution)/shard_map/ppermute | solution.py:415
  70.4 0.6 join_pieces.5.rest_4_
  71.0 1.6 %collective-permute-start.18 = (bf16[4,2,4,64,128]{4,3,2,1,0:T(8,128)(2,1)S(1)}, bf16[4,2,4,64,128]{4,3,2,1,0:T(8,128)(2,1)S(1)}, u32[]{:S(2)}, u32[]{:S(2)}) collective-permute-start(bf16[4,2,4,64,128]{4,3,2,1,0:T(8,128)(2,1)S(1)} %join_pieces.5.rest_4_), channel_id=1, source_target_pairs={{0,2},{1,3},{2,0},{3,1},{4,6},{5,7},{6,4},{7,5},{8,10},{9,11},{10,... | collective-permute-start | bytes 1572872 | tf_op jit(solution)/shard_map/ppermute | solution.py:422
  72.6 3.3 %collective-permute-start.3 = (bf16[2,4,64,128]{3,2,1,0:T(8,128)(2,1)S(1)}, bf16[2,4,64,128]{3,2,1,0:T(8,128)(2,1)S(1)}, u32[]{:S(2)}, u32[]{:S(2)}) collective-permute-start(bf16[2,4,64,128]{3,2,1,0:T(8,128)(2,1)S(1)} %get-tuple-element.87), channel_id=1, source_target_pairs={{0,4},{4,8},{8,12},{12,0},{1,5},{5,9},{9,13},{13,1},{2,6},{6,10},{... | collective-permute-start | bytes 393224 | tf_op jit(solution)/shard_map/ppermute | solution.py:415
  75.9 2.1 %collective-permute-start.4 = (bf16[2,4,64,128]{3,2,1,0:T(8,128)(2,1)S(1)}, bf16[2,4,64,128]{3,2,1,0:T(8,128)(2,1)S(1)}, u32[]{:S(2)}, u32[]{:S(2)}) collective-permute-start(bf16[2,4,64,128]{3,2,1,0:T(8,128)(2,1)S(1)} %get-tuple-element.88), channel_id=1, source_target_pairs={{0,8},{4,12},{8,0},{12,4},{1,9},{5,13},{9,1},{13,5},{2,10},{6,14},... | collective-permute-start | bytes 393224 | tf_op jit(solution)/shard_map/ppermute | solution.py:415
  77.9 0.3 collective-permute-start.5
  78.2 3.6 %collective-permute-done.3.rest_1_ = bf16[2,4,64,128]{3,2,1,0:T(8,128)(2,1)S(1)} collective-permute-done((bf16[2,4,64,128]{3,2,1,0:T(8,128)(2,1)S(1)}, bf16[2,4,64,128]{3,2,1,0:T(8,128)(2,1)S(1)}, u32[]{:S(2)}, u32[]{:S(2)}) %collective-permute-start.3) | collective-permute-done | bytes 131104 | tf_op jit(solution)/shard_map/ppermute | solution.py:415
  81.8 4.1 %collective-permute-done.4.rest_2_ = bf16[2,4,64,128]{3,2,1,0:T(8,128)(2,1)S(1)} collective-permute-done((bf16[2,4,64,128]{3,2,1,0:T(8,128)(2,1)S(1)}, bf16[2,4,64,128]{3,2,1,0:T(8,128)(2,1)S(1)}, u32[]{:S(2)}, u32[]{:S(2)}) %collective-permute-start.4) | collective-permute-done | bytes 131104 | tf_op jit(solution)/shard_map/ppermute | solution.py:415
  85.9 0.1 collective-permute-done.5.rest_3_
  86.1 0.6 join_pieces.6
  86.7 0.1 collective-permute-start.20
  86.8 0.6 collective-permute-start.19
  87.4 3.1 %collective-permute-start.6 = (bf16[2,4,64,128]{3,2,1,0:T(8,128)(2,1)S(1)}, bf16[2,4,64,128]{3,2,1,0:T(8,128)(2,1)S(1)}, u32[]{:S(2)}, u32[]{:S(2)}) collective-permute-start(bf16[2,4,64,128]{3,2,1,0:T(8,128)(2,1)S(1)} %get-tuple-element.91), channel_id=1, source_target_pairs={{0,4},{4,8},{8,12},{12,0},{1,5},{5,9},{9,13},{13,1},{2,6},{6,10},{... | collective-permute-start | bytes 393224 | tf_op jit(solution)/shard_map/ppermute | solution.py:415
  90.6 1.5 %collective-permute-start.7 = (bf16[2,4,64,128]{3,2,1,0:T(8,128)(2,1)S(1)}, bf16[2,4,64,128]{3,2,1,0:T(8,128)(2,1)S(1)}, u32[]{:S(2)}, u32[]{:S(2)}) collective-permute-start(bf16[2,4,64,128]{3,2,1,0:T(8,128)(2,1)S(1)} %get-tuple-element.92), channel_id=1, source_target_pairs={{0,8},{4,12},{8,0},{12,4},{1,9},{5,13},{9,1},{13,5},{2,10},{6,14},... | collective-permute-start | bytes 393224 | tf_op jit(solution)/shard_map/ppermute | solution.py:415
  92.0 0.9 collective-permute-start.8
  92.9 5.8 %correlate_tiles.5 = (f32[2,8,5,256,256]{4,3,2,1,0:T(8,128)}, f32[8,128]{1,0:T(8,128)S(1)}) custom-call(s32[11]{0:T(128)S(1)} %pad_add_fusion.rest_7_.rest_3_.rest_6_.table_ref, bf16[2,4,2,4,64,128]{5,4,3,2,1,0:T(8,128)(2,1)S(1)} %get-tuple-element.107.low_ref, bf16[2,4,2,4,64,128]{5,4,3,2,1,0:T(8,128)(2,1)S(1)} %collective-permute-done.20.high_ref), custom_call_target="tpu_custom_call" | custom-call | tf_op jit(solution)/shard_map/correlate_tiles/pallas_call | solution.py:381
  98.7 2.3 %collective-permute-done.7.rest_2_ = bf16[2,4,64,128]{3,2,1,0:T(8,128)(2,1)S(1)} collective-permute-done((bf16[2,4,64,128]{3,2,1,0:T(8,128)(2,1)S(1)}, bf16[2,4,64,128]{3,2,1,0:T(8,128)(2,1)S(1)}, u32[]{:S(2)}, u32[]{:S(2)}) %collective-permute-start.7) | collective-permute-done | bytes 131104 | tf_op jit(solution)/shard_map/ppermute | solution.py:415
  101.0 0.1 collective-permute-done.19.rest_5_
  101.1 0.6 join_pieces.7
  101.8 0.1 collective-permute-start.22
  101.9 1.3 collective-permute-start.21
  103.2 3.3 %collective-permute-start.9 = (bf16[2,4,32,128]{3,2,1,0:T(8,128)(2,1)S(1)}, bf16[2,4,32,128]{3,2,1,0:T(8,128)(2,1)S(1)}, u32[]{:S(2)}, u32[]{:S(2)}) collective-permute-start(bf16[2,4,32,128]{3,2,1,0:T(8,128)(2,1)S(1)} %get-tuple-element.95), channel_id=1, source_target_pairs={{0,4},{4,8},{8,12},{12,0},{1,5},{5,9},{9,13},{13,1},{2,6},{6,10},{... | collective-permute-start | bytes 196616 | tf_op jit(solution)/shard_map/ppermute | solution.py:415
  106.5 1.5 %collective-permute-start.10 = (bf16[2,4,32,128]{3,2,1,0:T(8,128)(2,1)S(1)}, bf16[2,4,32,128]{3,2,1,0:T(8,128)(2,1)S(1)}, u32[]{:S(2)}, u32[]{:S(2)}) collective-permute-start(bf16[2,4,32,128]{3,2,1,0:T(8,128)(2,1)S(1)} %get-tuple-element.96), channel_id=1, source_target_pairs={{0,8},{4,12},{8,0},{12,4},{1,9},{5,13},{9,1},{13,5},{2,10},{6,14},... | collective-permute-start | bytes 196616 | tf_op jit(solution)/shard_map/ppermute | solution.py:415
  108.0 0.8 collective-permute-start.11
  108.9 5.8 %correlate_tiles.6 = (f32[2,8,5,256,256]{4,3,2,1,0:T(8,128)}, f32[8,128]{1,0:T(8,128)S(1)}) custom-call(s32[11]{0:T(128)S(1)} %pad_add_fusion.rest_7_.rest_3_.rest_6_.table_ref, bf16[2,4,2,4,64,128]{5,4,3,2,1,0:T(8,128)(2,1)S(1)} %get-tuple-element.110.low_ref, ...), custom_call_target="tpu_custom_call", output_to_operand_aliasing={{0}: (3, {})} | custom-call | tf_op jit(solution)/shard_map/correlate_tiles/pallas_call | solution.py:381
  114.7 1.5 %collective-permute-done.21.rest_5_ = bf16[4,2,4,64,128]{4,3,2,1,0:T(8,128)(2,1)S(1)} collective-permute-done((bf16[4,2,4,64,128]{4,3,2,1,0:T(8,128)(2,1)S(1)}, bf16[4,2,4,64,128]{4,3,2,1,0:T(8,128)(2,1)S(1)}, u32[]{:S(2)}, u32[]{:S(2)}) %collective-permute-start.21) | collective-permute-done | bytes 524320 | tf_op jit(solution)/shard_map/ppermute | solution.py:422
  116.2 0.6 join_pieces.8
  116.9 1.3 collective-permute-start.23
  118.3 3.3 %collective-permute-start.12 = (bf16[2,4,32,128]{3,2,1,0:T(8,128)(2,1)S(1)}, bf16[2,4,32,128]{3,2,1,0:T(8,128)(2,1)S(1)}, u32[]{:S(2)}, u32[]{:S(2)}) collective-permute-start(bf16[2,4,32,128]{3,2,1,0:T(8,128)(2,1)S(1)} %get-tuple-element.99), channel_id=1, source_target_pairs={{0,4},{4,8},{8,12},{12,0},{1,5},{5,9},{9,13},{13,1},{2,6},{6,10},{... | collective-permute-start | bytes 196616 | tf_op jit(solution)/shard_map/ppermute | solution.py:415
  121.5 1.5 %collective-permute-start.13 = (bf16[2,4,32,128]{3,2,1,0:T(8,128)(2,1)S(1)}, bf16[2,4,32,128]{3,2,1,0:T(8,128)(2,1)S(1)}, u32[]{:S(2)}, u32[]{:S(2)}) collective-permute-start(bf16[2,4,32,128]{3,2,1,0:T(8,128)(2,1)S(1)} %get-tuple-element.100), channel_id=1, source_target_pairs={{0,8},{4,12},{8,0},{12,4},{1,9},{5,13},{9,1},{13,5},{2,10},{6,14},... | collective-permute-start | bytes 196616 | tf_op jit(solution)/shard_map/ppermute | solution.py:415
  123.1 0.8 collective-permute-start.14
  123.9 6.0 %correlate_tiles.7 = (f32[2,8,5,256,256]{4,3,2,1,0:T(8,128)}, f32[8,128]{1,0:T(8,128)S(1)}) custom-call(s32[11]{0:T(128)S(1)} %pad_add_fusion.rest_7_.rest_3_.rest_6_.table_ref, bf16[2,4,2,4,64,128]{5,4,3,2,1,0:T(8,128)(2,1)S(1)} %get-tuple-element.114.low_ref, ...), custom_call_target="tpu_custom_call", output_to_operand_aliasing={{0}: (3, {})} | custom-call | tf_op jit(solution)/shard_map/correlate_tiles/pallas_call | solution.py:381
  129.9 0.6 join_pieces.9
  130.7 1.8 %collective-permute-done.26.high_ref = bf16[2,4,2,4,32,128]{5,4,3,2,1,0:T(8,128)(2,1)S(1)} collective-permute-done((bf16[2,4,2,4,32,128]{5,4,3,2,1,0:T(8,128)(2,1)S(1)}, bf16[2,4,2,4,32,128]{5,4,3,2,1,0:T(8,128)(2,1)S(1)}, u32[]{:S(2)}, u32[]{:S(2)}) %collective-permute-start.26) | collective-permute-done | bytes 524320 | tf_op jit(solution)/shard_map/ppermute | solution.py:422
  132.5 4.4 %correlate_tiles.8 = (f32[2,8,5,256,256]{4,3,2,1,0:T(8,128)}, f32[8,128]{1,0:T(8,128)S(1)}) custom-call(s32[11]{0:T(128)S(1)} %pad_add_fusion.rest_7_.rest_3_.rest_6_.table_ref, bf16[2,4,2,4,32,128]{5,4,3,2,1,0:T(8,128)(2,1)S(1)} %get-tuple-element.118.low_ref, ...), custom_call_target="tpu_custom_call", output_to_operand_aliasing={{0}: (3, {})} | custom-call | tf_op jit(solution)/shard_map/correlate_tiles/pallas_call | solution.py:381
  136.9 2.4 %collective-permute-done.25.other_ref = bf16[4,2,4,32,128]{4,3,2,1,0:T(8,128)(2,1)S(1)} collective-permute-done((bf16[4,2,4,32,128]{4,3,2,1,0:T(8,128)(2,1)S(1)}, bf16[4,2,4,32,128]{4,3,2,1,0:T(8,128)(2,1)S(1)}, u32[]{:S(2)}, u32[]{:S(2)}) %collective-permute-start.25) | collective-permute-done | bytes 262176 | tf_op jit(solution)/shard_map/ppermute | solution.py:422
  139.5 1.9 %collective-permute-done.27.high_ref = bf16[2,4,2,4,32,128]{5,4,3,2,1,0:T(8,128)(2,1)S(1)} collective-permute-done((bf16[2,4,2,4,32,128]{5,4,3,2,1,0:T(8,128)(2,1)S(1)}, bf16[2,4,2,4,32,128]{5,4,3,2,1,0:T(8,128)(2,1)S(1)}, u32[]{:S(2)}, u32[]{:S(2)}) %collective-permute-start.27) | collective-permute-done | bytes 524320 | tf_op jit(solution)/shard_map/ppermute | solution.py:422
  141.4 5.0 %correlate_tiles.9 = (f32[2,8,5,256,256]{4,3,2,1,0:T(8,128)}, f32[8,128]{1,0:T(8,128)}) custom-call(s32[11]{0:T(128)S(1)} %pad_add_fusion.rest_7_.rest_3_.rest_6_.table_ref, bf16[2,4,2,4,32,128]{5,4,3,2,1,0:T(8,128)(2,1)S(1)} %pair_blocks.1.low_ref, ...), custom_call_target="tpu_custom_call", output_to_operand_aliasing={{0}: (3, {})} | custom-call | tf_op jit(solution)/shard_map/correlate_tiles/pallas_call | solution.py:381
  (29 shorter events, 0.4 us)
Async XLA Ops:
  0.1 1.6 %copy-start = (bf16[2,2048,256]{2,1,0:T(8,128)(2,1)S(1)}, bf16[2,2048,256]{2,1,0:T(8,128)(2,1)}, u32[]{:S(2)}) copy-start(bf16[2,2048,256]{2,1,0:T(8,128)(2,1)} %v_ref.1) | copy-start | bytes 6291460
  4.4 19.2 %collective-permute-start = (bf16[2,64,2048]{2,1,0:T(8,128)(2,1)}, bf16[2,64,2048]{2,1,0:T(8,128)(2,1)S(1)}, u32[]{:S(2)}, u32[]{:S(2)}) collective-permute-start(bf16[2,64,2048]{2,1,0:T(8,128)(2,1)} %get-tuple-element.65), channel_id=1, source_target_pairs={{0,4},{4,8},{8,12},{12,0},{1,5},{5,9},{9,13},{13,1},{2,6},{6,10},{... | collective-permute-start | bytes 1572872 | tf_op jit(solution)/shard_map/ppermute | solution.py:415
  7.4 36.8 %collective-permute-start.1 = (bf16[2,64,2048]{2,1,0:T(8,128)(2,1)S(1)}, bf16[2,64,2048]{2,1,0:T(8,128)(2,1)S(1)}, u32[]{:S(2)}, u32[]{:S(2)}) collective-permute-start(bf16[2,64,2048]{2,1,0:T(8,128)(2,1)S(1)} %get-tuple-element.66), channel_id=1, source_target_pairs={{0,8},{4,12},{8,0},{12,4},{1,9},{5,13},{9,1},{13,5},{2,10},{6,14},... | collective-permute-start | bytes 1572872 | tf_op jit(solution)/shard_map/ppermute | solution.py:415
  10.0 34.2 %collective-permute-start.2 = (bf16[2,64,2048]{2,1,0:T(8,128)(2,1)S(1)}, bf16[2,64,2048]{2,1,0:T(8,128)(2,1)S(1)}, u32[]{:S(2)}, u32[]{:S(2)}) collective-permute-start(bf16[2,64,2048]{2,1,0:T(8,128)(2,1)S(1)} %get-tuple-element.67), channel_id=1, source_target_pairs={{0,12},{4,0},{8,4},{12,8},{1,13},{5,1},{9,5},{13,9},{2,14},{6,2},{... | collective-permute-start | bytes 1572872 | tf_op jit(solution)/shard_map/ppermute | solution.py:415
  18.1 1.1 copy-start.1
  19.2 1.1 copy-start.2
  20.4 0.7 copy-start.3
  21.1 0.7 copy-start.4
  49.0 17.8 %collective-permute-start.15 = (bf16[2,4,64,128]{3,2,1,0:T(8,128)(2,1)S(1)}, bf16[2,4,64,128]{3,2,1,0:T(8,128)(2,1)S(1)}, u32[]{:S(2)}, u32[]{:S(2)}) collective-permute-start(bf16[2,4,64,128]{3,2,1,0:T(8,128)(2,1)S(1)} %get-tuple-element.103), channel_id=1, source_target_pairs={{0,4},{4,8},{8,12},{12,0},{1,5},{5,9},{9,13},{13,1},{2,6},{6,10},{... | collective-permute-start | bytes 393224 | tf_op jit(solution)/shard_map/ppermute | solution.py:415
  60.8 9.7 %collective-permute-start.16 = (bf16[2,4,64,128]{3,2,1,0:T(8,128)(2,1)S(1)}, bf16[2,4,64,128]{3,2,1,0:T(8,128)(2,1)S(1)}, u32[]{:S(2)}, u32[]{:S(2)}) collective-permute-start(bf16[2,4,64,128]{3,2,1,0:T(8,128)(2,1)S(1)} %get-tuple-element.104), channel_id=1, source_target_pairs={{0,8},{4,12},{8,0},{12,4},{1,9},{5,13},{9,1},{13,5},{2,10},{6,14},... | collective-permute-start | bytes 393224 | tf_op jit(solution)/shard_map/ppermute | solution.py:415
  62.3 8.1 %collective-permute-start.17 = (bf16[2,4,64,128]{3,2,1,0:T(8,128)(2,1)S(1)}, bf16[2,4,64,128]{3,2,1,0:T(8,128)(2,1)S(1)}, u32[]{:S(2)}, u32[]{:S(2)}) collective-permute-start(bf16[2,4,64,128]{3,2,1,0:T(8,128)(2,1)S(1)} %get-tuple-element.105), channel_id=1, source_target_pairs={{0,12},{4,0},{8,4},{12,8},{1,13},{5,1},{9,5},{13,9},{2,14},{6,2},{... | collective-permute-start | bytes 393224 | tf_op jit(solution)/shard_map/ppermute | solution.py:415
  71.0 15.0 %collective-permute-start.18 = (bf16[4,2,4,64,128]{4,3,2,1,0:T(8,128)(2,1)S(1)}, bf16[4,2,4,64,128]{4,3,2,1,0:T(8,128)(2,1)S(1)}, u32[]{:S(2)}, u32[]{:S(2)}) collective-permute-start(bf16[4,2,4,64,128]{4,3,2,1,0:T(8,128)(2,1)S(1)} %join_pieces.5.rest_4_), channel_id=1, source_target_pairs={{0,2},{1,3},{2,0},{3,1},{4,6},{5,7},{6,4},{7,5},{8,10},{9,11},{10,... | collective-permute-start | bytes 1572872 | tf_op jit(solution)/shard_map/ppermute | solution.py:422
  72.6 9.3 %collective-permute-start.3 = (bf16[2,4,64,128]{3,2,1,0:T(8,128)(2,1)S(1)}, bf16[2,4,64,128]{3,2,1,0:T(8,128)(2,1)S(1)}, u32[]{:S(2)}, u32[]{:S(2)}) collective-permute-start(bf16[2,4,64,128]{3,2,1,0:T(8,128)(2,1)S(1)} %get-tuple-element.87), channel_id=1, source_target_pairs={{0,4},{4,8},{8,12},{12,0},{1,5},{5,9},{9,13},{13,1},{2,6},{6,10},{... | collective-permute-start | bytes 393224 | tf_op jit(solution)/shard_map/ppermute | solution.py:415
  75.9 10.1 %collective-permute-start.4 = (bf16[2,4,64,128]{3,2,1,0:T(8,128)(2,1)S(1)}, bf16[2,4,64,128]{3,2,1,0:T(8,128)(2,1)S(1)}, u32[]{:S(2)}, u32[]{:S(2)}) collective-permute-start(bf16[2,4,64,128]{3,2,1,0:T(8,128)(2,1)S(1)} %get-tuple-element.88), channel_id=1, source_target_pairs={{0,8},{4,12},{8,0},{12,4},{1,9},{5,13},{9,1},{13,5},{2,10},{6,14},... | collective-permute-start | bytes 393224 | tf_op jit(solution)/shard_map/ppermute | solution.py:415
  77.9 8.1 %collective-permute-start.5 = (bf16[2,4,64,128]{3,2,1,0:T(8,128)(2,1)S(1)}, bf16[2,4,64,128]{3,2,1,0:T(8,128)(2,1)S(1)}, u32[]{:S(2)}, u32[]{:S(2)}) collective-permute-start(bf16[2,4,64,128]{3,2,1,0:T(8,128)(2,1)S(1)} %get-tuple-element.89), channel_id=1, source_target_pairs={{0,12},{4,0},{8,4},{12,8},{1,13},{5,1},{9,5},{13,9},{2,14},{6,2},{... | collective-permute-start | bytes 393224 | tf_op jit(solution)/shard_map/ppermute | solution.py:415
  86.7 6.2 %collective-permute-start.20 = (bf16[2,4,2,4,64,128]{5,4,3,2,1,0:T(8,128)(2,1)S(1)}, bf16[2,4,2,4,64,128]{5,4,3,2,1,0:T(8,128)(2,1)S(1)}, u32[]{:S(2)}, u32[]{:S(2)}) collective-permute-start(bf16[2,4,2,4,64,128]{5,4,3,2,1,0:T(8,128)(2,1)S(1)} %get-tuple-element.107.low_ref), channel_id=1, source_target_pairs={{0,1},{1,0},{2,3},{3,2},{4,5},{5,4},{6,7},{7,6},{8,9},{9,8},{10,11... | collective-permute-start | bytes 3145736 | tf_op jit(solution)/shard_map/ppermute | solution.py:422
  86.8 14.3 %collective-permute-start.19 = (bf16[4,2,4,64,128]{4,3,2,1,0:T(8,128)(2,1)S(1)}, bf16[4,2,4,64,128]{4,3,2,1,0:T(8,128)(2,1)S(1)}, u32[]{:S(2)}, u32[]{:S(2)}) collective-permute-start(bf16[4,2,4,64,128]{4,3,2,1,0:T(8,128)(2,1)S(1)} %get-tuple-element.106.rest_4_), channel_id=1, source_target_pairs={{0,2},{1,3},{2,0},{3,1},{4,6},{5,7},{6,4},{7,5},{8,10},{9,11},{10,... | collective-permute-start | bytes 1572872 | tf_op jit(solution)/shard_map/ppermute | solution.py:422
  87.4 11.3 %collective-permute-start.6 = (bf16[2,4,64,128]{3,2,1,0:T(8,128)(2,1)S(1)}, bf16[2,4,64,128]{3,2,1,0:T(8,128)(2,1)S(1)}, u32[]{:S(2)}, u32[]{:S(2)}) collective-permute-start(bf16[2,4,64,128]{3,2,1,0:T(8,128)(2,1)S(1)} %get-tuple-element.91), channel_id=1, source_target_pairs={{0,4},{4,8},{8,12},{12,0},{1,5},{5,9},{9,13},{13,1},{2,6},{6,10},{... | collective-permute-start | bytes 393224 | tf_op jit(solution)/shard_map/ppermute | solution.py:415
  90.6 10.5 %collective-permute-start.7 = (bf16[2,4,64,128]{3,2,1,0:T(8,128)(2,1)S(1)}, bf16[2,4,64,128]{3,2,1,0:T(8,128)(2,1)S(1)}, u32[]{:S(2)}, u32[]{:S(2)}) collective-permute-start(bf16[2,4,64,128]{3,2,1,0:T(8,128)(2,1)S(1)} %get-tuple-element.92), channel_id=1, source_target_pairs={{0,8},{4,12},{8,0},{12,4},{1,9},{5,13},{9,1},{13,5},{2,10},{6,14},... | collective-permute-start | bytes 393224 | tf_op jit(solution)/shard_map/ppermute | solution.py:415
  92.0 9.0 %collective-permute-start.8 = (bf16[2,4,64,128]{3,2,1,0:T(8,128)(2,1)S(1)}, bf16[2,4,64,128]{3,2,1,0:T(8,128)(2,1)S(1)}, u32[]{:S(2)}, u32[]{:S(2)}) collective-permute-start(bf16[2,4,64,128]{3,2,1,0:T(8,128)(2,1)S(1)} %get-tuple-element.93), channel_id=1, source_target_pairs={{0,12},{4,0},{8,4},{12,8},{1,13},{5,1},{9,5},{13,9},{2,14},{6,2},{... | collective-permute-start | bytes 393224 | tf_op jit(solution)/shard_map/ppermute | solution.py:415
  101.8 7.1 %collective-permute-start.22 = (bf16[2,4,2,4,64,128]{5,4,3,2,1,0:T(8,128)(2,1)S(1)}, bf16[2,4,2,4,64,128]{5,4,3,2,1,0:T(8,128)(2,1)S(1)}, u32[]{:S(2)}, u32[]{:S(2)}) collective-permute-start(bf16[2,4,2,4,64,128]{5,4,3,2,1,0:T(8,128)(2,1)S(1)} %get-tuple-element.110.low_ref), channel_id=1, source_target_pairs={{0,1},{1,0},{2,3},{3,2},{4,5},{5,4},{6,7},{7,6},{8,9},{9,8},{10,11... | collective-permute-start | bytes 3145736 | tf_op jit(solution)/shard_map/ppermute | solution.py:422
  101.9 14.3 %collective-permute-start.21 = (bf16[4,2,4,64,128]{4,3,2,1,0:T(8,128)(2,1)S(1)}, bf16[4,2,4,64,128]{4,3,2,1,0:T(8,128)(2,1)S(1)}, u32[]{:S(2)}, u32[]{:S(2)}) collective-permute-start(bf16[4,2,4,64,128]{4,3,2,1,0:T(8,128)(2,1)S(1)} %get-tuple-element.109.rest_4_), channel_id=1, source_target_pairs={{0,2},{1,3},{2,0},{3,1},{4,6},{5,7},{6,4},{7,5},{8,10},{9,11},{10,... | collective-permute-start | bytes 1572872 | tf_op jit(solution)/shard_map/ppermute | solution.py:422
  103.2 11.4 %collective-permute-start.9 = (bf16[2,4,32,128]{3,2,1,0:T(8,128)(2,1)S(1)}, bf16[2,4,32,128]{3,2,1,0:T(8,128)(2,1)S(1)}, u32[]{:S(2)}, u32[]{:S(2)}) collective-permute-start(bf16[2,4,32,128]{3,2,1,0:T(8,128)(2,1)S(1)} %get-tuple-element.95), channel_id=1, source_target_pairs={{0,4},{4,8},{8,12},{12,0},{1,5},{5,9},{9,13},{13,1},{2,6},{6,10},{... | collective-permute-start | bytes 196616 | tf_op jit(solution)/shard_map/ppermute | solution.py:415
  106.5 8.2 %collective-permute-start.10 = (bf16[2,4,32,128]{3,2,1,0:T(8,128)(2,1)S(1)}, bf16[2,4,32,128]{3,2,1,0:T(8,128)(2,1)S(1)}, u32[]{:S(2)}, u32[]{:S(2)}) collective-permute-start(bf16[2,4,32,128]{3,2,1,0:T(8,128)(2,1)S(1)} %get-tuple-element.96), channel_id=1, source_target_pairs={{0,8},{4,12},{8,0},{12,4},{1,9},{5,13},{9,1},{13,5},{2,10},{6,14},... | collective-permute-start | bytes 196616 | tf_op jit(solution)/shard_map/ppermute | solution.py:415
  108.0 6.6 %collective-permute-start.11 = (bf16[2,4,32,128]{3,2,1,0:T(8,128)(2,1)S(1)}, bf16[2,4,32,128]{3,2,1,0:T(8,128)(2,1)S(1)}, u32[]{:S(2)}, u32[]{:S(2)}) collective-permute-start(bf16[2,4,32,128]{3,2,1,0:T(8,128)(2,1)S(1)} %get-tuple-element.97), channel_id=1, source_target_pairs={{0,12},{4,0},{8,4},{12,8},{1,13},{5,1},{9,5},{13,9},{2,14},{6,2},{... | collective-permute-start | bytes 196616 | tf_op jit(solution)/shard_map/ppermute | solution.py:415
  116.9 7.1 %collective-permute-start.24 = (bf16[2,4,2,4,64,128]{5,4,3,2,1,0:T(8,128)(2,1)S(1)}, bf16[2,4,2,4,64,128]{5,4,3,2,1,0:T(8,128)(2,1)S(1)}, u32[]{:S(2)}, u32[]{:S(2)}) collective-permute-start(bf16[2,4,2,4,64,128]{5,4,3,2,1,0:T(8,128)(2,1)S(1)} %get-tuple-element.114.low_ref), channel_id=1, source_target_pairs={{0,1},{1,0},{2,3},{3,2},{4,5},{5,4},{6,7},{7,6},{8,9},{9,8},{10,11... | collective-permute-start | bytes 3145736 | tf_op jit(solution)/shard_map/ppermute | solution.py:422
  116.9 13.0 %collective-permute-start.23 = (bf16[4,2,4,32,128]{4,3,2,1,0:T(8,128)(2,1)S(1)}, bf16[4,2,4,32,128]{4,3,2,1,0:T(8,128)(2,1)S(1)}, u32[]{:S(2)}, u32[]{:S(2)}) collective-permute-start(bf16[4,2,4,32,128]{4,3,2,1,0:T(8,128)(2,1)S(1)} %get-tuple-element.113.rest_4_), channel_id=1, source_target_pairs={{0,2},{1,3},{2,0},{3,1},{4,6},{5,7},{6,4},{7,5},{8,10},{9,11},{10,... | collective-permute-start | bytes 786440 | tf_op jit(solution)/shard_map/ppermute | solution.py:422
  118.3 11.6 %collective-permute-start.12 = (bf16[2,4,32,128]{3,2,1,0:T(8,128)(2,1)S(1)}, bf16[2,4,32,128]{3,2,1,0:T(8,128)(2,1)S(1)}, u32[]{:S(2)}, u32[]{:S(2)}) collective-permute-start(bf16[2,4,32,128]{3,2,1,0:T(8,128)(2,1)S(1)} %get-tuple-element.99), channel_id=1, source_target_pairs={{0,4},{4,8},{8,12},{12,0},{1,5},{5,9},{9,13},{13,1},{2,6},{6,10},{... | collective-permute-start | bytes 196616 | tf_op jit(solution)/shard_map/ppermute | solution.py:415
  121.5 8.4 %collective-permute-start.13 = (bf16[2,4,32,128]{3,2,1,0:T(8,128)(2,1)S(1)}, bf16[2,4,32,128]{3,2,1,0:T(8,128)(2,1)S(1)}, u32[]{:S(2)}, u32[]{:S(2)}) collective-permute-start(bf16[2,4,32,128]{3,2,1,0:T(8,128)(2,1)S(1)} %get-tuple-element.100), channel_id=1, source_target_pairs={{0,8},{4,12},{8,0},{12,4},{1,9},{5,13},{9,1},{13,5},{2,10},{6,14},... | collective-permute-start | bytes 196616 | tf_op jit(solution)/shard_map/ppermute | solution.py:415
  123.1 6.8 %collective-permute-start.14 = (bf16[2,4,32,128]{3,2,1,0:T(8,128)(2,1)S(1)}, bf16[2,4,32,128]{3,2,1,0:T(8,128)(2,1)S(1)}, u32[]{:S(2)}, u32[]{:S(2)}) collective-permute-start(bf16[2,4,32,128]{3,2,1,0:T(8,128)(2,1)S(1)} %get-tuple-element.101), channel_id=1, source_target_pairs={{0,12},{4,0},{8,4},{12,8},{1,13},{5,1},{9,5},{13,9},{2,14},{6,2},{... | collective-permute-start | bytes 196616 | tf_op jit(solution)/shard_map/ppermute | solution.py:415
  130.5 2.0 %collective-permute-start.26 = (bf16[2,4,2,4,32,128]{5,4,3,2,1,0:T(8,128)(2,1)S(1)}, bf16[2,4,2,4,32,128]{5,4,3,2,1,0:T(8,128)(2,1)S(1)}, u32[]{:S(2)}, u32[]{:S(2)}) collective-permute-start(bf16[2,4,2,4,32,128]{5,4,3,2,1,0:T(8,128)(2,1)S(1)} %get-tuple-element.118.low_ref), channel_id=1, source_target_pairs={{0,1},{1,0},{2,3},{3,2},{4,5},{5,4},{6,7},{7,6},{8,9},{9,8},{10,11... | collective-permute-start | bytes 1572872 | tf_op jit(solution)/shard_map/ppermute | solution.py:422
  130.6 8.7 %collective-permute-start.25 = (bf16[4,2,4,32,128]{4,3,2,1,0:T(8,128)(2,1)S(1)}, bf16[4,2,4,32,128]{4,3,2,1,0:T(8,128)(2,1)S(1)}, u32[]{:S(2)}, u32[]{:S(2)}) collective-permute-start(bf16[4,2,4,32,128]{4,3,2,1,0:T(8,128)(2,1)S(1)} %get-tuple-element.117.own_ref), channel_id=1, source_target_pairs={{0,2},{1,3},{2,0},{3,1},{4,6},{5,7},{6,4},{7,5},{8,10},{9,11},{10,... | collective-permute-start | bytes 786440 | tf_op jit(solution)/shard_map/ppermute | solution.py:422
  139.4 2.0 %collective-permute-start.27 = (bf16[2,4,2,4,32,128]{5,4,3,2,1,0:T(8,128)(2,1)S(1)}, bf16[2,4,2,4,32,128]{5,4,3,2,1,0:T(8,128)(2,1)S(1)}, u32[]{:S(2)}, u32[]{:S(2)}) collective-permute-start(bf16[2,4,2,4,32,128]{5,4,3,2,1,0:T(8,128)(2,1)S(1)} %pair_blocks.1.low_ref), channel_id=1, source_target_pairs={{0,1},{1,0},{2,3},{3,2},{4,5},{5,4},{6,7},{7,6},{8,9},{9,8},{10,11... | collective-permute-start | bytes 1572872 | tf_op jit(solution)/shard_map/ppermute | solution.py:422

commit v3 on v1

--- a/solution.py
+++ b/solution.py
@@ -311,18 +311,16 @@
 
     for at, block in enumerate(order):
         source = (low_ref, high_ref)[at // half].at[at % half]
-
-        @pl.loop(0, senders)
-        def _(sender, block=block, source=source):
+        for sender in range(senders):
             for part in range(2):
                 for chunk in range(chunks):
-                    row = pl.multiple_of(part * side + (chunk * senders + sender) * run, run)
+                    row = part * side + (chunk * senders + sender) * run
                     pieces = [
                         source[sender, part, s, chunk * run : (chunk + 1) * run]
                         for s in range(spectra)
                     ]
                     for c in range(coarse):
-                        left[c, block, pl.ds(row, run), :] = jnp.concatenate(
+                        left[c, block, row : row + run, :] = jnp.concatenate(
                             [piece[:, c * AVG : (c + 1) * AVG] for piece in pieces], axis=1
                         )
 

time: 142 us -> 141 us (level)
  Pallas kernels: 37.5 us -> 28.3 us
  waiting for transfers between devices: 47.4 us -> 54.4 us
    pallas_call x4, Pallas kernels: 23.9 us -> 14.7 us  [correlate(): pl.pallas_call(functools.partial(correlate_kernel, chunks, 1.0 / (AVG * s...]
    ppermute x15, waiting for transfers between devices: 36.9 us -> 41.4 us  [spread(): lax.ppermute(pieces[d], 'ft', [(i, (i + d) % count) for i in range(count)])]
    ppermute x8, waiting for transfers between devices: 10.5 us -> 13 us  [exchange(): return lax.ppermute(own, 'bl', [(i, i ^ bit) for i in range(count)])]
  transfers between devices with their start and end apart: 23 -> 23, of which waited for: 11 -> 11; matrix products, arithmetic and copies ran while one was open for 6% -> 6% of each run, Pallas kernels for 15% -> 10%
where the time goes in v3:
time: 141 us; the launch traced here: 139 us
  waiting for transfers between devices  54.4 us (39%)
  starting transfers between devices  42.3 us (30%)
  Pallas kernels  28.3 us (20%)
  local copies, waits for them, and re-layouts  9.17 us (7%)
  other arithmetic  4.61 us (3%)
    ppermute x15, waiting for transfers between devices, spread(): lax.ppermute(pieces[d], 'ft', [(i, (i + d) % count) for i in range(count)])  41.4 us
    ppermute x15, starting transfers between devices, spread(): lax.ppermute(pieces[d], 'ft', [(i, (i + d) % count) for i in range(count)])  37.9 us
    pallas_call x4, Pallas kernels, correlate(): pl.pallas_call(functools.partial(correlate_kernel, chunks, 1.0 / (AVG * s...  14.7 us
    ppermute x8, waiting for transfers between devices, exchange(): return lax.ppermute(own, 'bl', [(i, i ^ bit) for i in range(count)])  13 us
    pallas_call x2, Pallas kernels, transform_cut(): pl.pallas_call(kernel, grid_spec=pltpu.PrefetchScalarGridSpec(num_scalar_...  8.24 us
    unnamed x10, local copies, waits for them, and re-layouts  5.25 us
    ppermute x8, starting transfers between devices, exchange(): return lax.ppermute(own, 'bl', [(i, i ^ bit) for i in range(count)])  4.38 us
    reshape x2, local copies, waits for them, and re-layouts, per_device_kernels(): coef_table = coefs.reshape(taps, MXU, radix).transpose(0, 2, 1)  3.92 us
  transfers between devices with their start and end apart: 23, of which 11 were waited for; matrix products, arithmetic and copies ran while one was open for 6% of the time, Pallas kernels for 10%

profile of v3, /device:TPU:0, one launch (start us, length us, event | category | flops | bytes accessed | tf_op | source)
XLA Modules:
  0.0 139.1 jit_solution(15175096462809665226)
XLA Ops:
  0.0 0.1 pad_add_fusion.1.place_ref
  0.1 1.6 %copy-done = bf16[2,2048,256]{2,1,0:T(8,128)(2,1)S(1)} copy-done((bf16[2,2048,256]{2,1,0:T(8,128)(2,1)S(1)}, bf16[2,2048,256]{2,1,0:T(8,128)(2,1)}, u32[]{:S(2)}) %copy-start) | copy-done | bytes 2097176
  1.7 2.7 %pack_inputs.1 = (bf16[2,64,2048]{2,1,0:T(8,128)(2,1)S(1)}, bf16[2,64,2048]{2,1,0:T(8,128)(2,1)}, bf16[2,64,2048]{2,1,0:T(8,128)(2,1)S(1)}, bf16[2,64,2048]{2,1,0:T(8,128)(2,1)S(1)}) custom-call(s32[8]{0:T(128)S(1)} %pad_add_fusion.1.place_ref, bf16[2,2048,256]{2,1,0:T(8,128)(2,1)S(1)} %copy-done), custom_call_target="tpu_custom_call" | custom-call | tf_op jit(solution)/shard_map/pack_inputs/pallas_call | solution.py:97
  4.4 3.0 %collective-permute-start = (bf16[2,64,2048]{2,1,0:T(8,128)(2,1)}, bf16[2,64,2048]{2,1,0:T(8,128)(2,1)S(1)}, u32[]{:S(2)}, u32[]{:S(2)}) collective-permute-start(bf16[2,64,2048]{2,1,0:T(8,128)(2,1)} %get-tuple-element.53), channel_id=1, source_target_pairs={{0,4},{4,8},{8,12},{12,0},{1,5},{5,9},{9,13},{13,1},{2,6},{6,10},{... | collective-permute-start | bytes 1572872 | tf_op jit(solution)/shard_map/ppermute | solution.py:396
  7.4 2.6 %collective-permute-start.1 = (bf16[2,64,2048]{2,1,0:T(8,128)(2,1)S(1)}, bf16[2,64,2048]{2,1,0:T(8,128)(2,1)S(1)}, u32[]{:S(2)}, u32[]{:S(2)}) collective-permute-start(bf16[2,64,2048]{2,1,0:T(8,128)(2,1)S(1)} %get-tuple-element.54), channel_id=1, source_target_pairs={{0,8},{4,12},{8,0},{12,4},{1,9},{5,13},{9,1},{13,5},{2,10},{6,14},... | collective-permute-start | bytes 1572872 | tf_op jit(solution)/shard_map/ppermute | solution.py:396
  10.0 1.3 collective-permute-start.2
  11.3 0.8 fusion.1
  12.1 2.4 %reshape.11 = f32[8,256,8]{2,1,0:T(8,128)} reshape(f32[8,2048]{1,0:T(8,128)} %param.16) | data formatting | bytes 131072 | tf_op jit(solution)/shard_map/reshape | solution.py:479
  14.5 1.5 %copy.20 = f32[8,256,8]{1,2,0:T(8,128)S(1)} copy(f32[8,256,8]{2,1,0:T(8,128)} %reshape.11) | data formatting | bytes 131072 | tf_op jit(solution)/shard_map/reshape | solution.py:479
  16.0 0.7 broadcast_compare_fusion
  16.7 0.6 reduce_sum.69
  17.3 0.8 select_reduce_fusion.3
  18.1 1.1 copy-done.1
  19.2 1.1 copy-done.2
  20.4 0.7 copy-done.3
  21.0 0.7 copy-done.4
  21.7 0.1 stage_tables.1
  21.9 0.8 multiply_reduce_fusion
  22.7 0.2 select_reduce_fusion.1
  22.8 0.7 pad_add_fusion.rest_7_.rest_3_.rest_6_.table_ref
  23.6 0.0 collective-permute-done.rest_1_
  23.6 20.6 %collective-permute-done.1.rest_2_ = bf16[2,64,2048]{2,1,0:T(8,128)(2,1)S(1)} collective-permute-done((bf16[2,64,2048]{2,1,0:T(8,128)(2,1)S(1)}, bf16[2,64,2048]{2,1,0:T(8,128)(2,1)S(1)}, u32[]{:S(2)}, u32[]{:S(2)}) %collective-permute-start.1) | collective-permute-done | bytes 524320 | tf_op jit(solution)/shard_map/ppermute | solution.py:396
  44.2 0.0 collective-permute-done.2.rest_3_
  44.2 4.8 %filter_transform.1 = (bf16[2,4,64,128]{3,2,1,0:T(8,128)(2,1)S(1)}, bf16[2,4,64,128]{3,2,1,0:T(8,128)(2,1)S(1)}, bf16[2,4,64,128]{3,2,1,0:T(8,128)(2,1)S(1)}, bf...) custom-call(s32[8]{0:T(128)S(1)} %pad_add_fusion.1.place_ref, ...), custom_call_target="tpu_custom_call" | custom-call | flops 1610612736 | bytes 6291456 | tf_op jit(solution)/shard_map/filter_transform/pallas_call | solution.py:226
  49.0 11.8 %collective-permute-start.12 = (bf16[2,4,64,128]{3,2,1,0:T(8,128)(2,1)S(1)}, bf16[2,4,64,128]{3,2,1,0:T(8,128)(2,1)S(1)}, u32[]{:S(2)}, u32[]{:S(2)}) collective-permute-start(bf16[2,4,64,128]{3,2,1,0:T(8,128)(2,1)S(1)} %get-tuple-element.83), channel_id=1, source_target_pairs={{0,4},{4,8},{8,12},{12,0},{1,5},{5,9},{9,13},{13,1},{2,6},{6,10},{... | collective-permute-start | bytes 393224 | tf_op jit(solution)/shard_map/ppermute | solution.py:396
  60.7 1.6 %collective-permute-start.13 = (bf16[2,4,64,128]{3,2,1,0:T(8,128)(2,1)S(1)}, bf16[2,4,64,128]{3,2,1,0:T(8,128)(2,1)S(1)}, u32[]{:S(2)}, u32[]{:S(2)}) collective-permute-start(bf16[2,4,64,128]{3,2,1,0:T(8,128)(2,1)S(1)} %get-tuple-element.84), channel_id=1, source_target_pairs={{0,8},{4,12},{8,0},{12,4},{1,9},{5,13},{9,1},{13,5},{2,10},{6,14},... | collective-permute-start | bytes 393224 | tf_op jit(solution)/shard_map/ppermute | solution.py:396
  62.3 0.8 collective-permute-start.14
  63.2 3.4 %transform_rest.1 = (bf16[2,4,64,128]{3,2,1,0:T(8,128)(2,1)S(1)}, bf16[2,4,64,128]{3,2,1,0:T(8,128)(2,1)S(1)}, bf16[2,4,64,128]{3,2,1,0:T(8,128)(2,1)S(1)}, bf16...) custom-call(s32[8]{0:T(128)S(1)} %pad_add_fusion.1.place_ref, ...), custom_call_target="tpu_custom_call" | custom-call | flops 1610612736 | bytes 6291456 | tf_op jit(solution)/shard_map/transform_rest/pallas_call | solution.py:226
  66.6 3.8 %collective-permute-done.13.rest_2_ = bf16[2,4,64,128]{3,2,1,0:T(8,128)(2,1)S(1)} collective-permute-done((bf16[2,4,64,128]{3,2,1,0:T(8,128)(2,1)S(1)}, bf16[2,4,64,128]{3,2,1,0:T(8,128)(2,1)S(1)}, u32[]{:S(2)}, u32[]{:S(2)}) %collective-permute-start.13) | collective-permute-done | bytes 131104 | tf_op jit(solution)/shard_map/ppermute | solution.py:396
  70.4 0.6 join_pieces.4.rest_4_
  71.0 1.6 %collective-permute-start.15 = (bf16[4,2,4,64,128]{4,3,2,1,0:T(8,128)(2,1)S(1)}, bf16[4,2,4,64,128]{4,3,2,1,0:T(8,128)(2,1)S(1)}, u32[]{:S(2)}, u32[]{:S(2)}) collective-permute-start(bf16[4,2,4,64,128]{4,3,2,1,0:T(8,128)(2,1)S(1)} %join_pieces.4.rest_4_), channel_id=1, source_target_pairs={{0,2},{1,3},{2,0},{3,1},{4,6},{5,7},{6,4},{7,5},{8,10},{9,11},{10,... | collective-permute-start | bytes 1572872 | tf_op jit(solution)/shard_map/ppermute | solution.py:403
  72.6 3.3 %collective-permute-start.3 = (bf16[2,4,64,128]{3,2,1,0:T(8,128)(2,1)S(1)}, bf16[2,4,64,128]{3,2,1,0:T(8,128)(2,1)S(1)}, u32[]{:S(2)}, u32[]{:S(2)}) collective-permute-start(bf16[2,4,64,128]{3,2,1,0:T(8,128)(2,1)S(1)} %get-tuple-element.71), channel_id=1, source_target_pairs={{0,4},{4,8},{8,12},{12,0},{1,5},{5,9},{9,13},{13,1},{2,6},{6,10},{... | collective-permute-start | bytes 393224 | tf_op jit(solution)/shard_map/ppermute | solution.py:396
  75.8 2.1 %collective-permute-start.4 = (bf16[2,4,64,128]{3,2,1,0:T(8,128)(2,1)S(1)}, bf16[2,4,64,128]{3,2,1,0:T(8,128)(2,1)S(1)}, u32[]{:S(2)}, u32[]{:S(2)}) collective-permute-start(bf16[2,4,64,128]{3,2,1,0:T(8,128)(2,1)S(1)} %get-tuple-element.72), channel_id=1, source_target_pairs={{0,8},{4,12},{8,0},{12,4},{1,9},{5,13},{9,1},{13,5},{2,10},{6,14},... | collective-permute-start | bytes 393224 | tf_op jit(solution)/shard_map/ppermute | solution.py:396
  77.9 0.3 collective-permute-start.5
  78.2 3.6 %collective-permute-done.3.rest_1_ = bf16[2,4,64,128]{3,2,1,0:T(8,128)(2,1)S(1)} collective-permute-done((bf16[2,4,64,128]{3,2,1,0:T(8,128)(2,1)S(1)}, bf16[2,4,64,128]{3,2,1,0:T(8,128)(2,1)S(1)}, u32[]{:S(2)}, u32[]{:S(2)}) %collective-permute-start.3) | collective-permute-done | bytes 131104 | tf_op jit(solution)/shard_map/ppermute | solution.py:396
  81.8 4.1 %collective-permute-done.4.rest_2_ = bf16[2,4,64,128]{3,2,1,0:T(8,128)(2,1)S(1)} collective-permute-done((bf16[2,4,64,128]{3,2,1,0:T(8,128)(2,1)S(1)}, bf16[2,4,64,128]{3,2,1,0:T(8,128)(2,1)S(1)}, u32[]{:S(2)}, u32[]{:S(2)}) %collective-permute-start.4) | collective-permute-done | bytes 131104 | tf_op jit(solution)/shard_map/ppermute | solution.py:396
  85.9 0.1 collective-permute-done.5.rest_3_
  86.1 0.6 join_pieces.5
  86.7 0.1 collective-permute-start.17
  86.8 0.6 collective-permute-start.16
  87.4 3.1 %collective-permute-start.6 = (bf16[2,4,64,128]{3,2,1,0:T(8,128)(2,1)S(1)}, bf16[2,4,64,128]{3,2,1,0:T(8,128)(2,1)S(1)}, u32[]{:S(2)}, u32[]{:S(2)}) collective-permute-start(bf16[2,4,64,128]{3,2,1,0:T(8,128)(2,1)S(1)} %get-tuple-element.75), channel_id=1, source_target_pairs={{0,4},{4,8},{8,12},{12,0},{1,5},{5,9},{9,13},{13,1},{2,6},{6,10},{... | collective-permute-start | bytes 393224 | tf_op jit(solution)/shard_map/ppermute | solution.py:396
  90.5 1.5 %collective-permute-start.7 = (bf16[2,4,64,128]{3,2,1,0:T(8,128)(2,1)S(1)}, bf16[2,4,64,128]{3,2,1,0:T(8,128)(2,1)S(1)}, u32[]{:S(2)}, u32[]{:S(2)}) collective-permute-start(bf16[2,4,64,128]{3,2,1,0:T(8,128)(2,1)S(1)} %get-tuple-element.76), channel_id=1, source_target_pairs={{0,8},{4,12},{8,0},{12,4},{1,9},{5,13},{9,1},{13,5},{2,10},{6,14},... | collective-permute-start | bytes 393224 | tf_op jit(solution)/shard_map/ppermute | solution.py:396
  92.0 0.9 collective-permute-start.8
  92.9 3.5 %correlate_tiles.4 = (f32[2,8,5,256,256]{4,3,2,1,0:T(8,128)}, f32[8,128]{1,0:T(8,128)S(1)}) custom-call(s32[11]{0:T(128)S(1)} %pad_add_fusion.rest_7_.rest_3_.rest_6_.table_ref, bf16[2,4,2,4,64,128]{5,4,3,2,1,0:T(8,128)(2,1)S(1)} %get-tuple-element.87.low_ref, bf16[2,4,2,4,64,128]{5,4,3,2,1,0:T(8,128)(2,1)S(1)} %collective-permute-done.17.high_ref), custom_call_target="tpu_custom_call" | custom-call | tf_op jit(solution)/shard_map/correlate_tiles/pallas_call | solution.py:362
  96.5 4.5 %collective-permute-done.7.rest_2_ = bf16[2,4,64,128]{3,2,1,0:T(8,128)(2,1)S(1)} collective-permute-done((bf16[2,4,64,128]{3,2,1,0:T(8,128)(2,1)S(1)}, bf16[2,4,64,128]{3,2,1,0:T(8,128)(2,1)S(1)}, u32[]{:S(2)}, u32[]{:S(2)}) %collective-permute-start.7) | collective-permute-done | bytes 131104 | tf_op jit(solution)/shard_map/ppermute | solution.py:396
  101.0 0.1 collective-permute-done.16.rest_5_
  101.1 0.6 join_pieces.6
  101.8 0.1 collective-permute-start.19
  101.9 1.3 collective-permute-start.18
  103.2 3.3 %collective-permute-start.9 = (bf16[2,4,64,128]{3,2,1,0:T(8,128)(2,1)S(1)}, bf16[2,4,64,128]{3,2,1,0:T(8,128)(2,1)S(1)}, u32[]{:S(2)}, u32[]{:S(2)}) collective-permute-start(bf16[2,4,64,128]{3,2,1,0:T(8,128)(2,1)S(1)} %get-tuple-element.79), channel_id=1, source_target_pairs={{0,4},{4,8},{8,12},{12,0},{1,5},{5,9},{9,13},{13,1},{2,6},{6,10},{... | collective-permute-start | bytes 393224 | tf_op jit(solution)/shard_map/ppermute | solution.py:396
  106.5 1.5 %collective-permute-start.10 = (bf16[2,4,64,128]{3,2,1,0:T(8,128)(2,1)S(1)}, bf16[2,4,64,128]{3,2,1,0:T(8,128)(2,1)S(1)}, u32[]{:S(2)}, u32[]{:S(2)}) collective-permute-start(bf16[2,4,64,128]{3,2,1,0:T(8,128)(2,1)S(1)} %get-tuple-element.80), channel_id=1, source_target_pairs={{0,8},{4,12},{8,0},{12,4},{1,9},{5,13},{9,1},{13,5},{2,10},{6,14},... | collective-permute-start | bytes 393224 | tf_op jit(solution)/shard_map/ppermute | solution.py:396
  108.0 0.8 collective-permute-start.11
  108.8 3.5 %correlate_tiles.5 = (f32[2,8,5,256,256]{4,3,2,1,0:T(8,128)}, f32[8,128]{1,0:T(8,128)S(1)}) custom-call(s32[11]{0:T(128)S(1)} %pad_add_fusion.rest_7_.rest_3_.rest_6_.table_ref, bf16[2,4,2,4,64,128]{5,4,3,2,1,0:T(8,128)(2,1)S(1)} %get-tuple-element.90.low_ref, ...), custom_call_target="tpu_custom_call", output_to_operand_aliasing={{0}: (3, {})} | custom-call | tf_op jit(solution)/shard_map/correlate_tiles/pallas_call | solution.py:362
  112.4 4.6 %collective-permute-done.10.rest_2_ = bf16[2,4,64,128]{3,2,1,0:T(8,128)(2,1)S(1)} collective-permute-done((bf16[2,4,64,128]{3,2,1,0:T(8,128)(2,1)S(1)}, bf16[2,4,64,128]{3,2,1,0:T(8,128)(2,1)S(1)}, u32[]{:S(2)}, u32[]{:S(2)}) %collective-permute-start.10) | collective-permute-done | bytes 131104 | tf_op jit(solution)/shard_map/ppermute | solution.py:396
  117.0 0.6 join_pieces.7
  117.6 0.1 collective-permute-start.21
  117.7 0.6 collective-permute-start.20
  118.3 2.0 %collective-permute-done.21.high_ref = bf16[2,4,2,4,64,128]{5,4,3,2,1,0:T(8,128)(2,1)S(1)} collective-permute-done((bf16[2,4,2,4,64,128]{5,4,3,2,1,0:T(8,128)(2,1)S(1)}, bf16[2,4,2,4,64,128]{5,4,3,2,1,0:T(8,128)(2,1)S(1)}, u32[]{:S(2)}, u32[]{:S(2)}) %collective-permute-start.21) | collective-permute-done | bytes 1048608 | tf_op jit(solution)/shard_map/ppermute | solution.py:403
  120.4 3.5 %correlate_tiles.6 = (f32[2,8,5,256,256]{4,3,2,1,0:T(8,128)}, f32[8,128]{1,0:T(8,128)S(1)}) custom-call(s32[11]{0:T(128)S(1)} %pad_add_fusion.rest_7_.rest_3_.rest_6_.table_ref, bf16[2,4,2,4,64,128]{5,4,3,2,1,0:T(8,128)(2,1)S(1)} %get-tuple-element.94.low_ref, ...), custom_call_target="tpu_custom_call", output_to_operand_aliasing={{0}: (3, {})} | custom-call | tf_op jit(solution)/shard_map/correlate_tiles/pallas_call | solution.py:362
  123.9 8.1 %collective-permute-done.20.other_ref = bf16[4,2,4,64,128]{4,3,2,1,0:T(8,128)(2,1)S(1)} collective-permute-done((bf16[4,2,4,64,128]{4,3,2,1,0:T(8,128)(2,1)S(1)}, bf16[4,2,4,64,128]{4,3,2,1,0:T(8,128)(2,1)S(1)}, u32[]{:S(2)}, u32[]{:S(2)}) %collective-permute-start.20) | collective-permute-done | bytes 524320 | tf_op jit(solution)/shard_map/ppermute | solution.py:403
  132.1 0.1 pair_blocks.1.low_ref
  132.1 0.1 collective-permute-start.22
  132.2 2.6 %collective-permute-done.22.high_ref = bf16[2,4,2,4,64,128]{5,4,3,2,1,0:T(8,128)(2,1)S(1)} collective-permute-done((bf16[2,4,2,4,64,128]{5,4,3,2,1,0:T(8,128)(2,1)S(1)}, bf16[2,4,2,4,64,128]{5,4,3,2,1,0:T(8,128)(2,1)S(1)}, u32[]{:S(2)}, u32[]{:S(2)}) %collective-permute-start.22) | collective-permute-done | bytes 1048608 | tf_op jit(solution)/shard_map/ppermute | solution.py:403
  134.9 4.1 %correlate_tiles.7 = (f32[2,8,5,256,256]{4,3,2,1,0:T(8,128)}, f32[8,128]{1,0:T(8,128)}) custom-call(s32[11]{0:T(128)S(1)} %pad_add_fusion.rest_7_.rest_3_.rest_6_.table_ref, bf16[2,4,2,4,64,128]{5,4,3,2,1,0:T(8,128)(2,1)S(1)} %pair_blocks.1.low_ref, ...), custom_call_target="tpu_custom_call", output_to_operand_aliasing={{0}: (3, {})} | custom-call | tf_op jit(solution)/shard_map/correlate_tiles/pallas_call | solution.py:362
  (17 shorter events, 0.1 us)
Async XLA Ops:
  0.1 1.6 %copy-start = (bf16[2,2048,256]{2,1,0:T(8,128)(2,1)S(1)}, bf16[2,2048,256]{2,1,0:T(8,128)(2,1)}, u32[]{:S(2)}) copy-start(bf16[2,2048,256]{2,1,0:T(8,128)(2,1)} %v_ref.1) | copy-start | bytes 6291460
  4.4 19.2 %collective-permute-start = (bf16[2,64,2048]{2,1,0:T(8,128)(2,1)}, bf16[2,64,2048]{2,1,0:T(8,128)(2,1)S(1)}, u32[]{:S(2)}, u32[]{:S(2)}) collective-permute-start(bf16[2,64,2048]{2,1,0:T(8,128)(2,1)} %get-tuple-element.53), channel_id=1, source_target_pairs={{0,4},{4,8},{8,12},{12,0},{1,5},{5,9},{9,13},{13,1},{2,6},{6,10},{... | collective-permute-start | bytes 1572872 | tf_op jit(solution)/shard_map/ppermute | solution.py:396
  7.4 36.8 %collective-permute-start.1 = (bf16[2,64,2048]{2,1,0:T(8,128)(2,1)S(1)}, bf16[2,64,2048]{2,1,0:T(8,128)(2,1)S(1)}, u32[]{:S(2)}, u32[]{:S(2)}) collective-permute-start(bf16[2,64,2048]{2,1,0:T(8,128)(2,1)S(1)} %get-tuple-element.54), channel_id=1, source_target_pairs={{0,8},{4,12},{8,0},{12,4},{1,9},{5,13},{9,1},{13,5},{2,10},{6,14},... | collective-permute-start | bytes 1572872 | tf_op jit(solution)/shard_map/ppermute | solution.py:396
  10.0 34.2 %collective-permute-start.2 = (bf16[2,64,2048]{2,1,0:T(8,128)(2,1)S(1)}, bf16[2,64,2048]{2,1,0:T(8,128)(2,1)S(1)}, u32[]{:S(2)}, u32[]{:S(2)}) collective-permute-start(bf16[2,64,2048]{2,1,0:T(8,128)(2,1)S(1)} %get-tuple-element.55), channel_id=1, source_target_pairs={{0,12},{4,0},{8,4},{12,8},{1,13},{5,1},{9,5},{13,9},{2,14},{6,2},{... | collective-permute-start | bytes 1572872 | tf_op jit(solution)/shard_map/ppermute | solution.py:396
  18.1 1.1 copy-start.1
  19.2 1.1 copy-start.2
  20.3 0.7 copy-start.3
  21.0 0.7 copy-start.4
  49.0 17.6 %collective-permute-start.12 = (bf16[2,4,64,128]{3,2,1,0:T(8,128)(2,1)S(1)}, bf16[2,4,64,128]{3,2,1,0:T(8,128)(2,1)S(1)}, u32[]{:S(2)}, u32[]{:S(2)}) collective-permute-start(bf16[2,4,64,128]{3,2,1,0:T(8,128)(2,1)S(1)} %get-tuple-element.83), channel_id=1, source_target_pairs={{0,4},{4,8},{8,12},{12,0},{1,5},{5,9},{9,13},{13,1},{2,6},{6,10},{... | collective-permute-start | bytes 393224 | tf_op jit(solution)/shard_map/ppermute | solution.py:396
  60.7 9.7 %collective-permute-start.13 = (bf16[2,4,64,128]{3,2,1,0:T(8,128)(2,1)S(1)}, bf16[2,4,64,128]{3,2,1,0:T(8,128)(2,1)S(1)}, u32[]{:S(2)}, u32[]{:S(2)}) collective-permute-start(bf16[2,4,64,128]{3,2,1,0:T(8,128)(2,1)S(1)} %get-tuple-element.84), channel_id=1, source_target_pairs={{0,8},{4,12},{8,0},{12,4},{1,9},{5,13},{9,1},{13,5},{2,10},{6,14},... | collective-permute-start | bytes 393224 | tf_op jit(solution)/shard_map/ppermute | solution.py:396
  62.3 8.1 %collective-permute-start.14 = (bf16[2,4,64,128]{3,2,1,0:T(8,128)(2,1)S(1)}, bf16[2,4,64,128]{3,2,1,0:T(8,128)(2,1)S(1)}, u32[]{:S(2)}, u32[]{:S(2)}) collective-permute-start(bf16[2,4,64,128]{3,2,1,0:T(8,128)(2,1)S(1)} %get-tuple-element.85), channel_id=1, source_target_pairs={{0,12},{4,0},{8,4},{12,8},{1,13},{5,1},{9,5},{13,9},{2,14},{6,2},{... | collective-permute-start | bytes 393224 | tf_op jit(solution)/shard_map/ppermute | solution.py:396
  71.0 15.1 %collective-permute-start.15 = (bf16[4,2,4,64,128]{4,3,2,1,0:T(8,128)(2,1)S(1)}, bf16[4,2,4,64,128]{4,3,2,1,0:T(8,128)(2,1)S(1)}, u32[]{:S(2)}, u32[]{:S(2)}) collective-permute-start(bf16[4,2,4,64,128]{4,3,2,1,0:T(8,128)(2,1)S(1)} %join_pieces.4.rest_4_), channel_id=1, source_target_pairs={{0,2},{1,3},{2,0},{3,1},{4,6},{5,7},{6,4},{7,5},{8,10},{9,11},{10,... | collective-permute-start | bytes 1572872 | tf_op jit(solution)/shard_map/ppermute | solution.py:403
  72.6 9.3 %collective-permute-start.3 = (bf16[2,4,64,128]{3,2,1,0:T(8,128)(2,1)S(1)}, bf16[2,4,64,128]{3,2,1,0:T(8,128)(2,1)S(1)}, u32[]{:S(2)}, u32[]{:S(2)}) collective-permute-start(bf16[2,4,64,128]{3,2,1,0:T(8,128)(2,1)S(1)} %get-tuple-element.71), channel_id=1, source_target_pairs={{0,4},{4,8},{8,12},{12,0},{1,5},{5,9},{9,13},{13,1},{2,6},{6,10},{... | collective-permute-start | bytes 393224 | tf_op jit(solution)/shard_map/ppermute | solution.py:396
  75.8 10.1 %collective-permute-start.4 = (bf16[2,4,64,128]{3,2,1,0:T(8,128)(2,1)S(1)}, bf16[2,4,64,128]{3,2,1,0:T(8,128)(2,1)S(1)}, u32[]{:S(2)}, u32[]{:S(2)}) collective-permute-start(bf16[2,4,64,128]{3,2,1,0:T(8,128)(2,1)S(1)} %get-tuple-element.72), channel_id=1, source_target_pairs={{0,8},{4,12},{8,0},{12,4},{1,9},{5,13},{9,1},{13,5},{2,10},{6,14},... | collective-permute-start | bytes 393224 | tf_op jit(solution)/shard_map/ppermute | solution.py:396
  77.9 8.1 %collective-permute-start.5 = (bf16[2,4,64,128]{3,2,1,0:T(8,128)(2,1)S(1)}, bf16[2,4,64,128]{3,2,1,0:T(8,128)(2,1)S(1)}, u32[]{:S(2)}, u32[]{:S(2)}) collective-permute-start(bf16[2,4,64,128]{3,2,1,0:T(8,128)(2,1)S(1)} %get-tuple-element.73), channel_id=1, source_target_pairs={{0,12},{4,0},{8,4},{12,8},{1,13},{5,1},{9,5},{13,9},{2,14},{6,2},{... | collective-permute-start | bytes 393224 | tf_op jit(solution)/shard_map/ppermute | solution.py:396
  86.7 6.2 %collective-permute-start.17 = (bf16[2,4,2,4,64,128]{5,4,3,2,1,0:T(8,128)(2,1)S(1)}, bf16[2,4,2,4,64,128]{5,4,3,2,1,0:T(8,128)(2,1)S(1)}, u32[]{:S(2)}, u32[]{:S(2)}) collective-permute-start(bf16[2,4,2,4,64,128]{5,4,3,2,1,0:T(8,128)(2,1)S(1)} %get-tuple-element.87.low_ref), channel_id=1, source_target_pairs={{0,1},{1,0},{2,3},{3,2},{4,5},{5,4},{6,7},{7,6},{8,9},{9,8},{10,11... | collective-permute-start | bytes 3145736 | tf_op jit(solution)/shard_map/ppermute | solution.py:403
  86.8 14.3 %collective-permute-start.16 = (bf16[4,2,4,64,128]{4,3,2,1,0:T(8,128)(2,1)S(1)}, bf16[4,2,4,64,128]{4,3,2,1,0:T(8,128)(2,1)S(1)}, u32[]{:S(2)}, u32[]{:S(2)}) collective-permute-start(bf16[4,2,4,64,128]{4,3,2,1,0:T(8,128)(2,1)S(1)} %get-tuple-element.86.rest_4_), channel_id=1, source_target_pairs={{0,2},{1,3},{2,0},{3,1},{4,6},{5,7},{6,4},{7,5},{8,10},{9,11},{10,... | collective-permute-start | bytes 1572872 | tf_op jit(solution)/shard_map/ppermute | solution.py:403
  87.4 9.1 %collective-permute-start.6 = (bf16[2,4,64,128]{3,2,1,0:T(8,128)(2,1)S(1)}, bf16[2,4,64,128]{3,2,1,0:T(8,128)(2,1)S(1)}, u32[]{:S(2)}, u32[]{:S(2)}) collective-permute-start(bf16[2,4,64,128]{3,2,1,0:T(8,128)(2,1)S(1)} %get-tuple-element.75), channel_id=1, source_target_pairs={{0,4},{4,8},{8,12},{12,0},{1,5},{5,9},{9,13},{13,1},{2,6},{6,10},{... | collective-permute-start | bytes 393224 | tf_op jit(solution)/shard_map/ppermute | solution.py:396
  90.5 10.5 %collective-permute-start.7 = (bf16[2,4,64,128]{3,2,1,0:T(8,128)(2,1)S(1)}, bf16[2,4,64,128]{3,2,1,0:T(8,128)(2,1)S(1)}, u32[]{:S(2)}, u32[]{:S(2)}) collective-permute-start(bf16[2,4,64,128]{3,2,1,0:T(8,128)(2,1)S(1)} %get-tuple-element.76), channel_id=1, source_target_pairs={{0,8},{4,12},{8,0},{12,4},{1,9},{5,13},{9,1},{13,5},{2,10},{6,14},... | collective-permute-start | bytes 393224 | tf_op jit(solution)/shard_map/ppermute | solution.py:396
  92.0 9.0 %collective-permute-start.8 = (bf16[2,4,64,128]{3,2,1,0:T(8,128)(2,1)S(1)}, bf16[2,4,64,128]{3,2,1,0:T(8,128)(2,1)S(1)}, u32[]{:S(2)}, u32[]{:S(2)}) collective-permute-start(bf16[2,4,64,128]{3,2,1,0:T(8,128)(2,1)S(1)} %get-tuple-element.77), channel_id=1, source_target_pairs={{0,12},{4,0},{8,4},{12,8},{1,13},{5,1},{9,5},{13,9},{2,14},{6,2},{... | collective-permute-start | bytes 393224 | tf_op jit(solution)/shard_map/ppermute | solution.py:396
  101.8 7.1 %collective-permute-start.19 = (bf16[2,4,2,4,64,128]{5,4,3,2,1,0:T(8,128)(2,1)S(1)}, bf16[2,4,2,4,64,128]{5,4,3,2,1,0:T(8,128)(2,1)S(1)}, u32[]{:S(2)}, u32[]{:S(2)}) collective-permute-start(bf16[2,4,2,4,64,128]{5,4,3,2,1,0:T(8,128)(2,1)S(1)} %get-tuple-element.90.low_ref), channel_id=1, source_target_pairs={{0,1},{1,0},{2,3},{3,2},{4,5},{5,4},{6,7},{7,6},{8,9},{9,8},{10,11... | collective-permute-start | bytes 3145736 | tf_op jit(solution)/shard_map/ppermute | solution.py:403
  101.9 15.1 %collective-permute-start.18 = (bf16[4,2,4,64,128]{4,3,2,1,0:T(8,128)(2,1)S(1)}, bf16[4,2,4,64,128]{4,3,2,1,0:T(8,128)(2,1)S(1)}, u32[]{:S(2)}, u32[]{:S(2)}) collective-permute-start(bf16[4,2,4,64,128]{4,3,2,1,0:T(8,128)(2,1)S(1)} %get-tuple-element.89.rest_4_), channel_id=1, source_target_pairs={{0,2},{1,3},{2,0},{3,1},{4,6},{5,7},{6,4},{7,5},{8,10},{9,11},{10,... | collective-permute-start | bytes 1572872 | tf_op jit(solution)/shard_map/ppermute | solution.py:403
  103.2 9.2 %collective-permute-start.9 = (bf16[2,4,64,128]{3,2,1,0:T(8,128)(2,1)S(1)}, bf16[2,4,64,128]{3,2,1,0:T(8,128)(2,1)S(1)}, u32[]{:S(2)}, u32[]{:S(2)}) collective-permute-start(bf16[2,4,64,128]{3,2,1,0:T(8,128)(2,1)S(1)} %get-tuple-element.79), channel_id=1, source_target_pairs={{0,4},{4,8},{8,12},{12,0},{1,5},{5,9},{9,13},{13,1},{2,6},{6,10},{... | collective-permute-start | bytes 393224 | tf_op jit(solution)/shard_map/ppermute | solution.py:396
  106.5 10.5 %collective-permute-start.10 = (bf16[2,4,64,128]{3,2,1,0:T(8,128)(2,1)S(1)}, bf16[2,4,64,128]{3,2,1,0:T(8,128)(2,1)S(1)}, u32[]{:S(2)}, u32[]{:S(2)}) collective-permute-start(bf16[2,4,64,128]{3,2,1,0:T(8,128)(2,1)S(1)} %get-tuple-element.80), channel_id=1, source_target_pairs={{0,8},{4,12},{8,0},{12,4},{1,9},{5,13},{9,1},{13,5},{2,10},{6,14},... | collective-permute-start | bytes 393224 | tf_op jit(solution)/shard_map/ppermute | solution.py:396
  108.0 9.0 %collective-permute-start.11 = (bf16[2,4,64,128]{3,2,1,0:T(8,128)(2,1)S(1)}, bf16[2,4,64,128]{3,2,1,0:T(8,128)(2,1)S(1)}, u32[]{:S(2)}, u32[]{:S(2)}) collective-permute-start(bf16[2,4,64,128]{3,2,1,0:T(8,128)(2,1)S(1)} %get-tuple-element.81), channel_id=1, source_target_pairs={{0,12},{4,0},{8,4},{12,8},{1,13},{5,1},{9,5},{13,9},{2,14},{6,2},{... | collective-permute-start | bytes 393224 | tf_op jit(solution)/shard_map/ppermute | solution.py:396
  117.6 2.7 %collective-permute-start.21 = (bf16[2,4,2,4,64,128]{5,4,3,2,1,0:T(8,128)(2,1)S(1)}, bf16[2,4,2,4,64,128]{5,4,3,2,1,0:T(8,128)(2,1)S(1)}, u32[]{:S(2)}, u32[]{:S(2)}) collective-permute-start(bf16[2,4,2,4,64,128]{5,4,3,2,1,0:T(8,128)(2,1)S(1)} %get-tuple-element.94.low_ref), channel_id=1, source_target_pairs={{0,1},{1,0},{2,3},{3,2},{4,5},{5,4},{6,7},{7,6},{8,9},{9,8},{10,11... | collective-permute-start | bytes 3145736 | tf_op jit(solution)/shard_map/ppermute | solution.py:403
  117.7 14.3 %collective-permute-start.20 = (bf16[4,2,4,64,128]{4,3,2,1,0:T(8,128)(2,1)S(1)}, bf16[4,2,4,64,128]{4,3,2,1,0:T(8,128)(2,1)S(1)}, u32[]{:S(2)}, u32[]{:S(2)}) collective-permute-start(bf16[4,2,4,64,128]{4,3,2,1,0:T(8,128)(2,1)S(1)} %get-tuple-element.93.own_ref), channel_id=1, source_target_pairs={{0,2},{1,3},{2,0},{3,1},{4,6},{5,7},{6,4},{7,5},{8,10},{9,11},{10,... | collective-permute-start | bytes 1572872 | tf_op jit(solution)/shard_map/ppermute | solution.py:403
  132.1 2.7 %collective-permute-start.22 = (bf16[2,4,2,4,64,128]{5,4,3,2,1,0:T(8,128)(2,1)S(1)}, bf16[2,4,2,4,64,128]{5,4,3,2,1,0:T(8,128)(2,1)S(1)}, u32[]{:S(2)}, u32[]{:S(2)}) collective-permute-start(bf16[2,4,2,4,64,128]{5,4,3,2,1,0:T(8,128)(2,1)S(1)} %pair_blocks.1.low_ref), channel_id=1, source_target_pairs={{0,1},{1,0},{2,3},{3,2},{4,5},{5,4},{6,7},{7,6},{8,9},{9,8},{10,11... | collective-permute-start | bytes 3145736 | tf_op jit(solution)/shard_map/ppermute | solution.py:403

commit v4 on v3

--- a/solution.py
+++ b/solution.py
@@ -134,7 +134,7 @@
     spectra, _, rows, samples = held.shape
     taps, radix, inner = c_ref.shape
     for shift in range(len(v_refs)):
-        held[place_ref[len(v_refs) + shift]] = v_refs[shift][...]
+        held[place_ref[shift]] = v_refs[shift][...]
 
     @pl.loop(0, radix)
     def _(phase):
@@ -253,7 +253,7 @@
     def kernel(place_ref, *rest):
         ins, outs = rest[: count + len(before)], rest[count + len(before) + 1 :]
         for shift in range(count):
-            outs[0][place_ref[count + shift]] = ins[shift][...]
+            outs[0][place_ref[shift]] = ins[shift][...]
         for at in range(len(before)):
             outs[1][at] = ins[count + at][...]
 
@@ -385,16 +385,14 @@
 
 
 def places(count):
-    steps = np.arange(count, dtype=np.int32)
-    index = lax.axis_index("ft").astype(jnp.int32)
-    return jnp.concatenate([(index + steps) % count, (index + count - steps) % count])
+    return lax.axis_index("ft").astype(jnp.int32) ^ np.arange(count, dtype=np.int32)
 
 
 def spread(pieces):
     count = len(pieces)
     return [pieces[0]] + [
-        lax.ppermute(pieces[d], "ft", [(i, (i + d) % count) for i in range(count)])
-        for d in range(1, count)
+        lax.ppermute(pieces[r], "ft", [(i, i ^ r) for i in range(count)])
+        for r in range(1, count)
     ]
 
 
@@ -461,6 +459,7 @@
         and chan_count % MXU == 0
         and radix & (radix - 1) == 0
         and radix % dests == 0
+        and dests & (dests - 1) == 0
         and radix <= 8
         and blocks & (blocks - 1) == 0
         and blocks > 2

time: 141 us -> 146 us (1.035)
  waiting for transfers between devices: 54.4 us -> 65.3 us
  starting transfers between devices: 42.3 us -> 36.6 us
    ppermute x15, waiting for transfers between devices: 41.4 us -> 52.4 us  [spread(): lax.ppermute(pieces[r], 'ft', [(i, i ^ r) for i in range(count)])]
    ppermute x15, starting transfers between devices: 37.9 us -> 32 us  [spread(): lax.ppermute(pieces[r], 'ft', [(i, i ^ r) for i in range(count)])]
  transfers between devices with their start and end apart: 23 -> 23, of which waited for: 11 -> 10; matrix products, arithmetic and copies ran while one was open for 6% -> 6% of each run, Pallas kernels for 10% -> 10%
where the time goes in v4:
time: 146 us; the launch traced here: 144 us
  waiting for transfers between devices  65.3 us (45%)
  starting transfers between devices  36.6 us (25%)
  Pallas kernels  28.3 us (19%)
  local copies, waits for them, and re-layouts  9.17 us (6%)
  other arithmetic  4.53 us (3%)
    ppermute x15, waiting for transfers between devices, spread(): lax.ppermute(pieces[r], 'ft', [(i, i ^ r) for i in range(count)])  52.4 us
    ppermute x15, starting transfers between devices, spread(): lax.ppermute(pieces[r], 'ft', [(i, i ^ r) for i in range(count)])  32 us
    pallas_call x4, Pallas kernels, correlate(): pl.pallas_call(functools.partial(correlate_kernel, chunks, 1.0 / (AVG * s...  14.7 us
    ppermute x8, waiting for transfers between devices, exchange(): return lax.ppermute(own, 'bl', [(i, i ^ bit) for i in range(count)])  12.9 us
    pallas_call x2, Pallas kernels, transform_cut(): pl.pallas_call(kernel, grid_spec=pltpu.PrefetchScalarGridSpec(num_scalar_...  8.24 us
    unnamed x10, local copies, waits for them, and re-layouts  5.25 us
    ppermute x8, starting transfers between devices, exchange(): return lax.ppermute(own, 'bl', [(i, i ^ bit) for i in range(count)])  4.61 us
    reshape x2, local copies, waits for them, and re-layouts, per_device_kernels(): coef_table = coefs.reshape(taps, MXU, radix).transpose(0, 2, 1)  3.92 us
  transfers between devices with their start and end apart: 23, of which 10 were waited for; matrix products, arithmetic and copies ran while one was open for 6% of the time, Pallas kernels for 10%

profile of v4, /device:TPU:0, one launch (start us, length us, event | category | flops | bytes accessed | tf_op | source)
XLA Modules:
  0.0 144.3 jit_solution(7163603653130113503)
XLA Ops:
  0.0 1.6 %copy-done = bf16[2,2048,256]{2,1,0:T(8,128)(2,1)S(1)} copy-done((bf16[2,2048,256]{2,1,0:T(8,128)(2,1)S(1)}, bf16[2,2048,256]{2,1,0:T(8,128)(2,1)}, u32[]{:S(2)}) %copy-start) | copy-done | bytes 2097176
  1.6 2.7 %pack_inputs.1 = (bf16[2,64,2048]{2,1,0:T(8,128)(2,1)S(1)}, bf16[2,64,2048]{2,1,0:T(8,128)(2,1)}, bf16[2,64,2048]{2,1,0:T(8,128)(2,1)S(1)}, bf16[2,64,2048]{2,1,0:T(8,128)(2,1)S(1)}) custom-call(s32[4]{0:T(128)S(1)} %iota_xor_fusion.place_ref, bf16[2,2048,256]{2,1,0:T(8,128)(2,1)S(1)} %copy-done), custom_call_target="tpu_custom_call" | custom-call | tf_op jit(solution)/shard_map/pack_inputs/pallas_call | solution.py:97
  4.3 3.0 %collective-permute-start = (bf16[2,64,2048]{2,1,0:T(8,128)(2,1)}, bf16[2,64,2048]{2,1,0:T(8,128)(2,1)S(1)}, u32[]{:S(2)}, u32[]{:S(2)}) collective-permute-start(bf16[2,64,2048]{2,1,0:T(8,128)(2,1)} %get-tuple-element.53), channel_id=1, source_target_pairs={{0,4},{4,0},{8,12},{12,8},{1,5},{5,1},{9,13},{13,9},{2,6},{6,2},{1... | collective-permute-start | bytes 1572872 | tf_op jit(solution)/shard_map/ppermute | solution.py:394
  7.3 2.6 %collective-permute-start.1 = (bf16[2,64,2048]{2,1,0:T(8,128)(2,1)S(1)}, bf16[2,64,2048]{2,1,0:T(8,128)(2,1)S(1)}, u32[]{:S(2)}, u32[]{:S(2)}) collective-permute-start(bf16[2,64,2048]{2,1,0:T(8,128)(2,1)S(1)} %get-tuple-element.54), channel_id=1, source_target_pairs={{0,8},{4,12},{8,0},{12,4},{1,9},{5,13},{9,1},{13,5},{2,10},{6,14},... | collective-permute-start | bytes 1572872 | tf_op jit(solution)/shard_map/ppermute | solution.py:394
  9.9 0.0 collective-permute-start.2
  9.9 0.8 fusion.1
  10.7 2.4 %reshape.11 = f32[8,256,8]{2,1,0:T(8,128)} reshape(f32[8,2048]{1,0:T(8,128)} %param.16) | data formatting | bytes 131072 | tf_op jit(solution)/shard_map/reshape | solution.py:478
  13.1 1.5 %copy.20 = f32[8,256,8]{1,2,0:T(8,128)S(1)} copy(f32[8,256,8]{2,1,0:T(8,128)} %reshape.11) | data formatting | bytes 131072 | tf_op jit(solution)/shard_map/reshape | solution.py:478
  14.6 0.7 broadcast_compare_fusion
  15.3 0.6 reduce_sum.69
  15.9 0.8 select_reduce_fusion.3
  16.7 1.1 copy-done.1
  17.8 1.1 copy-done.2
  18.9 0.7 copy-done.3
  19.6 0.7 copy-done.4
  20.3 0.1 stage_tables.1
  20.4 0.8 multiply_reduce_fusion
  21.2 0.2 select_reduce_fusion.1
  21.4 0.7 pad_add_fusion.rest_7_.rest_3_.rest_6_.table_ref
  22.1 7.9 %collective-permute-done.rest_1_ = bf16[2,64,2048]{2,1,0:T(8,128)(2,1)S(1)} collective-permute-done((bf16[2,64,2048]{2,1,0:T(8,128)(2,1)}, bf16[2,64,2048]{2,1,0:T(8,128)(2,1)S(1)}, u32[]{:S(2)}, u32[]{:S(2)}) %collective-permute-start) | collective-permute-done | bytes 524320 | tf_op jit(solution)/shard_map/ppermute | solution.py:394
  30.0 15.5 %collective-permute-done.1.rest_2_ = bf16[2,64,2048]{2,1,0:T(8,128)(2,1)S(1)} collective-permute-done((bf16[2,64,2048]{2,1,0:T(8,128)(2,1)S(1)}, bf16[2,64,2048]{2,1,0:T(8,128)(2,1)S(1)}, u32[]{:S(2)}, u32[]{:S(2)}) %collective-permute-start.1) | collective-permute-done | bytes 524320 | tf_op jit(solution)/shard_map/ppermute | solution.py:394
  45.5 0.0 collective-permute-done.2.rest_3_
  45.5 4.8 %filter_transform.1 = (bf16[2,4,64,128]{3,2,1,0:T(8,128)(2,1)S(1)}, bf16[2,4,64,128]{3,2,1,0:T(8,128)(2,1)S(1)}, bf16[2,4,64,128]{3,2,1,0:T(8,128)(2,1)S(1)}, bf...) custom-call(s32[4]{0:T(128)S(1)} %iota_xor_fusion.place_ref, ...), custom_call_target="tpu_custom_call" | custom-call | flops 1610612736 | bytes 6291456 | tf_op jit(solution)/shard_map/filter_transform/pallas_call | solution.py:226
  50.3 10.4 %collective-permute-start.12 = (bf16[2,4,64,128]{3,2,1,0:T(8,128)(2,1)S(1)}, bf16[2,4,64,128]{3,2,1,0:T(8,128)(2,1)S(1)}, u32[]{:S(2)}, u32[]{:S(2)}) collective-permute-start(bf16[2,4,64,128]{3,2,1,0:T(8,128)(2,1)S(1)} %get-tuple-element.83), channel_id=1, source_target_pairs={{0,4},{4,0},{8,12},{12,8},{1,5},{5,1},{9,13},{13,9},{2,6},{6,2},{1... | collective-permute-start | bytes 393224 | tf_op jit(solution)/shard_map/ppermute | solution.py:394
  60.8 1.1 collective-permute-start.13
  61.9 1.4 collective-permute-start.14
  63.3 3.4 %transform_rest.1 = (bf16[2,4,64,128]{3,2,1,0:T(8,128)(2,1)S(1)}, bf16[2,4,64,128]{3,2,1,0:T(8,128)(2,1)S(1)}, bf16[2,4,64,128]{3,2,1,0:T(8,128)(2,1)S(1)}, bf16...) custom-call(s32[4]{0:T(128)S(1)} %iota_xor_fusion.place_ref, ...), custom_call_target="tpu_custom_call" | custom-call | flops 1610612736 | bytes 6291456 | tf_op jit(solution)/shard_map/transform_rest/pallas_call | solution.py:226
  66.7 0.0 collective-permute-done.12.rest_1_
  66.7 5.8 %collective-permute-done.13.rest_2_ = bf16[2,4,64,128]{3,2,1,0:T(8,128)(2,1)S(1)} collective-permute-done((bf16[2,4,64,128]{3,2,1,0:T(8,128)(2,1)S(1)}, bf16[2,4,64,128]{3,2,1,0:T(8,128)(2,1)S(1)}, u32[]{:S(2)}, u32[]{:S(2)}) %collective-permute-start.13) | collective-permute-done | bytes 131104 | tf_op jit(solution)/shard_map/ppermute | solution.py:394
  72.6 0.0 collective-permute-done.14.rest_3_
  72.6 0.6 join_pieces.4.rest_4_
  73.2 1.6 %collective-permute-start.15 = (bf16[4,2,4,64,128]{4,3,2,1,0:T(8,128)(2,1)S(1)}, bf16[4,2,4,64,128]{4,3,2,1,0:T(8,128)(2,1)S(1)}, u32[]{:S(2)}, u32[]{:S(2)}) collective-permute-start(bf16[4,2,4,64,128]{4,3,2,1,0:T(8,128)(2,1)S(1)} %join_pieces.4.rest_4_), channel_id=1, source_target_pairs={{0,2},{1,3},{2,0},{3,1},{4,6},{5,7},{6,4},{7,5},{8,10},{9,11},{10,... | collective-permute-start | bytes 1572872 | tf_op jit(solution)/shard_map/ppermute | solution.py:401
  74.7 2.0 %collective-permute-start.3 = (bf16[2,4,64,128]{3,2,1,0:T(8,128)(2,1)S(1)}, bf16[2,4,64,128]{3,2,1,0:T(8,128)(2,1)S(1)}, u32[]{:S(2)}, u32[]{:S(2)}) collective-permute-start(bf16[2,4,64,128]{3,2,1,0:T(8,128)(2,1)S(1)} %get-tuple-element.71), channel_id=1, source_target_pairs={{0,4},{4,0},{8,12},{12,8},{1,5},{5,1},{9,13},{13,9},{2,6},{6,2},{1... | collective-permute-start | bytes 393224 | tf_op jit(solution)/shard_map/ppermute | solution.py:394
  76.7 1.0 collective-permute-start.4
  77.6 1.5 %collective-permute-start.5 = (bf16[2,4,64,128]{3,2,1,0:T(8,128)(2,1)S(1)}, bf16[2,4,64,128]{3,2,1,0:T(8,128)(2,1)S(1)}, u32[]{:S(2)}, u32[]{:S(2)}) collective-permute-start(bf16[2,4,64,128]{3,2,1,0:T(8,128)(2,1)S(1)} %get-tuple-element.73), channel_id=1, source_target_pairs={{0,12},{4,8},{8,4},{12,0},{1,13},{5,9},{9,5},{13,1},{2,14},{6,10},... | collective-permute-start | bytes 393224 | tf_op jit(solution)/shard_map/ppermute | solution.py:394
  79.1 1.7 %collective-permute-done.3.rest_1_ = bf16[2,4,64,128]{3,2,1,0:T(8,128)(2,1)S(1)} collective-permute-done((bf16[2,4,64,128]{3,2,1,0:T(8,128)(2,1)S(1)}, bf16[2,4,64,128]{3,2,1,0:T(8,128)(2,1)S(1)}, u32[]{:S(2)}, u32[]{:S(2)}) %collective-permute-start.3) | collective-permute-done | bytes 131104 | tf_op jit(solution)/shard_map/ppermute | solution.py:394
  80.8 7.6 %collective-permute-done.4.rest_2_ = bf16[2,4,64,128]{3,2,1,0:T(8,128)(2,1)S(1)} collective-permute-done((bf16[2,4,64,128]{3,2,1,0:T(8,128)(2,1)S(1)}, bf16[2,4,64,128]{3,2,1,0:T(8,128)(2,1)S(1)}, u32[]{:S(2)}, u32[]{:S(2)}) %collective-permute-start.4) | collective-permute-done | bytes 131104 | tf_op jit(solution)/shard_map/ppermute | solution.py:394
  88.4 0.0 collective-permute-done.5.rest_3_
  88.4 0.6 join_pieces.5
  89.1 0.1 collective-permute-start.17
  89.1 0.6 collective-permute-start.16
  89.7 2.0 %collective-permute-start.6 = (bf16[2,4,64,128]{3,2,1,0:T(8,128)(2,1)S(1)}, bf16[2,4,64,128]{3,2,1,0:T(8,128)(2,1)S(1)}, u32[]{:S(2)}, u32[]{:S(2)}) collective-permute-start(bf16[2,4,64,128]{3,2,1,0:T(8,128)(2,1)S(1)} %get-tuple-element.75), channel_id=1, source_target_pairs={{0,4},{4,0},{8,12},{12,8},{1,5},{5,1},{9,13},{13,9},{2,6},{6,2},{1... | collective-permute-start | bytes 393224 | tf_op jit(solution)/shard_map/ppermute | solution.py:394
  91.7 0.9 collective-permute-start.7
  92.6 1.5 %collective-permute-start.8 = (bf16[2,4,64,128]{3,2,1,0:T(8,128)(2,1)S(1)}, bf16[2,4,64,128]{3,2,1,0:T(8,128)(2,1)S(1)}, u32[]{:S(2)}, u32[]{:S(2)}) collective-permute-start(bf16[2,4,64,128]{3,2,1,0:T(8,128)(2,1)S(1)} %get-tuple-element.77), channel_id=1, source_target_pairs={{0,12},{4,8},{8,4},{12,0},{1,13},{5,9},{9,5},{13,1},{2,14},{6,10},... | collective-permute-start | bytes 393224 | tf_op jit(solution)/shard_map/ppermute | solution.py:394
  94.1 3.5 %correlate_tiles.4 = (f32[2,8,5,256,256]{4,3,2,1,0:T(8,128)}, f32[8,128]{1,0:T(8,128)S(1)}) custom-call(s32[11]{0:T(128)S(1)} %pad_add_fusion.rest_7_.rest_3_.rest_6_.table_ref, bf16[2,4,2,4,64,128]{5,4,3,2,1,0:T(8,128)(2,1)S(1)} %get-tuple-element.87.low_ref, bf16[2,4,2,4,64,128]{5,4,3,2,1,0:T(8,128)(2,1)S(1)} %collective-permute-done.17.high_ref), custom_call_target="tpu_custom_call" | custom-call | tf_op jit(solution)/shard_map/correlate_tiles/pallas_call | solution.py:362
  97.7 6.9 %collective-permute-done.7.rest_2_ = bf16[2,4,64,128]{3,2,1,0:T(8,128)(2,1)S(1)} collective-permute-done((bf16[2,4,64,128]{3,2,1,0:T(8,128)(2,1)S(1)}, bf16[2,4,64,128]{3,2,1,0:T(8,128)(2,1)S(1)}, u32[]{:S(2)}, u32[]{:S(2)}) %collective-permute-start.7) | collective-permute-done | bytes 131104 | tf_op jit(solution)/shard_map/ppermute | solution.py:394
  104.6 0.6 join_pieces.6
  105.3 0.1 collective-permute-start.19
  105.3 1.5 %collective-permute-start.18 = (bf16[4,2,4,64,128]{4,3,2,1,0:T(8,128)(2,1)S(1)}, bf16[4,2,4,64,128]{4,3,2,1,0:T(8,128)(2,1)S(1)}, u32[]{:S(2)}, u32[]{:S(2)}) collective-permute-start(bf16[4,2,4,64,128]{4,3,2,1,0:T(8,128)(2,1)S(1)} %get-tuple-element.89.rest_4_), channel_id=1, source_target_pairs={{0,2},{1,3},{2,0},{3,1},{4,6},{5,7},{6,4},{7,5},{8,10},{9,11},{10,... | collective-permute-start | bytes 1572872 | tf_op jit(solution)/shard_map/ppermute | solution.py:401
  106.9 2.3 %collective-permute-start.9 = (bf16[2,4,64,128]{3,2,1,0:T(8,128)(2,1)S(1)}, bf16[2,4,64,128]{3,2,1,0:T(8,128)(2,1)S(1)}, u32[]{:S(2)}, u32[]{:S(2)}) collective-permute-start(bf16[2,4,64,128]{3,2,1,0:T(8,128)(2,1)S(1)} %get-tuple-element.79), channel_id=1, source_target_pairs={{0,4},{4,0},{8,12},{12,8},{1,5},{5,1},{9,13},{13,9},{2,6},{6,2},{1... | collective-permute-start | bytes 393224 | tf_op jit(solution)/shard_map/ppermute | solution.py:394
  109.2 0.9 collective-permute-start.10
  110.1 1.5 %collective-permute-start.11 = (bf16[2,4,64,128]{3,2,1,0:T(8,128)(2,1)S(1)}, bf16[2,4,64,128]{3,2,1,0:T(8,128)(2,1)S(1)}, u32[]{:S(2)}, u32[]{:S(2)}) collective-permute-start(bf16[2,4,64,128]{3,2,1,0:T(8,128)(2,1)S(1)} %get-tuple-element.81), channel_id=1, source_target_pairs={{0,12},{4,8},{8,4},{12,0},{1,13},{5,9},{9,5},{13,1},{2,14},{6,10},... | collective-permute-start | bytes 393224 | tf_op jit(solution)/shard_map/ppermute | solution.py:394
  111.6 3.5 %correlate_tiles.5 = (f32[2,8,5,256,256]{4,3,2,1,0:T(8,128)}, f32[8,128]{1,0:T(8,128)S(1)}) custom-call(s32[11]{0:T(128)S(1)} %pad_add_fusion.rest_7_.rest_3_.rest_6_.table_ref, bf16[2,4,2,4,64,128]{5,4,3,2,1,0:T(8,128)(2,1)S(1)} %get-tuple-element.90.low_ref, ...), custom_call_target="tpu_custom_call", output_to_operand_aliasing={{0}: (3, {})} | custom-call | tf_op jit(solution)/shard_map/correlate_tiles/pallas_call | solution.py:362
  115.1 7.0 %collective-permute-done.10.rest_2_ = bf16[2,4,64,128]{3,2,1,0:T(8,128)(2,1)S(1)} collective-permute-done((bf16[2,4,64,128]{3,2,1,0:T(8,128)(2,1)S(1)}, bf16[2,4,64,128]{3,2,1,0:T(8,128)(2,1)S(1)}, u32[]{:S(2)}, u32[]{:S(2)}) %collective-permute-start.10) | collective-permute-done | bytes 131104 | tf_op jit(solution)/shard_map/ppermute | solution.py:394
  122.1 0.6 join_pieces.7
  122.8 0.1 collective-permute-start.21
  122.9 0.6 collective-permute-start.20
  123.5 2.0 %collective-permute-done.21.high_ref = bf16[2,4,2,4,64,128]{5,4,3,2,1,0:T(8,128)(2,1)S(1)} collective-permute-done((bf16[2,4,2,4,64,128]{5,4,3,2,1,0:T(8,128)(2,1)S(1)}, bf16[2,4,2,4,64,128]{5,4,3,2,1,0:T(8,128)(2,1)S(1)}, u32[]{:S(2)}, u32[]{:S(2)}) %collective-permute-start.21) | collective-permute-done | bytes 1048608 | tf_op jit(solution)/shard_map/ppermute | solution.py:401
  125.5 3.5 %correlate_tiles.6 = (f32[2,8,5,256,256]{4,3,2,1,0:T(8,128)}, f32[8,128]{1,0:T(8,128)S(1)}) custom-call(s32[11]{0:T(128)S(1)} %pad_add_fusion.rest_7_.rest_3_.rest_6_.table_ref, bf16[2,4,2,4,64,128]{5,4,3,2,1,0:T(8,128)(2,1)S(1)} %get-tuple-element.94.low_ref, ...), custom_call_target="tpu_custom_call", output_to_operand_aliasing={{0}: (3, {})} | custom-call | tf_op jit(solution)/shard_map/correlate_tiles/pallas_call | solution.py:362
  129.0 8.2 %collective-permute-done.20.other_ref = bf16[4,2,4,64,128]{4,3,2,1,0:T(8,128)(2,1)S(1)} collective-permute-done((bf16[4,2,4,64,128]{4,3,2,1,0:T(8,128)(2,1)S(1)}, bf16[4,2,4,64,128]{4,3,2,1,0:T(8,128)(2,1)S(1)}, u32[]{:S(2)}, u32[]{:S(2)}) %collective-permute-start.20) | collective-permute-done | bytes 524320 | tf_op jit(solution)/shard_map/ppermute | solution.py:401
  137.2 0.1 pair_blocks.1.low_ref
  137.3 0.1 collective-permute-start.22
  137.3 2.6 %collective-permute-done.22.high_ref = bf16[2,4,2,4,64,128]{5,4,3,2,1,0:T(8,128)(2,1)S(1)} collective-permute-done((bf16[2,4,2,4,64,128]{5,4,3,2,1,0:T(8,128)(2,1)S(1)}, bf16[2,4,2,4,64,128]{5,4,3,2,1,0:T(8,128)(2,1)S(1)}, u32[]{:S(2)}, u32[]{:S(2)}) %collective-permute-start.22) | collective-permute-done | bytes 1048608 | tf_op jit(solution)/shard_map/ppermute | solution.py:401
  140.0 4.1 %correlate_tiles.7 = (f32[2,8,5,256,256]{4,3,2,1,0:T(8,128)}, f32[8,128]{1,0:T(8,128)}) custom-call(s32[11]{0:T(128)S(1)} %pad_add_fusion.rest_7_.rest_3_.rest_6_.table_ref, bf16[2,4,2,4,64,128]{5,4,3,2,1,0:T(8,128)(2,1)S(1)} %pair_blocks.1.low_ref, ...), custom_call_target="tpu_custom_call", output_to_operand_aliasing={{0}: (3, {})} | custom-call | tf_op jit(solution)/shard_map/correlate_tiles/pallas_call | solution.py:362
  (16 shorter events, 0.0 us)
Async XLA Ops:
  0.0 1.6 %copy-start = (bf16[2,2048,256]{2,1,0:T(8,128)(2,1)S(1)}, bf16[2,2048,256]{2,1,0:T(8,128)(2,1)}, u32[]{:S(2)}) copy-start(bf16[2,2048,256]{2,1,0:T(8,128)(2,1)} %v_ref.1) | copy-start | bytes 6291460
  4.3 25.7 %collective-permute-start = (bf16[2,64,2048]{2,1,0:T(8,128)(2,1)}, bf16[2,64,2048]{2,1,0:T(8,128)(2,1)S(1)}, u32[]{:S(2)}, u32[]{:S(2)}) collective-permute-start(bf16[2,64,2048]{2,1,0:T(8,128)(2,1)} %get-tuple-element.53), channel_id=1, source_target_pairs={{0,4},{4,0},{8,12},{12,8},{1,5},{5,1},{9,13},{13,9},{2,6},{6,2},{1... | collective-permute-start | bytes 1572872 | tf_op jit(solution)/shard_map/ppermute | solution.py:394
  7.3 38.2 %collective-permute-start.1 = (bf16[2,64,2048]{2,1,0:T(8,128)(2,1)S(1)}, bf16[2,64,2048]{2,1,0:T(8,128)(2,1)S(1)}, u32[]{:S(2)}, u32[]{:S(2)}) collective-permute-start(bf16[2,64,2048]{2,1,0:T(8,128)(2,1)S(1)} %get-tuple-element.54), channel_id=1, source_target_pairs={{0,8},{4,12},{8,0},{12,4},{1,9},{5,13},{9,1},{13,5},{2,10},{6,14},... | collective-permute-start | bytes 1572872 | tf_op jit(solution)/shard_map/ppermute | solution.py:394
  9.9 35.6 %collective-permute-start.2 = (bf16[2,64,2048]{2,1,0:T(8,128)(2,1)S(1)}, bf16[2,64,2048]{2,1,0:T(8,128)(2,1)S(1)}, u32[]{:S(2)}, u32[]{:S(2)}) collective-permute-start(bf16[2,64,2048]{2,1,0:T(8,128)(2,1)S(1)} %get-tuple-element.55), channel_id=1, source_target_pairs={{0,12},{4,8},{8,4},{12,0},{1,13},{5,9},{9,5},{13,1},{2,14},{6,10},... | collective-permute-start | bytes 1572872 | tf_op jit(solution)/shard_map/ppermute | solution.py:394
  16.7 1.1 copy-start.1
  17.8 1.1 copy-start.2
  18.9 0.7 copy-start.3
  19.6 0.7 copy-start.4
  50.3 16.4 %collective-permute-start.12 = (bf16[2,4,64,128]{3,2,1,0:T(8,128)(2,1)S(1)}, bf16[2,4,64,128]{3,2,1,0:T(8,128)(2,1)S(1)}, u32[]{:S(2)}, u32[]{:S(2)}) collective-permute-start(bf16[2,4,64,128]{3,2,1,0:T(8,128)(2,1)S(1)} %get-tuple-element.83), channel_id=1, source_target_pairs={{0,4},{4,0},{8,12},{12,8},{1,5},{5,1},{9,13},{13,9},{2,6},{6,2},{1... | collective-permute-start | bytes 393224 | tf_op jit(solution)/shard_map/ppermute | solution.py:394
  60.8 11.8 %collective-permute-start.13 = (bf16[2,4,64,128]{3,2,1,0:T(8,128)(2,1)S(1)}, bf16[2,4,64,128]{3,2,1,0:T(8,128)(2,1)S(1)}, u32[]{:S(2)}, u32[]{:S(2)}) collective-permute-start(bf16[2,4,64,128]{3,2,1,0:T(8,128)(2,1)S(1)} %get-tuple-element.84), channel_id=1, source_target_pairs={{0,8},{4,12},{8,0},{12,4},{1,9},{5,13},{9,1},{13,5},{2,10},{6,14},... | collective-permute-start | bytes 393224 | tf_op jit(solution)/shard_map/ppermute | solution.py:394
  61.9 10.7 %collective-permute-start.14 = (bf16[2,4,64,128]{3,2,1,0:T(8,128)(2,1)S(1)}, bf16[2,4,64,128]{3,2,1,0:T(8,128)(2,1)S(1)}, u32[]{:S(2)}, u32[]{:S(2)}) collective-permute-start(bf16[2,4,64,128]{3,2,1,0:T(8,128)(2,1)S(1)} %get-tuple-element.85), channel_id=1, source_target_pairs={{0,12},{4,8},{8,4},{12,0},{1,13},{5,9},{9,5},{13,1},{2,14},{6,10},... | collective-permute-start | bytes 393224 | tf_op jit(solution)/shard_map/ppermute | solution.py:394
  73.2 15.2 %collective-permute-start.15 = (bf16[4,2,4,64,128]{4,3,2,1,0:T(8,128)(2,1)S(1)}, bf16[4,2,4,64,128]{4,3,2,1,0:T(8,128)(2,1)S(1)}, u32[]{:S(2)}, u32[]{:S(2)}) collective-permute-start(bf16[4,2,4,64,128]{4,3,2,1,0:T(8,128)(2,1)S(1)} %join_pieces.4.rest_4_), channel_id=1, source_target_pairs={{0,2},{1,3},{2,0},{3,1},{4,6},{5,7},{6,4},{7,5},{8,10},{9,11},{10,... | collective-permute-start | bytes 1572872 | tf_op jit(solution)/shard_map/ppermute | solution.py:401
  74.7 6.1 %collective-permute-start.3 = (bf16[2,4,64,128]{3,2,1,0:T(8,128)(2,1)S(1)}, bf16[2,4,64,128]{3,2,1,0:T(8,128)(2,1)S(1)}, u32[]{:S(2)}, u32[]{:S(2)}) collective-permute-start(bf16[2,4,64,128]{3,2,1,0:T(8,128)(2,1)S(1)} %get-tuple-element.71), channel_id=1, source_target_pairs={{0,4},{4,0},{8,12},{12,8},{1,5},{5,1},{9,13},{13,9},{2,6},{6,2},{1... | collective-permute-start | bytes 393224 | tf_op jit(solution)/shard_map/ppermute | solution.py:394
  76.7 11.7 %collective-permute-start.4 = (bf16[2,4,64,128]{3,2,1,0:T(8,128)(2,1)S(1)}, bf16[2,4,64,128]{3,2,1,0:T(8,128)(2,1)S(1)}, u32[]{:S(2)}, u32[]{:S(2)}) collective-permute-start(bf16[2,4,64,128]{3,2,1,0:T(8,128)(2,1)S(1)} %get-tuple-element.72), channel_id=1, source_target_pairs={{0,8},{4,12},{8,0},{12,4},{1,9},{5,13},{9,1},{13,5},{2,10},{6,14},... | collective-permute-start | bytes 393224 | tf_op jit(solution)/shard_map/ppermute | solution.py:394
  77.6 10.8 %collective-permute-start.5 = (bf16[2,4,64,128]{3,2,1,0:T(8,128)(2,1)S(1)}, bf16[2,4,64,128]{3,2,1,0:T(8,128)(2,1)S(1)}, u32[]{:S(2)}, u32[]{:S(2)}) collective-permute-start(bf16[2,4,64,128]{3,2,1,0:T(8,128)(2,1)S(1)} %get-tuple-element.73), channel_id=1, source_target_pairs={{0,12},{4,8},{8,4},{12,0},{1,13},{5,9},{9,5},{13,1},{2,14},{6,10},... | collective-permute-start | bytes 393224 | tf_op jit(solution)/shard_map/ppermute | solution.py:394
  89.1 5.1 %collective-permute-start.17 = (bf16[2,4,2,4,64,128]{5,4,3,2,1,0:T(8,128)(2,1)S(1)}, bf16[2,4,2,4,64,128]{5,4,3,2,1,0:T(8,128)(2,1)S(1)}, u32[]{:S(2)}, u32[]{:S(2)}) collective-permute-start(bf16[2,4,2,4,64,128]{5,4,3,2,1,0:T(8,128)(2,1)S(1)} %get-tuple-element.87.low_ref), channel_id=1, source_target_pairs={{0,1},{1,0},{2,3},{3,2},{4,5},{5,4},{6,7},{7,6},{8,9},{9,8},{10,11... | collective-permute-start | bytes 3145736 | tf_op jit(solution)/shard_map/ppermute | solution.py:401
  89.1 15.5 %collective-permute-start.16 = (bf16[4,2,4,64,128]{4,3,2,1,0:T(8,128)(2,1)S(1)}, bf16[4,2,4,64,128]{4,3,2,1,0:T(8,128)(2,1)S(1)}, u32[]{:S(2)}, u32[]{:S(2)}) collective-permute-start(bf16[4,2,4,64,128]{4,3,2,1,0:T(8,128)(2,1)S(1)} %get-tuple-element.86.rest_4_), channel_id=1, source_target_pairs={{0,2},{1,3},{2,0},{3,1},{4,6},{5,7},{6,4},{7,5},{8,10},{9,11},{10,... | collective-permute-start | bytes 1572872 | tf_op jit(solution)/shard_map/ppermute | solution.py:401
  89.7 7.9 %collective-permute-start.6 = (bf16[2,4,64,128]{3,2,1,0:T(8,128)(2,1)S(1)}, bf16[2,4,64,128]{3,2,1,0:T(8,128)(2,1)S(1)}, u32[]{:S(2)}, u32[]{:S(2)}) collective-permute-start(bf16[2,4,64,128]{3,2,1,0:T(8,128)(2,1)S(1)} %get-tuple-element.75), channel_id=1, source_target_pairs={{0,4},{4,0},{8,12},{12,8},{1,5},{5,1},{9,13},{13,9},{2,6},{6,2},{1... | collective-permute-start | bytes 393224 | tf_op jit(solution)/shard_map/ppermute | solution.py:394
  91.7 12.9 %collective-permute-start.7 = (bf16[2,4,64,128]{3,2,1,0:T(8,128)(2,1)S(1)}, bf16[2,4,64,128]{3,2,1,0:T(8,128)(2,1)S(1)}, u32[]{:S(2)}, u32[]{:S(2)}) collective-permute-start(bf16[2,4,64,128]{3,2,1,0:T(8,128)(2,1)S(1)} %get-tuple-element.76), channel_id=1, source_target_pairs={{0,8},{4,12},{8,0},{12,4},{1,9},{5,13},{9,1},{13,5},{2,10},{6,14},... | collective-permute-start | bytes 393224 | tf_op jit(solution)/shard_map/ppermute | solution.py:394
  92.6 12.0 %collective-permute-start.8 = (bf16[2,4,64,128]{3,2,1,0:T(8,128)(2,1)S(1)}, bf16[2,4,64,128]{3,2,1,0:T(8,128)(2,1)S(1)}, u32[]{:S(2)}, u32[]{:S(2)}) collective-permute-start(bf16[2,4,64,128]{3,2,1,0:T(8,128)(2,1)S(1)} %get-tuple-element.77), channel_id=1, source_target_pairs={{0,12},{4,8},{8,4},{12,0},{1,13},{5,9},{9,5},{13,1},{2,14},{6,10},... | collective-permute-start | bytes 393224 | tf_op jit(solution)/shard_map/ppermute | solution.py:394
  105.3 6.3 %collective-permute-start.19 = (bf16[2,4,2,4,64,128]{5,4,3,2,1,0:T(8,128)(2,1)S(1)}, bf16[2,4,2,4,64,128]{5,4,3,2,1,0:T(8,128)(2,1)S(1)}, u32[]{:S(2)}, u32[]{:S(2)}) collective-permute-start(bf16[2,4,2,4,64,128]{5,4,3,2,1,0:T(8,128)(2,1)S(1)} %get-tuple-element.90.low_ref), channel_id=1, source_target_pairs={{0,1},{1,0},{2,3},{3,2},{4,5},{5,4},{6,7},{7,6},{8,9},{9,8},{10,11... | collective-permute-start | bytes 3145736 | tf_op jit(solution)/shard_map/ppermute | solution.py:401
  105.3 16.8 %collective-permute-start.18 = (bf16[4,2,4,64,128]{4,3,2,1,0:T(8,128)(2,1)S(1)}, bf16[4,2,4,64,128]{4,3,2,1,0:T(8,128)(2,1)S(1)}, u32[]{:S(2)}, u32[]{:S(2)}) collective-permute-start(bf16[4,2,4,64,128]{4,3,2,1,0:T(8,128)(2,1)S(1)} %get-tuple-element.89.rest_4_), channel_id=1, source_target_pairs={{0,2},{1,3},{2,0},{3,1},{4,6},{5,7},{6,4},{7,5},{8,10},{9,11},{10,... | collective-permute-start | bytes 1572872 | tf_op jit(solution)/shard_map/ppermute | solution.py:401
  106.9 8.2 %collective-permute-start.9 = (bf16[2,4,64,128]{3,2,1,0:T(8,128)(2,1)S(1)}, bf16[2,4,64,128]{3,2,1,0:T(8,128)(2,1)S(1)}, u32[]{:S(2)}, u32[]{:S(2)}) collective-permute-start(bf16[2,4,64,128]{3,2,1,0:T(8,128)(2,1)S(1)} %get-tuple-element.79), channel_id=1, source_target_pairs={{0,4},{4,0},{8,12},{12,8},{1,5},{5,1},{9,13},{13,9},{2,6},{6,2},{1... | collective-permute-start | bytes 393224 | tf_op jit(solution)/shard_map/ppermute | solution.py:394
  109.2 12.9 %collective-permute-start.10 = (bf16[2,4,64,128]{3,2,1,0:T(8,128)(2,1)S(1)}, bf16[2,4,64,128]{3,2,1,0:T(8,128)(2,1)S(1)}, u32[]{:S(2)}, u32[]{:S(2)}) collective-permute-start(bf16[2,4,64,128]{3,2,1,0:T(8,128)(2,1)S(1)} %get-tuple-element.80), channel_id=1, source_target_pairs={{0,8},{4,12},{8,0},{12,4},{1,9},{5,13},{9,1},{13,5},{2,10},{6,14},... | collective-permute-start | bytes 393224 | tf_op jit(solution)/shard_map/ppermute | solution.py:394
  110.1 12.0 %collective-permute-start.11 = (bf16[2,4,64,128]{3,2,1,0:T(8,128)(2,1)S(1)}, bf16[2,4,64,128]{3,2,1,0:T(8,128)(2,1)S(1)}, u32[]{:S(2)}, u32[]{:S(2)}) collective-permute-start(bf16[2,4,64,128]{3,2,1,0:T(8,128)(2,1)S(1)} %get-tuple-element.81), channel_id=1, source_target_pairs={{0,12},{4,8},{8,4},{12,0},{1,13},{5,9},{9,5},{13,1},{2,14},{6,10},... | collective-permute-start | bytes 393224 | tf_op jit(solution)/shard_map/ppermute | solution.py:394
  122.8 2.7 %collective-permute-start.21 = (bf16[2,4,2,4,64,128]{5,4,3,2,1,0:T(8,128)(2,1)S(1)}, bf16[2,4,2,4,64,128]{5,4,3,2,1,0:T(8,128)(2,1)S(1)}, u32[]{:S(2)}, u32[]{:S(2)}) collective-permute-start(bf16[2,4,2,4,64,128]{5,4,3,2,1,0:T(8,128)(2,1)S(1)} %get-tuple-element.94.low_ref), channel_id=1, source_target_pairs={{0,1},{1,0},{2,3},{3,2},{4,5},{5,4},{6,7},{7,6},{8,9},{9,8},{10,11... | collective-permute-start | bytes 3145736 | tf_op jit(solution)/shard_map/ppermute | solution.py:401
  122.9 14.3 %collective-permute-start.20 = (bf16[4,2,4,64,128]{4,3,2,1,0:T(8,128)(2,1)S(1)}, bf16[4,2,4,64,128]{4,3,2,1,0:T(8,128)(2,1)S(1)}, u32[]{:S(2)}, u32[]{:S(2)}) collective-permute-start(bf16[4,2,4,64,128]{4,3,2,1,0:T(8,128)(2,1)S(1)} %get-tuple-element.93.own_ref), channel_id=1, source_target_pairs={{0,2},{1,3},{2,0},{3,1},{4,6},{5,7},{6,4},{7,5},{8,10},{9,11},{10,... | collective-permute-start | bytes 1572872 | tf_op jit(solution)/shard_map/ppermute | solution.py:401
  137.3 2.7 %collective-permute-start.22 = (bf16[2,4,2,4,64,128]{5,4,3,2,1,0:T(8,128)(2,1)S(1)}, bf16[2,4,2,4,64,128]{5,4,3,2,1,0:T(8,128)(2,1)S(1)}, u32[]{:S(2)}, u32[]{:S(2)}) collective-permute-start(bf16[2,4,2,4,64,128]{5,4,3,2,1,0:T(8,128)(2,1)S(1)} %pair_blocks.1.low_ref), channel_id=1, source_target_pairs={{0,1},{1,0},{2,3},{3,2},{4,5},{5,4},{6,7},{7,6},{8,9},{9,8},{10,11... | collective-permute-start | bytes 3145736 | tf_op jit(solution)/shard_map/ppermute | solution.py:401

commit v5 on v3

--- a/solution.py
+++ b/solution.py
@@ -392,10 +392,10 @@
 
 def spread(pieces):
     count = len(pieces)
-    return [pieces[0]] + [
-        lax.ppermute(pieces[d], "ft", [(i, (i + d) % count) for i in range(count)])
-        for d in range(1, count)
-    ]
+    arrived = [pieces[0]] + [None] * (count - 1)
+    for d in sorted(range(1, count), key=lambda d: abs(d - count // 2)):
+        arrived[d] = lax.ppermute(pieces[d], "ft", [(i, (i + d) % count) for i in range(count)])
+    return arrived
 
 
 def exchange(own, bit):

time: 141 us -> 141 us (level)
  no operation moved by 1% of the time
where the time goes in v5:
time: 141 us; the launch traced here: 139 us
  waiting for transfers between devices  54.4 us (39%)
  starting transfers between devices  42.3 us (30%)
  Pallas kernels  28.3 us (20%)
  local copies, waits for them, and re-layouts  9.17 us (7%)
  other arithmetic  4.61 us (3%)
    ppermute x15, waiting for transfers between devices, spread(): lax.ppermute(pieces[d], 'ft', [(i, (i + d) % count) for i in range(count)])  41.4 us
    ppermute x15, starting transfers between devices, spread(): lax.ppermute(pieces[d], 'ft', [(i, (i + d) % count) for i in range(count)])  37.9 us
    pallas_call x4, Pallas kernels, correlate(): pl.pallas_call(functools.partial(correlate_kernel, chunks, 1.0 / (AVG * s...  14.7 us
    ppermute x8, waiting for transfers between devices, exchange(): return lax.ppermute(own, 'bl', [(i, i ^ bit) for i in range(count)])  13 us
    pallas_call x2, Pallas kernels, transform_cut(): pl.pallas_call(kernel, grid_spec=pltpu.PrefetchScalarGridSpec(num_scalar_...  8.24 us
    unnamed x10, local copies, waits for them, and re-layouts  5.25 us
    ppermute x8, starting transfers between devices, exchange(): return lax.ppermute(own, 'bl', [(i, i ^ bit) for i in range(count)])  4.38 us
    reshape x2, local copies, waits for them, and re-layouts, per_device_kernels(): coef_table = coefs.reshape(taps, MXU, radix).transpose(0, 2, 1)  3.92 us
  transfers between devices with their start and end apart: 23, of which 11 were waited for; matrix products, arithmetic and copies ran while one was open for 6% of the time, Pallas kernels for 10%

profile of v5, /device:TPU:0, one launch (start us, length us, event | category | flops | bytes accessed | tf_op | source)
XLA Modules:
  0.0 139.1 jit_solution(15175096462809665226)
XLA Ops:
  0.0 0.1 pad_add_fusion.1.place_ref
  0.1 1.6 %copy-done = bf16[2,2048,256]{2,1,0:T(8,128)(2,1)S(1)} copy-done((bf16[2,2048,256]{2,1,0:T(8,128)(2,1)S(1)}, bf16[2,2048,256]{2,1,0:T(8,128)(2,1)}, u32[]{:S(2)}) %copy-start) | copy-done | bytes 2097176
  1.7 2.7 %pack_inputs.1 = (bf16[2,64,2048]{2,1,0:T(8,128)(2,1)S(1)}, bf16[2,64,2048]{2,1,0:T(8,128)(2,1)}, bf16[2,64,2048]{2,1,0:T(8,128)(2,1)S(1)}, bf16[2,64,2048]{2,1,0:T(8,128)(2,1)S(1)}) custom-call(s32[8]{0:T(128)S(1)} %pad_add_fusion.1.place_ref, bf16[2,2048,256]{2,1,0:T(8,128)(2,1)S(1)} %copy-done), custom_call_target="tpu_custom_call" | custom-call | tf_op jit(solution)/shard_map/pack_inputs/pallas_call | solution.py:97
  4.4 3.0 %collective-permute-start = (bf16[2,64,2048]{2,1,0:T(8,128)(2,1)}, bf16[2,64,2048]{2,1,0:T(8,128)(2,1)S(1)}, u32[]{:S(2)}, u32[]{:S(2)}) collective-permute-start(bf16[2,64,2048]{2,1,0:T(8,128)(2,1)} %get-tuple-element.53), channel_id=1, source_target_pairs={{0,4},{4,8},{8,12},{12,0},{1,5},{5,9},{9,13},{13,1},{2,6},{6,10},{... | collective-permute-start | bytes 1572872 | tf_op jit(solution)/shard_map/ppermute | solution.py:397
  7.4 2.6 %collective-permute-start.1 = (bf16[2,64,2048]{2,1,0:T(8,128)(2,1)S(1)}, bf16[2,64,2048]{2,1,0:T(8,128)(2,1)S(1)}, u32[]{:S(2)}, u32[]{:S(2)}) collective-permute-start(bf16[2,64,2048]{2,1,0:T(8,128)(2,1)S(1)} %get-tuple-element.54), channel_id=1, source_target_pairs={{0,8},{4,12},{8,0},{12,4},{1,9},{5,13},{9,1},{13,5},{2,10},{6,14},... | collective-permute-start | bytes 1572872 | tf_op jit(solution)/shard_map/ppermute | solution.py:397
  10.0 1.3 collective-permute-start.2
  11.3 0.8 fusion.1
  12.1 2.4 %reshape.11 = f32[8,256,8]{2,1,0:T(8,128)} reshape(f32[8,2048]{1,0:T(8,128)} %param.16) | data formatting | bytes 131072 | tf_op jit(solution)/shard_map/reshape | solution.py:479
  14.5 1.5 %copy.20 = f32[8,256,8]{1,2,0:T(8,128)S(1)} copy(f32[8,256,8]{2,1,0:T(8,128)} %reshape.11) | data formatting | bytes 131072 | tf_op jit(solution)/shard_map/reshape | solution.py:479
  16.0 0.7 broadcast_compare_fusion
  16.7 0.6 reduce_sum.69
  17.3 0.8 select_reduce_fusion.3
  18.1 1.1 copy-done.1
  19.2 1.1 copy-done.2
  20.4 0.7 copy-done.3
  21.0 0.7 copy-done.4
  21.7 0.1 stage_tables.1
  21.9 0.8 multiply_reduce_fusion
  22.7 0.2 select_reduce_fusion.1
  22.8 0.7 pad_add_fusion.rest_7_.rest_3_.rest_6_.table_ref
  23.6 0.0 collective-permute-done.rest_1_
  23.6 20.6 %collective-permute-done.1.rest_2_ = bf16[2,64,2048]{2,1,0:T(8,128)(2,1)S(1)} collective-permute-done((bf16[2,64,2048]{2,1,0:T(8,128)(2,1)S(1)}, bf16[2,64,2048]{2,1,0:T(8,128)(2,1)S(1)}, u32[]{:S(2)}, u32[]{:S(2)}) %collective-permute-start.1) | collective-permute-done | bytes 524320 | tf_op jit(solution)/shard_map/ppermute | solution.py:397
  44.2 4.8 %filter_transform.1 = (bf16[2,4,64,128]{3,2,1,0:T(8,128)(2,1)S(1)}, bf16[2,4,64,128]{3,2,1,0:T(8,128)(2,1)S(1)}, bf16[2,4,64,128]{3,2,1,0:T(8,128)(2,1)S(1)}, bf...) custom-call(s32[8]{0:T(128)S(1)} %pad_add_fusion.1.place_ref, ...), custom_call_target="tpu_custom_call" | custom-call | flops 1610612736 | bytes 6291456 | tf_op jit(solution)/shard_map/filter_transform/pallas_call | solution.py:226
  49.0 11.8 %collective-permute-start.12 = (bf16[2,4,64,128]{3,2,1,0:T(8,128)(2,1)S(1)}, bf16[2,4,64,128]{3,2,1,0:T(8,128)(2,1)S(1)}, u32[]{:S(2)}, u32[]{:S(2)}) collective-permute-start(bf16[2,4,64,128]{3,2,1,0:T(8,128)(2,1)S(1)} %get-tuple-element.83), channel_id=1, source_target_pairs={{0,4},{4,8},{8,12},{12,0},{1,5},{5,9},{9,13},{13,1},{2,6},{6,10},{... | collective-permute-start | bytes 393224 | tf_op jit(solution)/shard_map/ppermute | solution.py:397
  60.7 1.6 %collective-permute-start.13 = (bf16[2,4,64,128]{3,2,1,0:T(8,128)(2,1)S(1)}, bf16[2,4,64,128]{3,2,1,0:T(8,128)(2,1)S(1)}, u32[]{:S(2)}, u32[]{:S(2)}) collective-permute-start(bf16[2,4,64,128]{3,2,1,0:T(8,128)(2,1)S(1)} %get-tuple-element.84), channel_id=1, source_target_pairs={{0,8},{4,12},{8,0},{12,4},{1,9},{5,13},{9,1},{13,5},{2,10},{6,14},... | collective-permute-start | bytes 393224 | tf_op jit(solution)/shard_map/ppermute | solution.py:397
  62.3 0.8 collective-permute-start.14
  63.2 3.4 %transform_rest.1 = (bf16[2,4,64,128]{3,2,1,0:T(8,128)(2,1)S(1)}, bf16[2,4,64,128]{3,2,1,0:T(8,128)(2,1)S(1)}, bf16[2,4,64,128]{3,2,1,0:T(8,128)(2,1)S(1)}, bf16...) custom-call(s32[8]{0:T(128)S(1)} %pad_add_fusion.1.place_ref, ...), custom_call_target="tpu_custom_call" | custom-call | flops 1610612736 | bytes 6291456 | tf_op jit(solution)/shard_map/transform_rest/pallas_call | solution.py:226
  66.6 0.0 collective-permute-done.12.rest_1_
  66.6 3.8 %collective-permute-done.13.rest_2_ = bf16[2,4,64,128]{3,2,1,0:T(8,128)(2,1)S(1)} collective-permute-done((bf16[2,4,64,128]{3,2,1,0:T(8,128)(2,1)S(1)}, bf16[2,4,64,128]{3,2,1,0:T(8,128)(2,1)S(1)}, u32[]{:S(2)}, u32[]{:S(2)}) %collective-permute-start.13) | collective-permute-done | bytes 131104 | tf_op jit(solution)/shard_map/ppermute | solution.py:397
  70.4 0.6 join_pieces.4.rest_4_
  71.0 1.6 %collective-permute-start.15 = (bf16[4,2,4,64,128]{4,3,2,1,0:T(8,128)(2,1)S(1)}, bf16[4,2,4,64,128]{4,3,2,1,0:T(8,128)(2,1)S(1)}, u32[]{:S(2)}, u32[]{:S(2)}) collective-permute-start(bf16[4,2,4,64,128]{4,3,2,1,0:T(8,128)(2,1)S(1)} %join_pieces.4.rest_4_), channel_id=1, source_target_pairs={{0,2},{1,3},{2,0},{3,1},{4,6},{5,7},{6,4},{7,5},{8,10},{9,11},{10,... | collective-permute-start | bytes 1572872 | tf_op jit(solution)/shard_map/ppermute | solution.py:403
  72.6 3.3 %collective-permute-start.3 = (bf16[2,4,64,128]{3,2,1,0:T(8,128)(2,1)S(1)}, bf16[2,4,64,128]{3,2,1,0:T(8,128)(2,1)S(1)}, u32[]{:S(2)}, u32[]{:S(2)}) collective-permute-start(bf16[2,4,64,128]{3,2,1,0:T(8,128)(2,1)S(1)} %get-tuple-element.71), channel_id=1, source_target_pairs={{0,4},{4,8},{8,12},{12,0},{1,5},{5,9},{9,13},{13,1},{2,6},{6,10},{... | collective-permute-start | bytes 393224 | tf_op jit(solution)/shard_map/ppermute | solution.py:397
  75.8 2.1 %collective-permute-start.4 = (bf16[2,4,64,128]{3,2,1,0:T(8,128)(2,1)S(1)}, bf16[2,4,64,128]{3,2,1,0:T(8,128)(2,1)S(1)}, u32[]{:S(2)}, u32[]{:S(2)}) collective-permute-start(bf16[2,4,64,128]{3,2,1,0:T(8,128)(2,1)S(1)} %get-tuple-element.72), channel_id=1, source_target_pairs={{0,8},{4,12},{8,0},{12,4},{1,9},{5,13},{9,1},{13,5},{2,10},{6,14},... | collective-permute-start | bytes 393224 | tf_op jit(solution)/shard_map/ppermute | solution.py:397
  77.9 0.3 collective-permute-start.5
  78.2 3.6 %collective-permute-done.3.rest_1_ = bf16[2,4,64,128]{3,2,1,0:T(8,128)(2,1)S(1)} collective-permute-done((bf16[2,4,64,128]{3,2,1,0:T(8,128)(2,1)S(1)}, bf16[2,4,64,128]{3,2,1,0:T(8,128)(2,1)S(1)}, u32[]{:S(2)}, u32[]{:S(2)}) %collective-permute-start.3) | collective-permute-done | bytes 131104 | tf_op jit(solution)/shard_map/ppermute | solution.py:397
  81.8 4.1 %collective-permute-done.4.rest_2_ = bf16[2,4,64,128]{3,2,1,0:T(8,128)(2,1)S(1)} collective-permute-done((bf16[2,4,64,128]{3,2,1,0:T(8,128)(2,1)S(1)}, bf16[2,4,64,128]{3,2,1,0:T(8,128)(2,1)S(1)}, u32[]{:S(2)}, u32[]{:S(2)}) %collective-permute-start.4) | collective-permute-done | bytes 131104 | tf_op jit(solution)/shard_map/ppermute | solution.py:397
  85.9 0.1 collective-permute-done.5.rest_3_
  86.1 0.6 join_pieces.5
  86.7 0.1 collective-permute-start.17
  86.8 0.6 collective-permute-start.16
  87.4 3.1 %collective-permute-start.6 = (bf16[2,4,64,128]{3,2,1,0:T(8,128)(2,1)S(1)}, bf16[2,4,64,128]{3,2,1,0:T(8,128)(2,1)S(1)}, u32[]{:S(2)}, u32[]{:S(2)}) collective-permute-start(bf16[2,4,64,128]{3,2,1,0:T(8,128)(2,1)S(1)} %get-tuple-element.75), channel_id=1, source_target_pairs={{0,4},{4,8},{8,12},{12,0},{1,5},{5,9},{9,13},{13,1},{2,6},{6,10},{... | collective-permute-start | bytes 393224 | tf_op jit(solution)/shard_map/ppermute | solution.py:397
  90.5 1.5 %collective-permute-start.7 = (bf16[2,4,64,128]{3,2,1,0:T(8,128)(2,1)S(1)}, bf16[2,4,64,128]{3,2,1,0:T(8,128)(2,1)S(1)}, u32[]{:S(2)}, u32[]{:S(2)}) collective-permute-start(bf16[2,4,64,128]{3,2,1,0:T(8,128)(2,1)S(1)} %get-tuple-element.76), channel_id=1, source_target_pairs={{0,8},{4,12},{8,0},{12,4},{1,9},{5,13},{9,1},{13,5},{2,10},{6,14},... | collective-permute-start | bytes 393224 | tf_op jit(solution)/shard_map/ppermute | solution.py:397
  92.0 0.9 collective-permute-start.8
  92.9 3.5 %correlate_tiles.4 = (f32[2,8,5,256,256]{4,3,2,1,0:T(8,128)}, f32[8,128]{1,0:T(8,128)S(1)}) custom-call(s32[11]{0:T(128)S(1)} %pad_add_fusion.rest_7_.rest_3_.rest_6_.table_ref, bf16[2,4,2,4,64,128]{5,4,3,2,1,0:T(8,128)(2,1)S(1)} %get-tuple-element.87.low_ref, bf16[2,4,2,4,64,128]{5,4,3,2,1,0:T(8,128)(2,1)S(1)} %collective-permute-done.17.high_ref), custom_call_target="tpu_custom_call" | custom-call | tf_op jit(solution)/shard_map/correlate_tiles/pallas_call | solution.py:362
  96.5 4.5 %collective-permute-done.7.rest_2_ = bf16[2,4,64,128]{3,2,1,0:T(8,128)(2,1)S(1)} collective-permute-done((bf16[2,4,64,128]{3,2,1,0:T(8,128)(2,1)S(1)}, bf16[2,4,64,128]{3,2,1,0:T(8,128)(2,1)S(1)}, u32[]{:S(2)}, u32[]{:S(2)}) %collective-permute-start.7) | collective-permute-done | bytes 131104 | tf_op jit(solution)/shard_map/ppermute | solution.py:397
  101.0 0.1 collective-permute-done.16.rest_5_
  101.1 0.6 join_pieces.6
  101.8 0.1 collective-permute-start.19
  101.9 1.3 collective-permute-start.18
  103.2 3.3 %collective-permute-start.9 = (bf16[2,4,64,128]{3,2,1,0:T(8,128)(2,1)S(1)}, bf16[2,4,64,128]{3,2,1,0:T(8,128)(2,1)S(1)}, u32[]{:S(2)}, u32[]{:S(2)}) collective-permute-start(bf16[2,4,64,128]{3,2,1,0:T(8,128)(2,1)S(1)} %get-tuple-element.79), channel_id=1, source_target_pairs={{0,4},{4,8},{8,12},{12,0},{1,5},{5,9},{9,13},{13,1},{2,6},{6,10},{... | collective-permute-start | bytes 393224 | tf_op jit(solution)/shard_map/ppermute | solution.py:397
  106.5 1.5 %collective-permute-start.10 = (bf16[2,4,64,128]{3,2,1,0:T(8,128)(2,1)S(1)}, bf16[2,4,64,128]{3,2,1,0:T(8,128)(2,1)S(1)}, u32[]{:S(2)}, u32[]{:S(2)}) collective-permute-start(bf16[2,4,64,128]{3,2,1,0:T(8,128)(2,1)S(1)} %get-tuple-element.80), channel_id=1, source_target_pairs={{0,8},{4,12},{8,0},{12,4},{1,9},{5,13},{9,1},{13,5},{2,10},{6,14},... | collective-permute-start | bytes 393224 | tf_op jit(solution)/shard_map/ppermute | solution.py:397
  108.0 0.8 collective-permute-start.11
  108.8 3.5 %correlate_tiles.5 = (f32[2,8,5,256,256]{4,3,2,1,0:T(8,128)}, f32[8,128]{1,0:T(8,128)S(1)}) custom-call(s32[11]{0:T(128)S(1)} %pad_add_fusion.rest_7_.rest_3_.rest_6_.table_ref, bf16[2,4,2,4,64,128]{5,4,3,2,1,0:T(8,128)(2,1)S(1)} %get-tuple-element.90.low_ref, ...), custom_call_target="tpu_custom_call", output_to_operand_aliasing={{0}: (3, {})} | custom-call | tf_op jit(solution)/shard_map/correlate_tiles/pallas_call | solution.py:362
  112.4 4.6 %collective-permute-done.10.rest_2_ = bf16[2,4,64,128]{3,2,1,0:T(8,128)(2,1)S(1)} collective-permute-done((bf16[2,4,64,128]{3,2,1,0:T(8,128)(2,1)S(1)}, bf16[2,4,64,128]{3,2,1,0:T(8,128)(2,1)S(1)}, u32[]{:S(2)}, u32[]{:S(2)}) %collective-permute-start.10) | collective-permute-done | bytes 131104 | tf_op jit(solution)/shard_map/ppermute | solution.py:397
  117.0 0.6 join_pieces.7
  117.6 0.1 collective-permute-start.21
  117.7 0.6 collective-permute-start.20
  118.3 2.0 %collective-permute-done.21.high_ref = bf16[2,4,2,4,64,128]{5,4,3,2,1,0:T(8,128)(2,1)S(1)} collective-permute-done((bf16[2,4,2,4,64,128]{5,4,3,2,1,0:T(8,128)(2,1)S(1)}, bf16[2,4,2,4,64,128]{5,4,3,2,1,0:T(8,128)(2,1)S(1)}, u32[]{:S(2)}, u32[]{:S(2)}) %collective-permute-start.21) | collective-permute-done | bytes 1048608 | tf_op jit(solution)/shard_map/ppermute | solution.py:403
  120.4 3.5 %correlate_tiles.6 = (f32[2,8,5,256,256]{4,3,2,1,0:T(8,128)}, f32[8,128]{1,0:T(8,128)S(1)}) custom-call(s32[11]{0:T(128)S(1)} %pad_add_fusion.rest_7_.rest_3_.rest_6_.table_ref, bf16[2,4,2,4,64,128]{5,4,3,2,1,0:T(8,128)(2,1)S(1)} %get-tuple-element.94.low_ref, ...), custom_call_target="tpu_custom_call", output_to_operand_aliasing={{0}: (3, {})} | custom-call | tf_op jit(solution)/shard_map/correlate_tiles/pallas_call | solution.py:362
  123.9 8.2 %collective-permute-done.20.other_ref = bf16[4,2,4,64,128]{4,3,2,1,0:T(8,128)(2,1)S(1)} collective-permute-done((bf16[4,2,4,64,128]{4,3,2,1,0:T(8,128)(2,1)S(1)}, bf16[4,2,4,64,128]{4,3,2,1,0:T(8,128)(2,1)S(1)}, u32[]{:S(2)}, u32[]{:S(2)}) %collective-permute-start.20) | collective-permute-done | bytes 524320 | tf_op jit(solution)/shard_map/ppermute | solution.py:403
  132.1 0.1 pair_blocks.1.low_ref
  132.1 0.1 collective-permute-start.22
  132.2 2.6 %collective-permute-done.22.high_ref = bf16[2,4,2,4,64,128]{5,4,3,2,1,0:T(8,128)(2,1)S(1)} collective-permute-done((bf16[2,4,2,4,64,128]{5,4,3,2,1,0:T(8,128)(2,1)S(1)}, bf16[2,4,2,4,64,128]{5,4,3,2,1,0:T(8,128)(2,1)S(1)}, u32[]{:S(2)}, u32[]{:S(2)}) %collective-permute-start.22) | collective-permute-done | bytes 1048608 | tf_op jit(solution)/shard_map/ppermute | solution.py:403
  134.9 4.1 %correlate_tiles.7 = (f32[2,8,5,256,256]{4,3,2,1,0:T(8,128)}, f32[8,128]{1,0:T(8,128)}) custom-call(s32[11]{0:T(128)S(1)} %pad_add_fusion.rest_7_.rest_3_.rest_6_.table_ref, bf16[2,4,2,4,64,128]{5,4,3,2,1,0:T(8,128)(2,1)S(1)} %pair_blocks.1.low_ref, ...), custom_call_target="tpu_custom_call", output_to_operand_aliasing={{0}: (3, {})} | custom-call | tf_op jit(solution)/shard_map/correlate_tiles/pallas_call | solution.py:362
  (17 shorter events, 0.1 us)
Async XLA Ops:
  0.1 1.6 %copy-start = (bf16[2,2048,256]{2,1,0:T(8,128)(2,1)S(1)}, bf16[2,2048,256]{2,1,0:T(8,128)(2,1)}, u32[]{:S(2)}) copy-start(bf16[2,2048,256]{2,1,0:T(8,128)(2,1)} %v_ref.1) | copy-start | bytes 6291460
  4.4 19.2 %collective-permute-start = (bf16[2,64,2048]{2,1,0:T(8,128)(2,1)}, bf16[2,64,2048]{2,1,0:T(8,128)(2,1)S(1)}, u32[]{:S(2)}, u32[]{:S(2)}) collective-permute-start(bf16[2,64,2048]{2,1,0:T(8,128)(2,1)} %get-tuple-element.53), channel_id=1, source_target_pairs={{0,4},{4,8},{8,12},{12,0},{1,5},{5,9},{9,13},{13,1},{2,6},{6,10},{... | collective-permute-start | bytes 1572872 | tf_op jit(solution)/shard_map/ppermute | solution.py:397
  7.4 36.8 %collective-permute-start.1 = (bf16[2,64,2048]{2,1,0:T(8,128)(2,1)S(1)}, bf16[2,64,2048]{2,1,0:T(8,128)(2,1)S(1)}, u32[]{:S(2)}, u32[]{:S(2)}) collective-permute-start(bf16[2,64,2048]{2,1,0:T(8,128)(2,1)S(1)} %get-tuple-element.54), channel_id=1, source_target_pairs={{0,8},{4,12},{8,0},{12,4},{1,9},{5,13},{9,1},{13,5},{2,10},{6,14},... | collective-permute-start | bytes 1572872 | tf_op jit(solution)/shard_map/ppermute | solution.py:397
  10.0 34.2 %collective-permute-start.2 = (bf16[2,64,2048]{2,1,0:T(8,128)(2,1)S(1)}, bf16[2,64,2048]{2,1,0:T(8,128)(2,1)S(1)}, u32[]{:S(2)}, u32[]{:S(2)}) collective-permute-start(bf16[2,64,2048]{2,1,0:T(8,128)(2,1)S(1)} %get-tuple-element.55), channel_id=1, source_target_pairs={{0,12},{4,0},{8,4},{12,8},{1,13},{5,1},{9,5},{13,9},{2,14},{6,2},{... | collective-permute-start | bytes 1572872 | tf_op jit(solution)/shard_map/ppermute | solution.py:397
  18.1 1.1 copy-start.1
  19.2 1.1 copy-start.2
  20.3 0.7 copy-start.3
  21.0 0.7 copy-start.4
  49.0 17.6 %collective-permute-start.12 = (bf16[2,4,64,128]{3,2,1,0:T(8,128)(2,1)S(1)}, bf16[2,4,64,128]{3,2,1,0:T(8,128)(2,1)S(1)}, u32[]{:S(2)}, u32[]{:S(2)}) collective-permute-start(bf16[2,4,64,128]{3,2,1,0:T(8,128)(2,1)S(1)} %get-tuple-element.83), channel_id=1, source_target_pairs={{0,4},{4,8},{8,12},{12,0},{1,5},{5,9},{9,13},{13,1},{2,6},{6,10},{... | collective-permute-start | bytes 393224 | tf_op jit(solution)/shard_map/ppermute | solution.py:397
  60.7 9.7 %collective-permute-start.13 = (bf16[2,4,64,128]{3,2,1,0:T(8,128)(2,1)S(1)}, bf16[2,4,64,128]{3,2,1,0:T(8,128)(2,1)S(1)}, u32[]{:S(2)}, u32[]{:S(2)}) collective-permute-start(bf16[2,4,64,128]{3,2,1,0:T(8,128)(2,1)S(1)} %get-tuple-element.84), channel_id=1, source_target_pairs={{0,8},{4,12},{8,0},{12,4},{1,9},{5,13},{9,1},{13,5},{2,10},{6,14},... | collective-permute-start | bytes 393224 | tf_op jit(solution)/shard_map/ppermute | solution.py:397
  62.3 8.1 %collective-permute-start.14 = (bf16[2,4,64,128]{3,2,1,0:T(8,128)(2,1)S(1)}, bf16[2,4,64,128]{3,2,1,0:T(8,128)(2,1)S(1)}, u32[]{:S(2)}, u32[]{:S(2)}) collective-permute-start(bf16[2,4,64,128]{3,2,1,0:T(8,128)(2,1)S(1)} %get-tuple-element.85), channel_id=1, source_target_pairs={{0,12},{4,0},{8,4},{12,8},{1,13},{5,1},{9,5},{13,9},{2,14},{6,2},{... | collective-permute-start | bytes 393224 | tf_op jit(solution)/shard_map/ppermute | solution.py:397
  71.0 15.1 %collective-permute-start.15 = (bf16[4,2,4,64,128]{4,3,2,1,0:T(8,128)(2,1)S(1)}, bf16[4,2,4,64,128]{4,3,2,1,0:T(8,128)(2,1)S(1)}, u32[]{:S(2)}, u32[]{:S(2)}) collective-permute-start(bf16[4,2,4,64,128]{4,3,2,1,0:T(8,128)(2,1)S(1)} %join_pieces.4.rest_4_), channel_id=1, source_target_pairs={{0,2},{1,3},{2,0},{3,1},{4,6},{5,7},{6,4},{7,5},{8,10},{9,11},{10,... | collective-permute-start | bytes 1572872 | tf_op jit(solution)/shard_map/ppermute | solution.py:403
  72.6 9.3 %collective-permute-start.3 = (bf16[2,4,64,128]{3,2,1,0:T(8,128)(2,1)S(1)}, bf16[2,4,64,128]{3,2,1,0:T(8,128)(2,1)S(1)}, u32[]{:S(2)}, u32[]{:S(2)}) collective-permute-start(bf16[2,4,64,128]{3,2,1,0:T(8,128)(2,1)S(1)} %get-tuple-element.71), channel_id=1, source_target_pairs={{0,4},{4,8},{8,12},{12,0},{1,5},{5,9},{9,13},{13,1},{2,6},{6,10},{... | collective-permute-start | bytes 393224 | tf_op jit(solution)/shard_map/ppermute | solution.py:397
  75.8 10.1 %collective-permute-start.4 = (bf16[2,4,64,128]{3,2,1,0:T(8,128)(2,1)S(1)}, bf16[2,4,64,128]{3,2,1,0:T(8,128)(2,1)S(1)}, u32[]{:S(2)}, u32[]{:S(2)}) collective-permute-start(bf16[2,4,64,128]{3,2,1,0:T(8,128)(2,1)S(1)} %get-tuple-element.72), channel_id=1, source_target_pairs={{0,8},{4,12},{8,0},{12,4},{1,9},{5,13},{9,1},{13,5},{2,10},{6,14},... | collective-permute-start | bytes 393224 | tf_op jit(solution)/shard_map/ppermute | solution.py:397
  77.9 8.1 %collective-permute-start.5 = (bf16[2,4,64,128]{3,2,1,0:T(8,128)(2,1)S(1)}, bf16[2,4,64,128]{3,2,1,0:T(8,128)(2,1)S(1)}, u32[]{:S(2)}, u32[]{:S(2)}) collective-permute-start(bf16[2,4,64,128]{3,2,1,0:T(8,128)(2,1)S(1)} %get-tuple-element.73), channel_id=1, source_target_pairs={{0,12},{4,0},{8,4},{12,8},{1,13},{5,1},{9,5},{13,9},{2,14},{6,2},{... | collective-permute-start | bytes 393224 | tf_op jit(solution)/shard_map/ppermute | solution.py:397
  86.7 6.2 %collective-permute-start.17 = (bf16[2,4,2,4,64,128]{5,4,3,2,1,0:T(8,128)(2,1)S(1)}, bf16[2,4,2,4,64,128]{5,4,3,2,1,0:T(8,128)(2,1)S(1)}, u32[]{:S(2)}, u32[]{:S(2)}) collective-permute-start(bf16[2,4,2,4,64,128]{5,4,3,2,1,0:T(8,128)(2,1)S(1)} %get-tuple-element.87.low_ref), channel_id=1, source_target_pairs={{0,1},{1,0},{2,3},{3,2},{4,5},{5,4},{6,7},{7,6},{8,9},{9,8},{10,11... | collective-permute-start | bytes 3145736 | tf_op jit(solution)/shard_map/ppermute | solution.py:403
  86.8 14.3 %collective-permute-start.16 = (bf16[4,2,4,64,128]{4,3,2,1,0:T(8,128)(2,1)S(1)}, bf16[4,2,4,64,128]{4,3,2,1,0:T(8,128)(2,1)S(1)}, u32[]{:S(2)}, u32[]{:S(2)}) collective-permute-start(bf16[4,2,4,64,128]{4,3,2,1,0:T(8,128)(2,1)S(1)} %get-tuple-element.86.rest_4_), channel_id=1, source_target_pairs={{0,2},{1,3},{2,0},{3,1},{4,6},{5,7},{6,4},{7,5},{8,10},{9,11},{10,... | collective-permute-start | bytes 1572872 | tf_op jit(solution)/shard_map/ppermute | solution.py:403
  87.4 9.1 %collective-permute-start.6 = (bf16[2,4,64,128]{3,2,1,0:T(8,128)(2,1)S(1)}, bf16[2,4,64,128]{3,2,1,0:T(8,128)(2,1)S(1)}, u32[]{:S(2)}, u32[]{:S(2)}) collective-permute-start(bf16[2,4,64,128]{3,2,1,0:T(8,128)(2,1)S(1)} %get-tuple-element.75), channel_id=1, source_target_pairs={{0,4},{4,8},{8,12},{12,0},{1,5},{5,9},{9,13},{13,1},{2,6},{6,10},{... | collective-permute-start | bytes 393224 | tf_op jit(solution)/shard_map/ppermute | solution.py:397
  90.5 10.5 %collective-permute-start.7 = (bf16[2,4,64,128]{3,2,1,0:T(8,128)(2,1)S(1)}, bf16[2,4,64,128]{3,2,1,0:T(8,128)(2,1)S(1)}, u32[]{:S(2)}, u32[]{:S(2)}) collective-permute-start(bf16[2,4,64,128]{3,2,1,0:T(8,128)(2,1)S(1)} %get-tuple-element.76), channel_id=1, source_target_pairs={{0,8},{4,12},{8,0},{12,4},{1,9},{5,13},{9,1},{13,5},{2,10},{6,14},... | collective-permute-start | bytes 393224 | tf_op jit(solution)/shard_map/ppermute | solution.py:397
  92.0 9.0 %collective-permute-start.8 = (bf16[2,4,64,128]{3,2,1,0:T(8,128)(2,1)S(1)}, bf16[2,4,64,128]{3,2,1,0:T(8,128)(2,1)S(1)}, u32[]{:S(2)}, u32[]{:S(2)}) collective-permute-start(bf16[2,4,64,128]{3,2,1,0:T(8,128)(2,1)S(1)} %get-tuple-element.77), channel_id=1, source_target_pairs={{0,12},{4,0},{8,4},{12,8},{1,13},{5,1},{9,5},{13,9},{2,14},{6,2},{... | collective-permute-start | bytes 393224 | tf_op jit(solution)/shard_map/ppermute | solution.py:397
  101.8 7.1 %collective-permute-start.19 = (bf16[2,4,2,4,64,128]{5,4,3,2,1,0:T(8,128)(2,1)S(1)}, bf16[2,4,2,4,64,128]{5,4,3,2,1,0:T(8,128)(2,1)S(1)}, u32[]{:S(2)}, u32[]{:S(2)}) collective-permute-start(bf16[2,4,2,4,64,128]{5,4,3,2,1,0:T(8,128)(2,1)S(1)} %get-tuple-element.90.low_ref), channel_id=1, source_target_pairs={{0,1},{1,0},{2,3},{3,2},{4,5},{5,4},{6,7},{7,6},{8,9},{9,8},{10,11... | collective-permute-start | bytes 3145736 | tf_op jit(solution)/shard_map/ppermute | solution.py:403
  101.9 15.1 %collective-permute-start.18 = (bf16[4,2,4,64,128]{4,3,2,1,0:T(8,128)(2,1)S(1)}, bf16[4,2,4,64,128]{4,3,2,1,0:T(8,128)(2,1)S(1)}, u32[]{:S(2)}, u32[]{:S(2)}) collective-permute-start(bf16[4,2,4,64,128]{4,3,2,1,0:T(8,128)(2,1)S(1)} %get-tuple-element.89.rest_4_), channel_id=1, source_target_pairs={{0,2},{1,3},{2,0},{3,1},{4,6},{5,7},{6,4},{7,5},{8,10},{9,11},{10,... | collective-permute-start | bytes 1572872 | tf_op jit(solution)/shard_map/ppermute | solution.py:403
  103.2 9.2 %collective-permute-start.9 = (bf16[2,4,64,128]{3,2,1,0:T(8,128)(2,1)S(1)}, bf16[2,4,64,128]{3,2,1,0:T(8,128)(2,1)S(1)}, u32[]{:S(2)}, u32[]{:S(2)}) collective-permute-start(bf16[2,4,64,128]{3,2,1,0:T(8,128)(2,1)S(1)} %get-tuple-element.79), channel_id=1, source_target_pairs={{0,4},{4,8},{8,12},{12,0},{1,5},{5,9},{9,13},{13,1},{2,6},{6,10},{... | collective-permute-start | bytes 393224 | tf_op jit(solution)/shard_map/ppermute | solution.py:397
  106.5 10.5 %collective-permute-start.10 = (bf16[2,4,64,128]{3,2,1,0:T(8,128)(2,1)S(1)}, bf16[2,4,64,128]{3,2,1,0:T(8,128)(2,1)S(1)}, u32[]{:S(2)}, u32[]{:S(2)}) collective-permute-start(bf16[2,4,64,128]{3,2,1,0:T(8,128)(2,1)S(1)} %get-tuple-element.80), channel_id=1, source_target_pairs={{0,8},{4,12},{8,0},{12,4},{1,9},{5,13},{9,1},{13,5},{2,10},{6,14},... | collective-permute-start | bytes 393224 | tf_op jit(solution)/shard_map/ppermute | solution.py:397
  108.0 9.0 %collective-permute-start.11 = (bf16[2,4,64,128]{3,2,1,0:T(8,128)(2,1)S(1)}, bf16[2,4,64,128]{3,2,1,0:T(8,128)(2,1)S(1)}, u32[]{:S(2)}, u32[]{:S(2)}) collective-permute-start(bf16[2,4,64,128]{3,2,1,0:T(8,128)(2,1)S(1)} %get-tuple-element.81), channel_id=1, source_target_pairs={{0,12},{4,0},{8,4},{12,8},{1,13},{5,1},{9,5},{13,9},{2,14},{6,2},{... | collective-permute-start | bytes 393224 | tf_op jit(solution)/shard_map/ppermute | solution.py:397
  117.6 2.7 %collective-permute-start.21 = (bf16[2,4,2,4,64,128]{5,4,3,2,1,0:T(8,128)(2,1)S(1)}, bf16[2,4,2,4,64,128]{5,4,3,2,1,0:T(8,128)(2,1)S(1)}, u32[]{:S(2)}, u32[]{:S(2)}) collective-permute-start(bf16[2,4,2,4,64,128]{5,4,3,2,1,0:T(8,128)(2,1)S(1)} %get-tuple-element.94.low_ref), channel_id=1, source_target_pairs={{0,1},{1,0},{2,3},{3,2},{4,5},{5,4},{6,7},{7,6},{8,9},{9,8},{10,11... | collective-permute-start | bytes 3145736 | tf_op jit(solution)/shard_map/ppermute | solution.py:403
  117.7 14.3 %collective-permute-start.20 = (bf16[4,2,4,64,128]{4,3,2,1,0:T(8,128)(2,1)S(1)}, bf16[4,2,4,64,128]{4,3,2,1,0:T(8,128)(2,1)S(1)}, u32[]{:S(2)}, u32[]{:S(2)}) collective-permute-start(bf16[4,2,4,64,128]{4,3,2,1,0:T(8,128)(2,1)S(1)} %get-tuple-element.93.own_ref), channel_id=1, source_target_pairs={{0,2},{1,3},{2,0},{3,1},{4,6},{5,7},{6,4},{7,5},{8,10},{9,11},{10,... | collective-permute-start | bytes 1572872 | tf_op jit(solution)/shard_map/ppermute | solution.py:403
  132.1 2.7 %collective-permute-start.22 = (bf16[2,4,2,4,64,128]{5,4,3,2,1,0:T(8,128)(2,1)S(1)}, bf16[2,4,2,4,64,128]{5,4,3,2,1,0:T(8,128)(2,1)S(1)}, u32[]{:S(2)}, u32[]{:S(2)}) collective-permute-start(bf16[2,4,2,4,64,128]{5,4,3,2,1,0:T(8,128)(2,1)S(1)} %pair_blocks.1.low_ref), channel_id=1, source_target_pairs={{0,1},{1,0},{2,3},{3,2},{4,5},{5,4},{6,7},{7,6},{8,9},{9,8},{10,11... | collective-permute-start | bytes 3145736 | tf_op jit(solution)/shard_map/ppermute | solution.py:403

commit v6 on v3

--- a/solution.py
+++ b/solution.py
@@ -287,10 +287,9 @@
     )(own, other, after)
 
 
-def correlate_kernel(chunks, scale, first, table_ref, low_ref, high_ref, *rest):
+def correlate_kernel(order, chunks, scale, first, table_ref, *rest):
     o_ref, token_ref, left, tiles, empty, sems = rest[-6:]
-    half, senders, _, spectra, rows, lanes = low_ref.shape
-    order = block_order(2 * half)
+    each, senders, _, spectra, rows, lanes = rest[0].shape
     slots = o_ref.shape[2]
     coarse = lanes // AVG
     side = senders * rows
@@ -310,7 +309,7 @@
                 copy_out(empty, c, slot).start()
 
     for at, block in enumerate(order):
-        source = (low_ref, high_ref)[at // half].at[at % half]
+        source = rest[at // each].at[at % each]
         for sender in range(senders):
             for part in range(2):
                 for chunk in range(chunks):
@@ -348,26 +347,26 @@
             copy_out(empty, c, slot).wait()
 
 
-def correlate(table, gathered, first, channels, chunks, slots, vis):
-    half, senders, _, spectra, rows, lanes = gathered[0].shape
+def correlate(table, gathered, after, order, first, channels, chunks, slots, vis):
+    _, senders, _, spectra, rows, lanes = gathered[0].shape
     coarse = lanes // AVG
     side = senders * rows
     vmem = pl.BlockSpec(memory_space=pltpu.VMEM)
     anywhere = pl.BlockSpec(memory_space=pl.ANY)
-    args = [table, *gathered]
+    args = [table, *gathered, after]
     aliases = {}
     if vis is not None:
         args.append(vis)
         aliases = {len(args) - 1: 0}
     return pl.pallas_call(
-        functools.partial(correlate_kernel, chunks, 1.0 / (AVG * spectra), first),
+        functools.partial(correlate_kernel, order, chunks, 1.0 / (AVG * spectra), first),
         grid_spec=pltpu.PrefetchScalarGridSpec(
             num_scalar_prefetch=1,
             grid=(),
-            in_specs=[vmem, vmem] + [anywhere] * (len(args) - 3),
+            in_specs=[vmem] * len(gathered) + [anywhere] * (len(args) - 1 - len(gathered)),
             out_specs=[anywhere, vmem],
             scratch_shapes=[
-                pltpu.VMEM((coarse, 2 * half, 2 * side, spectra * AVG), jnp.bfloat16),
+                pltpu.VMEM((coarse, len(order), 2 * side, spectra * AVG), jnp.bfloat16),
                 pltpu.VMEM((coarse, slots, 2, side, side), jnp.float32),
                 pltpu.VMEM((2, side, side), jnp.float32),
                 pltpu.SemaphoreType.DMA((coarse, slots)),
@@ -411,6 +410,16 @@
         held = pair(held, other, after).reshape(-1, *held.shape[1:])
         other = exchange(held, bit)
     return held, other
+
+
+def gather_apart(own, partner, after):
+    bit = lax.axis_size("bl") // 4
+    partner, after = lax.optimization_barrier((partner, after))
+    held = [own[None], partner[None]]
+    while bit:
+        held = held + [exchange(block, bit) for block in held]
+        bit //= 2
+    return held, after
 
 
 def block_order(count):
@@ -512,14 +521,23 @@
             else:
                 (own,) = join(arrived, place, (), firsts[-1])
             other = exchange(own, half)
-        else:
-            held = pair(own, other, tokens[-1])
         if unit > 0:
-            gathered = gather_blocks(held, table)
+            if unit < units:
+                gathered, after = gather_blocks(held, table), table
+            else:
+                gathered, after = gather_apart(own, other, tokens[-1])
             cut, part = divmod(unit - 1, radix // dests)
             first = (part * MXU + cut * LANES) // AVG
             vis, token = correlate(
-                table, gathered, first, units * LANES // AVG, chunks, slot_cap, vis
+                table,
+                gathered,
+                after,
+                block_order(lax.axis_size("bl")),
+                first,
+                units * LANES // AVG,
+                chunks,
+                slot_cap,
+                vis,
             )
             tokens.append(token)
     return vis

time: 141 us -> 140 us (level)
    ppermute x8 -> x9, waiting for transfers between devices: 13 us -> 12.1 us  [exchange(): return lax.ppermute(own, 'bl', [(i, i ^ bit) for i in range(count)])]
    ppermute x8 -> x9, starting transfers between devices: 4.38 us -> 4.47 us  [exchange(): return lax.ppermute(own, 'bl', [(i, i ^ bit) for i in range(count)])]
    pallas_call x5 -> x4, Pallas kernels: 14.8 us -> 14.7 us  [correlate(): pl.pallas_call(functools.partial(correlate_kernel, order, chunks, 1.0 / (...]
  transfers between devices with their start and end apart: 23 -> 24, of which waited for: 11 -> 11; matrix products, arithmetic and copies ran while one was open for 6% -> 6% of each run, Pallas kernels for 10% -> 10%
where the time goes in v6:
time: 140 us; the launch traced here: 138 us
  waiting for transfers between devices  53.5 us (38%)
  starting transfers between devices  42.4 us (30%)
  Pallas kernels  28.3 us (20%)
  local copies, waits for them, and re-layouts  9.17 us (7%)
  other arithmetic  4.61 us (3%)
    ppermute x15, waiting for transfers between devices, spread(): lax.ppermute(pieces[d], 'ft', [(i, (i + d) % count) for i in range(count)])  41.4 us
    ppermute x15, starting transfers between devices, spread(): lax.ppermute(pieces[d], 'ft', [(i, (i + d) % count) for i in range(count)])  37.9 us
    pallas_call x4, Pallas kernels, correlate(): pl.pallas_call(functools.partial(correlate_kernel, order, chunks, 1.0 / (...  14.7 us
    ppermute x9, waiting for transfers between devices, exchange(): return lax.ppermute(own, 'bl', [(i, i ^ bit) for i in range(count)])  12.1 us
    pallas_call x2, Pallas kernels, transform_cut(): pl.pallas_call(kernel, grid_spec=pltpu.PrefetchScalarGridSpec(num_scalar_...  8.24 us
    unnamed x10, local copies, waits for them, and re-layouts  5.25 us
    ppermute x9, starting transfers between devices, exchange(): return lax.ppermute(own, 'bl', [(i, i ^ bit) for i in range(count)])  4.47 us
    reshape x2, local copies, waits for them, and re-layouts, per_device_kernels(): coef_table = coefs.reshape(taps, MXU, radix).transpose(0, 2, 1)  3.92 us
  transfers between devices with their start and end apart: 24, of which 11 were waited for; matrix products, arithmetic and copies ran while one was open for 6% of the time, Pallas kernels for 10%

profile of v6, /device:TPU:0, one launch (start us, length us, event | category | flops | bytes accessed | tf_op | source)
XLA Modules:
  0.0 138.3 jit_solution(12426423510945279008)
XLA Ops:
  0.0 0.1 pad_add_fusion.1.place_ref
  0.1 1.6 %copy-done = bf16[2,2048,256]{2,1,0:T(8,128)(2,1)S(1)} copy-done((bf16[2,2048,256]{2,1,0:T(8,128)(2,1)S(1)}, bf16[2,2048,256]{2,1,0:T(8,128)(2,1)}, u32[]{:S(2)}) %copy-start) | copy-done | bytes 2097176
  1.7 2.7 %pack_inputs.1 = (bf16[2,64,2048]{2,1,0:T(8,128)(2,1)S(1)}, bf16[2,64,2048]{2,1,0:T(8,128)(2,1)}, bf16[2,64,2048]{2,1,0:T(8,128)(2,1)S(1)}, bf16[2,64,2048]{2,1,0:T(8,128)(2,1)S(1)}) custom-call(s32[8]{0:T(128)S(1)} %pad_add_fusion.1.place_ref, bf16[2,2048,256]{2,1,0:T(8,128)(2,1)S(1)} %copy-done), custom_call_target="tpu_custom_call" | custom-call | tf_op jit(solution)/shard_map/pack_inputs/pallas_call | solution.py:97
  4.4 3.0 %collective-permute-start = (bf16[2,64,2048]{2,1,0:T(8,128)(2,1)}, bf16[2,64,2048]{2,1,0:T(8,128)(2,1)S(1)}, u32[]{:S(2)}, u32[]{:S(2)}) collective-permute-start(bf16[2,64,2048]{2,1,0:T(8,128)(2,1)} %get-tuple-element.55), channel_id=1, source_target_pairs={{0,4},{4,8},{8,12},{12,0},{1,5},{5,9},{9,13},{13,1},{2,6},{6,10},{... | collective-permute-start | bytes 1572872 | tf_op jit(solution)/shard_map/ppermute | solution.py:395
  7.4 2.6 %collective-permute-start.1 = (bf16[2,64,2048]{2,1,0:T(8,128)(2,1)S(1)}, bf16[2,64,2048]{2,1,0:T(8,128)(2,1)S(1)}, u32[]{:S(2)}, u32[]{:S(2)}) collective-permute-start(bf16[2,64,2048]{2,1,0:T(8,128)(2,1)S(1)} %get-tuple-element.56), channel_id=1, source_target_pairs={{0,8},{4,12},{8,0},{12,4},{1,9},{5,13},{9,1},{13,5},{2,10},{6,14},... | collective-permute-start | bytes 1572872 | tf_op jit(solution)/shard_map/ppermute | solution.py:395
  10.0 1.3 collective-permute-start.2
  11.3 0.8 fusion.1
  12.1 2.4 %reshape.11 = f32[8,256,8]{2,1,0:T(8,128)} reshape(f32[8,2048]{1,0:T(8,128)} %param.16) | data formatting | bytes 131072 | tf_op jit(solution)/shard_map/reshape | solution.py:488
  14.5 1.5 %copy.20 = f32[8,256,8]{1,2,0:T(8,128)S(1)} copy(f32[8,256,8]{2,1,0:T(8,128)} %reshape.11) | data formatting | bytes 131072 | tf_op jit(solution)/shard_map/reshape | solution.py:488
  16.0 0.7 broadcast_compare_fusion
  16.7 0.6 reduce_sum.69
  17.3 0.8 select_reduce_fusion.3
  18.1 1.1 copy-done.1
  19.2 1.1 copy-done.2
  20.4 0.7 copy-done.3
  21.1 0.7 copy-done.4
  21.7 0.1 stage_tables.1
  21.9 0.8 multiply_reduce_fusion
  22.7 0.2 select_reduce_fusion.1
  22.8 0.7 pad_add_fusion.rest_7_.rest_3_.rest_6_.table_ref.rest_2_
  23.6 20.6 %collective-permute-done.1.rest_2_ = bf16[2,64,2048]{2,1,0:T(8,128)(2,1)S(1)} collective-permute-done((bf16[2,64,2048]{2,1,0:T(8,128)(2,1)S(1)}, bf16[2,64,2048]{2,1,0:T(8,128)(2,1)S(1)}, u32[]{:S(2)}, u32[]{:S(2)}) %collective-permute-start.1) | collective-permute-done | bytes 524320 | tf_op jit(solution)/shard_map/ppermute | solution.py:395
  44.2 0.0 collective-permute-done.2.rest_3_
  44.2 4.8 %filter_transform.1 = (bf16[2,4,64,128]{3,2,1,0:T(8,128)(2,1)S(1)}, bf16[2,4,64,128]{3,2,1,0:T(8,128)(2,1)S(1)}, bf16[2,4,64,128]{3,2,1,0:T(8,128)(2,1)S(1)}, bf...) custom-call(s32[8]{0:T(128)S(1)} %pad_add_fusion.1.place_ref, ...), custom_call_target="tpu_custom_call" | custom-call | flops 1610612736 | bytes 6291456 | tf_op jit(solution)/shard_map/filter_transform/pallas_call | solution.py:226
  49.0 11.8 %collective-permute-start.12 = (bf16[2,4,64,128]{3,2,1,0:T(8,128)(2,1)S(1)}, bf16[2,4,64,128]{3,2,1,0:T(8,128)(2,1)S(1)}, u32[]{:S(2)}, u32[]{:S(2)}) collective-permute-start(bf16[2,4,64,128]{3,2,1,0:T(8,128)(2,1)S(1)} %get-tuple-element.85), channel_id=1, source_target_pairs={{0,4},{4,8},{8,12},{12,0},{1,5},{5,9},{9,13},{13,1},{2,6},{6,10},{... | collective-permute-start | bytes 393224 | tf_op jit(solution)/shard_map/ppermute | solution.py:395
  60.7 1.6 %collective-permute-start.13 = (bf16[2,4,64,128]{3,2,1,0:T(8,128)(2,1)S(1)}, bf16[2,4,64,128]{3,2,1,0:T(8,128)(2,1)S(1)}, u32[]{:S(2)}, u32[]{:S(2)}) collective-permute-start(bf16[2,4,64,128]{3,2,1,0:T(8,128)(2,1)S(1)} %get-tuple-element.86), channel_id=1, source_target_pairs={{0,8},{4,12},{8,0},{12,4},{1,9},{5,13},{9,1},{13,5},{2,10},{6,14},... | collective-permute-start | bytes 393224 | tf_op jit(solution)/shard_map/ppermute | solution.py:395
  62.3 0.8 collective-permute-start.14
  63.2 3.4 %transform_rest.1 = (bf16[2,4,64,128]{3,2,1,0:T(8,128)(2,1)S(1)}, bf16[2,4,64,128]{3,2,1,0:T(8,128)(2,1)S(1)}, bf16[2,4,64,128]{3,2,1,0:T(8,128)(2,1)S(1)}, bf16...) custom-call(s32[8]{0:T(128)S(1)} %pad_add_fusion.1.place_ref, ...), custom_call_target="tpu_custom_call" | custom-call | flops 1610612736 | bytes 6291456 | tf_op jit(solution)/shard_map/transform_rest/pallas_call | solution.py:226
  66.6 0.0 collective-permute-done.12.rest_1_
  66.6 3.8 %collective-permute-done.13.rest_2_ = bf16[2,4,64,128]{3,2,1,0:T(8,128)(2,1)S(1)} collective-permute-done((bf16[2,4,64,128]{3,2,1,0:T(8,128)(2,1)S(1)}, bf16[2,4,64,128]{3,2,1,0:T(8,128)(2,1)S(1)}, u32[]{:S(2)}, u32[]{:S(2)}) %collective-permute-start.13) | collective-permute-done | bytes 131104 | tf_op jit(solution)/shard_map/ppermute | solution.py:395
  70.4 0.0 collective-permute-done.14.rest_3_
  70.4 0.6 join_pieces.4.rest_4_
  71.0 1.6 %collective-permute-start.15 = (bf16[4,2,4,64,128]{4,3,2,1,0:T(8,128)(2,1)S(1)}, bf16[4,2,4,64,128]{4,3,2,1,0:T(8,128)(2,1)S(1)}, u32[]{:S(2)}, u32[]{:S(2)}) collective-permute-start(bf16[4,2,4,64,128]{4,3,2,1,0:T(8,128)(2,1)S(1)} %join_pieces.4.rest_4_), channel_id=1, source_target_pairs={{0,2},{1,3},{2,0},{3,1},{4,6},{5,7},{6,4},{7,5},{8,10},{9,11},{10,... | collective-permute-start | bytes 1572872 | tf_op jit(solution)/shard_map/ppermute | solution.py:402
  72.6 3.3 %collective-permute-start.3 = (bf16[2,4,64,128]{3,2,1,0:T(8,128)(2,1)S(1)}, bf16[2,4,64,128]{3,2,1,0:T(8,128)(2,1)S(1)}, u32[]{:S(2)}, u32[]{:S(2)}) collective-permute-start(bf16[2,4,64,128]{3,2,1,0:T(8,128)(2,1)S(1)} %get-tuple-element.73), channel_id=1, source_target_pairs={{0,4},{4,8},{8,12},{12,0},{1,5},{5,9},{9,13},{13,1},{2,6},{6,10},{... | collective-permute-start | bytes 393224 | tf_op jit(solution)/shard_map/ppermute | solution.py:395
  75.8 2.1 %collective-permute-start.4 = (bf16[2,4,64,128]{3,2,1,0:T(8,128)(2,1)S(1)}, bf16[2,4,64,128]{3,2,1,0:T(8,128)(2,1)S(1)}, u32[]{:S(2)}, u32[]{:S(2)}) collective-permute-start(bf16[2,4,64,128]{3,2,1,0:T(8,128)(2,1)S(1)} %get-tuple-element.74), channel_id=1, source_target_pairs={{0,8},{4,12},{8,0},{12,4},{1,9},{5,13},{9,1},{13,5},{2,10},{6,14},... | collective-permute-start | bytes 393224 | tf_op jit(solution)/shard_map/ppermute | solution.py:395
  77.9 0.3 collective-permute-start.5
  78.2 3.6 %collective-permute-done.3.rest_1_ = bf16[2,4,64,128]{3,2,1,0:T(8,128)(2,1)S(1)} collective-permute-done((bf16[2,4,64,128]{3,2,1,0:T(8,128)(2,1)S(1)}, bf16[2,4,64,128]{3,2,1,0:T(8,128)(2,1)S(1)}, u32[]{:S(2)}, u32[]{:S(2)}) %collective-permute-start.3) | collective-permute-done | bytes 131104 | tf_op jit(solution)/shard_map/ppermute | solution.py:395
  81.8 4.1 %collective-permute-done.4.rest_2_ = bf16[2,4,64,128]{3,2,1,0:T(8,128)(2,1)S(1)} collective-permute-done((bf16[2,4,64,128]{3,2,1,0:T(8,128)(2,1)S(1)}, bf16[2,4,64,128]{3,2,1,0:T(8,128)(2,1)S(1)}, u32[]{:S(2)}, u32[]{:S(2)}) %collective-permute-start.4) | collective-permute-done | bytes 131104 | tf_op jit(solution)/shard_map/ppermute | solution.py:395
  85.9 0.1 collective-permute-done.5.rest_3_
  86.1 0.6 join_pieces.5
  86.7 0.1 collective-permute-start.17
  86.8 0.6 collective-permute-start.16
  87.4 3.1 %collective-permute-start.6 = (bf16[2,4,64,128]{3,2,1,0:T(8,128)(2,1)S(1)}, bf16[2,4,64,128]{3,2,1,0:T(8,128)(2,1)S(1)}, u32[]{:S(2)}, u32[]{:S(2)}) collective-permute-start(bf16[2,4,64,128]{3,2,1,0:T(8,128)(2,1)S(1)} %get-tuple-element.77), channel_id=1, source_target_pairs={{0,4},{4,8},{8,12},{12,0},{1,5},{5,9},{9,13},{13,1},{2,6},{6,10},{... | collective-permute-start | bytes 393224 | tf_op jit(solution)/shard_map/ppermute | solution.py:395
  90.5 1.5 %collective-permute-start.7 = (bf16[2,4,64,128]{3,2,1,0:T(8,128)(2,1)S(1)}, bf16[2,4,64,128]{3,2,1,0:T(8,128)(2,1)S(1)}, u32[]{:S(2)}, u32[]{:S(2)}) collective-permute-start(bf16[2,4,64,128]{3,2,1,0:T(8,128)(2,1)S(1)} %get-tuple-element.78), channel_id=1, source_target_pairs={{0,8},{4,12},{8,0},{12,4},{1,9},{5,13},{9,1},{13,5},{2,10},{6,14},... | collective-permute-start | bytes 393224 | tf_op jit(solution)/shard_map/ppermute | solution.py:395
  92.0 0.9 collective-permute-start.8
  92.9 3.5 %correlate_tiles.4 = (f32[2,8,5,256,256]{4,3,2,1,0:T(8,128)}, f32[8,128]{1,0:T(8,128)S(1)}) custom-call(s32[11]{0:T(128)S(1)} %pad_add_fusion.rest_7_.rest_3_.rest_6_.table_ref.rest_2_, bf16[2,4,2,4,64,128]{5,4,3,2,1,0:T(8,128)(2,1)S(1)} %get-tuple-element.89.rest_0_, bf16[2,4,2,4,64,128]{5,4,3,2,1,0:T(8,128)(2,1)S(1)} %collective-permute-done.17.rest_1_, ...), custom_call_target="tpu_custom_call" | custom-call | tf_op jit(solution)/shard_map/correlate_tiles/pallas_call | solution.py:361
  96.5 4.5 %collective-permute-done.7.rest_2_ = bf16[2,4,64,128]{3,2,1,0:T(8,128)(2,1)S(1)} collective-permute-done((bf16[2,4,64,128]{3,2,1,0:T(8,128)(2,1)S(1)}, bf16[2,4,64,128]{3,2,1,0:T(8,128)(2,1)S(1)}, u32[]{:S(2)}, u32[]{:S(2)}) %collective-permute-start.7) | collective-permute-done | bytes 131104 | tf_op jit(solution)/shard_map/ppermute | solution.py:395
  101.0 0.1 collective-permute-done.16.rest_5_
  101.1 0.6 join_pieces.6
  101.8 0.1 collective-permute-start.19
  101.9 1.3 collective-permute-start.18
  103.2 3.3 %collective-permute-start.9 = (bf16[2,4,64,128]{3,2,1,0:T(8,128)(2,1)S(1)}, bf16[2,4,64,128]{3,2,1,0:T(8,128)(2,1)S(1)}, u32[]{:S(2)}, u32[]{:S(2)}) collective-permute-start(bf16[2,4,64,128]{3,2,1,0:T(8,128)(2,1)S(1)} %get-tuple-element.81), channel_id=1, source_target_pairs={{0,4},{4,8},{8,12},{12,0},{1,5},{5,9},{9,13},{13,1},{2,6},{6,10},{... | collective-permute-start | bytes 393224 | tf_op jit(solution)/shard_map/ppermute | solution.py:395
  106.5 1.5 %collective-permute-start.10 = (bf16[2,4,64,128]{3,2,1,0:T(8,128)(2,1)S(1)}, bf16[2,4,64,128]{3,2,1,0:T(8,128)(2,1)S(1)}, u32[]{:S(2)}, u32[]{:S(2)}) collective-permute-start(bf16[2,4,64,128]{3,2,1,0:T(8,128)(2,1)S(1)} %get-tuple-element.82), channel_id=1, source_target_pairs={{0,8},{4,12},{8,0},{12,4},{1,9},{5,13},{9,1},{13,5},{2,10},{6,14},... | collective-permute-start | bytes 393224 | tf_op jit(solution)/shard_map/ppermute | solution.py:395
  108.0 0.8 collective-permute-start.11
  108.8 3.5 %correlate_tiles.5 = (f32[2,8,5,256,256]{4,3,2,1,0:T(8,128)}, f32[8,128]{1,0:T(8,128)S(1)}) custom-call(s32[11]{0:T(128)S(1)} %pad_add_fusion.rest_7_.rest_3_.rest_6_.table_ref.rest_2_, bf16[2,4,2,4,64,128]{5,4,3,2,1,0:T(8,128)(2,1)S(1)} %get-tuple-element.92.rest_0_, ...), custom_call_target="tpu_custom_call", output_to_operand_aliasing={{0}: (4, {})} | custom-call | tf_op jit(solution)/shard_map/correlate_tiles/pallas_call | solution.py:361
  112.4 4.6 %collective-permute-done.10.rest_2_ = bf16[2,4,64,128]{3,2,1,0:T(8,128)(2,1)S(1)} collective-permute-done((bf16[2,4,64,128]{3,2,1,0:T(8,128)(2,1)S(1)}, bf16[2,4,64,128]{3,2,1,0:T(8,128)(2,1)S(1)}, u32[]{:S(2)}, u32[]{:S(2)}) %collective-permute-start.10) | collective-permute-done | bytes 131104 | tf_op jit(solution)/shard_map/ppermute | solution.py:395
  117.0 0.6 join_pieces.7
  117.6 0.1 collective-permute-start.21
  117.7 0.6 collective-permute-start.20
  118.3 0.2 collective-permute-start.22
  118.5 1.9 %collective-permute-done.21.rest_1_ = bf16[2,4,2,4,64,128]{5,4,3,2,1,0:T(8,128)(2,1)S(1)} collective-permute-done((bf16[2,4,2,4,64,128]{5,4,3,2,1,0:T(8,128)(2,1)S(1)}, bf16[2,4,2,4,64,128]{5,4,3,2,1,0:T(8,128)(2,1)S(1)}, u32[]{:S(2)}, u32[]{:S(2)}) %collective-permute-start.21) | collective-permute-done | bytes 1048608 | tf_op jit(solution)/shard_map/ppermute | solution.py:402
  120.4 3.5 %correlate_tiles.6 = (f32[2,8,5,256,256]{4,3,2,1,0:T(8,128)}, f32[8,128]{1,0:T(8,128)S(1)}) custom-call(s32[11]{0:T(128)S(1)} %pad_add_fusion.rest_7_.rest_3_.rest_6_.table_ref.rest_2_, bf16[2,4,2,4,64,128]{5,4,3,2,1,0:T(8,128)(2,1)S(1)} %get-tuple-element.96.rest_0_, ...), custom_call_target="tpu_custom_call", output_to_operand_aliasing={{0}: (4, {})} | custom-call | tf_op jit(solution)/shard_map/correlate_tiles/pallas_call | solution.py:361
  123.9 8.2 %collective-permute-done.20 = bf16[4,2,4,64,128]{4,3,2,1,0:T(8,128)(2,1)S(1)} collective-permute-done((bf16[4,2,4,64,128]{4,3,2,1,0:T(8,128)(2,1)S(1)}, bf16[4,2,4,64,128]{4,3,2,1,0:T(8,128)(2,1)S(1)}, u32[]{:S(2)}, u32[]{:S(2)}) %collective-permute-start.20) | collective-permute-done | bytes 524320 | tf_op jit(solution)/shard_map/ppermute | solution.py:402
  132.1 1.9 %collective-permute-done.23.rest_3_ = bf16[1,4,2,4,64,128]{5,4,3,2,1,0:T(8,128)(2,1)S(1)} collective-permute-done((bf16[1,4,2,4,64,128]{5,4,3,2,1,0:T(8,128)(2,1)S(1)}, bf16[1,4,2,4,64,128]{5,4,3,2,1,0:T(8,128)(2,1)S(1)}, u32[]{:S(2)}, u32[]{:S(2)}) %collective-permute-start.23) | collective-permute-done | bytes 524320 | tf_op jit(solution)/shard_map/ppermute | solution.py:402
  134.0 4.1 %correlate_tiles.7 = (f32[2,8,5,256,256]{4,3,2,1,0:T(8,128)}, f32[8,128]{1,0:T(8,128)}) custom-call(s32[11]{0:T(128)S(1)} %pad_add_fusion.rest_7_.rest_3_.rest_6_.table_ref.rest_2_, bf16[1,4,2,4,64,128]{5,4,3,2,1,0:T(8,128)(2,1)S(1)} %bitcast.5, bf16[1,4,2,4,64,128]{5,4,3,2,1,0:T(8,128)(2,1)S(1)} %bitcast.7, ...), custom_call_target="tpu_custom_call", output_to_operand_aliasing={{0}: (6, {})} | custom-call | tf_op jit(solution)/shard_map/correlate_tiles/pallas_call | solution.py:361
  (18 shorter events, 0.1 us)
Async XLA Ops:
  0.1 1.6 %copy-start = (bf16[2,2048,256]{2,1,0:T(8,128)(2,1)S(1)}, bf16[2,2048,256]{2,1,0:T(8,128)(2,1)}, u32[]{:S(2)}) copy-start(bf16[2,2048,256]{2,1,0:T(8,128)(2,1)} %v_ref.1) | copy-start | bytes 6291460
  4.4 19.2 %collective-permute-start = (bf16[2,64,2048]{2,1,0:T(8,128)(2,1)}, bf16[2,64,2048]{2,1,0:T(8,128)(2,1)S(1)}, u32[]{:S(2)}, u32[]{:S(2)}) collective-permute-start(bf16[2,64,2048]{2,1,0:T(8,128)(2,1)} %get-tuple-element.55), channel_id=1, source_target_pairs={{0,4},{4,8},{8,12},{12,0},{1,5},{5,9},{9,13},{13,1},{2,6},{6,10},{... | collective-permute-start | bytes 1572872 | tf_op jit(solution)/shard_map/ppermute | solution.py:395
  7.4 36.8 %collective-permute-start.1 = (bf16[2,64,2048]{2,1,0:T(8,128)(2,1)S(1)}, bf16[2,64,2048]{2,1,0:T(8,128)(2,1)S(1)}, u32[]{:S(2)}, u32[]{:S(2)}) collective-permute-start(bf16[2,64,2048]{2,1,0:T(8,128)(2,1)S(1)} %get-tuple-element.56), channel_id=1, source_target_pairs={{0,8},{4,12},{8,0},{12,4},{1,9},{5,13},{9,1},{13,5},{2,10},{6,14},... | collective-permute-start | bytes 1572872 | tf_op jit(solution)/shard_map/ppermute | solution.py:395
  10.0 34.2 %collective-permute-start.2 = (bf16[2,64,2048]{2,1,0:T(8,128)(2,1)S(1)}, bf16[2,64,2048]{2,1,0:T(8,128)(2,1)S(1)}, u32[]{:S(2)}, u32[]{:S(2)}) collective-permute-start(bf16[2,64,2048]{2,1,0:T(8,128)(2,1)S(1)} %get-tuple-element.57), channel_id=1, source_target_pairs={{0,12},{4,0},{8,4},{12,8},{1,13},{5,1},{9,5},{13,9},{2,14},{6,2},{... | collective-permute-start | bytes 1572872 | tf_op jit(solution)/shard_map/ppermute | solution.py:395
  18.1 1.1 copy-start.1
  19.2 1.1 copy-start.2
  20.4 0.7 copy-start.3
  21.1 0.7 copy-start.4
  49.0 17.6 %collective-permute-start.12 = (bf16[2,4,64,128]{3,2,1,0:T(8,128)(2,1)S(1)}, bf16[2,4,64,128]{3,2,1,0:T(8,128)(2,1)S(1)}, u32[]{:S(2)}, u32[]{:S(2)}) collective-permute-start(bf16[2,4,64,128]{3,2,1,0:T(8,128)(2,1)S(1)} %get-tuple-element.85), channel_id=1, source_target_pairs={{0,4},{4,8},{8,12},{12,0},{1,5},{5,9},{9,13},{13,1},{2,6},{6,10},{... | collective-permute-start | bytes 393224 | tf_op jit(solution)/shard_map/ppermute | solution.py:395
  60.7 9.7 %collective-permute-start.13 = (bf16[2,4,64,128]{3,2,1,0:T(8,128)(2,1)S(1)}, bf16[2,4,64,128]{3,2,1,0:T(8,128)(2,1)S(1)}, u32[]{:S(2)}, u32[]{:S(2)}) collective-permute-start(bf16[2,4,64,128]{3,2,1,0:T(8,128)(2,1)S(1)} %get-tuple-element.86), channel_id=1, source_target_pairs={{0,8},{4,12},{8,0},{12,4},{1,9},{5,13},{9,1},{13,5},{2,10},{6,14},... | collective-permute-start | bytes 393224 | tf_op jit(solution)/shard_map/ppermute | solution.py:395
  62.3 8.1 %collective-permute-start.14 = (bf16[2,4,64,128]{3,2,1,0:T(8,128)(2,1)S(1)}, bf16[2,4,64,128]{3,2,1,0:T(8,128)(2,1)S(1)}, u32[]{:S(2)}, u32[]{:S(2)}) collective-permute-start(bf16[2,4,64,128]{3,2,1,0:T(8,128)(2,1)S(1)} %get-tuple-element.87), channel_id=1, source_target_pairs={{0,12},{4,0},{8,4},{12,8},{1,13},{5,1},{9,5},{13,9},{2,14},{6,2},{... | collective-permute-start | bytes 393224 | tf_op jit(solution)/shard_map/ppermute | solution.py:395
  71.0 15.1 %collective-permute-start.15 = (bf16[4,2,4,64,128]{4,3,2,1,0:T(8,128)(2,1)S(1)}, bf16[4,2,4,64,128]{4,3,2,1,0:T(8,128)(2,1)S(1)}, u32[]{:S(2)}, u32[]{:S(2)}) collective-permute-start(bf16[4,2,4,64,128]{4,3,2,1,0:T(8,128)(2,1)S(1)} %join_pieces.4.rest_4_), channel_id=1, source_target_pairs={{0,2},{1,3},{2,0},{3,1},{4,6},{5,7},{6,4},{7,5},{8,10},{9,11},{10,... | collective-permute-start | bytes 1572872 | tf_op jit(solution)/shard_map/ppermute | solution.py:402
  72.6 9.3 %collective-permute-start.3 = (bf16[2,4,64,128]{3,2,1,0:T(8,128)(2,1)S(1)}, bf16[2,4,64,128]{3,2,1,0:T(8,128)(2,1)S(1)}, u32[]{:S(2)}, u32[]{:S(2)}) collective-permute-start(bf16[2,4,64,128]{3,2,1,0:T(8,128)(2,1)S(1)} %get-tuple-element.73), channel_id=1, source_target_pairs={{0,4},{4,8},{8,12},{12,0},{1,5},{5,9},{9,13},{13,1},{2,6},{6,10},{... | collective-permute-start | bytes 393224 | tf_op jit(solution)/shard_map/ppermute | solution.py:395
  75.8 10.1 %collective-permute-start.4 = (bf16[2,4,64,128]{3,2,1,0:T(8,128)(2,1)S(1)}, bf16[2,4,64,128]{3,2,1,0:T(8,128)(2,1)S(1)}, u32[]{:S(2)}, u32[]{:S(2)}) collective-permute-start(bf16[2,4,64,128]{3,2,1,0:T(8,128)(2,1)S(1)} %get-tuple-element.74), channel_id=1, source_target_pairs={{0,8},{4,12},{8,0},{12,4},{1,9},{5,13},{9,1},{13,5},{2,10},{6,14},... | collective-permute-start | bytes 393224 | tf_op jit(solution)/shard_map/ppermute | solution.py:395
  77.9 8.1 %collective-permute-start.5 = (bf16[2,4,64,128]{3,2,1,0:T(8,128)(2,1)S(1)}, bf16[2,4,64,128]{3,2,1,0:T(8,128)(2,1)S(1)}, u32[]{:S(2)}, u32[]{:S(2)}) collective-permute-start(bf16[2,4,64,128]{3,2,1,0:T(8,128)(2,1)S(1)} %get-tuple-element.75), channel_id=1, source_target_pairs={{0,12},{4,0},{8,4},{12,8},{1,13},{5,1},{9,5},{13,9},{2,14},{6,2},{... | collective-permute-start | bytes 393224 | tf_op jit(solution)/shard_map/ppermute | solution.py:395
  86.7 6.2 %collective-permute-start.17 = (bf16[2,4,2,4,64,128]{5,4,3,2,1,0:T(8,128)(2,1)S(1)}, bf16[2,4,2,4,64,128]{5,4,3,2,1,0:T(8,128)(2,1)S(1)}, u32[]{:S(2)}, u32[]{:S(2)}) collective-permute-start(bf16[2,4,2,4,64,128]{5,4,3,2,1,0:T(8,128)(2,1)S(1)} %get-tuple-element.89.rest_0_), channel_id=1, source_target_pairs={{0,1},{1,0},{2,3},{3,2},{4,5},{5,4},{6,7},{7,6},{8,9},{9,8},{10,11... | collective-permute-start | bytes 3145736 | tf_op jit(solution)/shard_map/ppermute | solution.py:402
  86.8 14.3 %collective-permute-start.16 = (bf16[4,2,4,64,128]{4,3,2,1,0:T(8,128)(2,1)S(1)}, bf16[4,2,4,64,128]{4,3,2,1,0:T(8,128)(2,1)S(1)}, u32[]{:S(2)}, u32[]{:S(2)}) collective-permute-start(bf16[4,2,4,64,128]{4,3,2,1,0:T(8,128)(2,1)S(1)} %get-tuple-element.88.rest_4_), channel_id=1, source_target_pairs={{0,2},{1,3},{2,0},{3,1},{4,6},{5,7},{6,4},{7,5},{8,10},{9,11},{10,... | collective-permute-start | bytes 1572872 | tf_op jit(solution)/shard_map/ppermute | solution.py:402
  87.4 9.1 %collective-permute-start.6 = (bf16[2,4,64,128]{3,2,1,0:T(8,128)(2,1)S(1)}, bf16[2,4,64,128]{3,2,1,0:T(8,128)(2,1)S(1)}, u32[]{:S(2)}, u32[]{:S(2)}) collective-permute-start(bf16[2,4,64,128]{3,2,1,0:T(8,128)(2,1)S(1)} %get-tuple-element.77), channel_id=1, source_target_pairs={{0,4},{4,8},{8,12},{12,0},{1,5},{5,9},{9,13},{13,1},{2,6},{6,10},{... | collective-permute-start | bytes 393224 | tf_op jit(solution)/shard_map/ppermute | solution.py:395
  90.5 10.5 %collective-permute-start.7 = (bf16[2,4,64,128]{3,2,1,0:T(8,128)(2,1)S(1)}, bf16[2,4,64,128]{3,2,1,0:T(8,128)(2,1)S(1)}, u32[]{:S(2)}, u32[]{:S(2)}) collective-permute-start(bf16[2,4,64,128]{3,2,1,0:T(8,128)(2,1)S(1)} %get-tuple-element.78), channel_id=1, source_target_pairs={{0,8},{4,12},{8,0},{12,4},{1,9},{5,13},{9,1},{13,5},{2,10},{6,14},... | collective-permute-start | bytes 393224 | tf_op jit(solution)/shard_map/ppermute | solution.py:395
  92.0 9.0 %collective-permute-start.8 = (bf16[2,4,64,128]{3,2,1,0:T(8,128)(2,1)S(1)}, bf16[2,4,64,128]{3,2,1,0:T(8,128)(2,1)S(1)}, u32[]{:S(2)}, u32[]{:S(2)}) collective-permute-start(bf16[2,4,64,128]{3,2,1,0:T(8,128)(2,1)S(1)} %get-tuple-element.79), channel_id=1, source_target_pairs={{0,12},{4,0},{8,4},{12,8},{1,13},{5,1},{9,5},{13,9},{2,14},{6,2},{... | collective-permute-start | bytes 393224 | tf_op jit(solution)/shard_map/ppermute | solution.py:395
  101.8 7.1 %collective-permute-start.19 = (bf16[2,4,2,4,64,128]{5,4,3,2,1,0:T(8,128)(2,1)S(1)}, bf16[2,4,2,4,64,128]{5,4,3,2,1,0:T(8,128)(2,1)S(1)}, u32[]{:S(2)}, u32[]{:S(2)}) collective-permute-start(bf16[2,4,2,4,64,128]{5,4,3,2,1,0:T(8,128)(2,1)S(1)} %get-tuple-element.92.rest_0_), channel_id=1, source_target_pairs={{0,1},{1,0},{2,3},{3,2},{4,5},{5,4},{6,7},{7,6},{8,9},{9,8},{10,11... | collective-permute-start | bytes 3145736 | tf_op jit(solution)/shard_map/ppermute | solution.py:402
  101.9 15.1 %collective-permute-start.18 = (bf16[4,2,4,64,128]{4,3,2,1,0:T(8,128)(2,1)S(1)}, bf16[4,2,4,64,128]{4,3,2,1,0:T(8,128)(2,1)S(1)}, u32[]{:S(2)}, u32[]{:S(2)}) collective-permute-start(bf16[4,2,4,64,128]{4,3,2,1,0:T(8,128)(2,1)S(1)} %get-tuple-element.91.rest_4_), channel_id=1, source_target_pairs={{0,2},{1,3},{2,0},{3,1},{4,6},{5,7},{6,4},{7,5},{8,10},{9,11},{10,... | collective-permute-start | bytes 1572872 | tf_op jit(solution)/shard_map/ppermute | solution.py:402
  103.2 9.2 %collective-permute-start.9 = (bf16[2,4,64,128]{3,2,1,0:T(8,128)(2,1)S(1)}, bf16[2,4,64,128]{3,2,1,0:T(8,128)(2,1)S(1)}, u32[]{:S(2)}, u32[]{:S(2)}) collective-permute-start(bf16[2,4,64,128]{3,2,1,0:T(8,128)(2,1)S(1)} %get-tuple-element.81), channel_id=1, source_target_pairs={{0,4},{4,8},{8,12},{12,0},{1,5},{5,9},{9,13},{13,1},{2,6},{6,10},{... | collective-permute-start | bytes 393224 | tf_op jit(solution)/shard_map/ppermute | solution.py:395
  106.5 10.5 %collective-permute-start.10 = (bf16[2,4,64,128]{3,2,1,0:T(8,128)(2,1)S(1)}, bf16[2,4,64,128]{3,2,1,0:T(8,128)(2,1)S(1)}, u32[]{:S(2)}, u32[]{:S(2)}) collective-permute-start(bf16[2,4,64,128]{3,2,1,0:T(8,128)(2,1)S(1)} %get-tuple-element.82), channel_id=1, source_target_pairs={{0,8},{4,12},{8,0},{12,4},{1,9},{5,13},{9,1},{13,5},{2,10},{6,14},... | collective-permute-start | bytes 393224 | tf_op jit(solution)/shard_map/ppermute | solution.py:395
  108.0 9.0 %collective-permute-start.11 = (bf16[2,4,64,128]{3,2,1,0:T(8,128)(2,1)S(1)}, bf16[2,4,64,128]{3,2,1,0:T(8,128)(2,1)S(1)}, u32[]{:S(2)}, u32[]{:S(2)}) collective-permute-start(bf16[2,4,64,128]{3,2,1,0:T(8,128)(2,1)S(1)} %get-tuple-element.83), channel_id=1, source_target_pairs={{0,12},{4,0},{8,4},{12,8},{1,13},{5,1},{9,5},{13,9},{2,14},{6,2},{... | collective-permute-start | bytes 393224 | tf_op jit(solution)/shard_map/ppermute | solution.py:395
  117.6 2.7 %collective-permute-start.21 = (bf16[2,4,2,4,64,128]{5,4,3,2,1,0:T(8,128)(2,1)S(1)}, bf16[2,4,2,4,64,128]{5,4,3,2,1,0:T(8,128)(2,1)S(1)}, u32[]{:S(2)}, u32[]{:S(2)}) collective-permute-start(bf16[2,4,2,4,64,128]{5,4,3,2,1,0:T(8,128)(2,1)S(1)} %get-tuple-element.96.rest_0_), channel_id=1, source_target_pairs={{0,1},{1,0},{2,3},{3,2},{4,5},{5,4},{6,7},{7,6},{8,9},{9,8},{10,11... | collective-permute-start | bytes 3145736 | tf_op jit(solution)/shard_map/ppermute | solution.py:402
  117.7 14.3 %collective-permute-start.20 = (bf16[4,2,4,64,128]{4,3,2,1,0:T(8,128)(2,1)S(1)}, bf16[4,2,4,64,128]{4,3,2,1,0:T(8,128)(2,1)S(1)}, u32[]{:S(2)}, u32[]{:S(2)}) collective-permute-start(bf16[4,2,4,64,128]{4,3,2,1,0:T(8,128)(2,1)S(1)} %get-tuple-element.95), channel_id=1, source_target_pairs={{0,2},{1,3},{2,0},{3,1},{4,6},{5,7},{6,4},{7,5},{8,10},{9,11},{10,... | collective-permute-start | bytes 1572872 | tf_op jit(solution)/shard_map/ppermute | solution.py:402
  118.3 13.7 %collective-permute-start.22 = (bf16[1,4,2,4,64,128]{5,4,3,2,1,0:T(8,128)(2,1)S(1)}, bf16[1,4,2,4,64,128]{5,4,3,2,1,0:T(8,128)(2,1)S(1)}, u32[]{:S(2)}, u32[]{:S(2)}) collective-permute-start(bf16[1,4,2,4,64,128]{5,4,3,2,1,0:T(8,128)(2,1)S(1)} %bitcast.4), channel_id=1, source_target_pairs={{0,1},{1,0},{2,3},{3,2},{4,5},{5,4},{6,7},{7,6},{8,9},{9,8},{10,11... | collective-permute-start | bytes 1572872 | tf_op jit(solution)/shard_map/ppermute | solution.py:402
  132.1 1.9 %collective-permute-start.23 = (bf16[1,4,2,4,64,128]{5,4,3,2,1,0:T(8,128)(2,1)S(1)}, bf16[1,4,2,4,64,128]{5,4,3,2,1,0:T(8,128)(2,1)S(1)}, u32[]{:S(2)}, u32[]{:S(2)}) collective-permute-start(bf16[1,4,2,4,64,128]{5,4,3,2,1,0:T(8,128)(2,1)S(1)} %bitcast.6), channel_id=1, source_target_pairs={{0,1},{1,0},{2,3},{3,2},{4,5},{5,4},{6,7},{7,6},{8,9},{9,8},{10,11... | collective-permute-start | bytes 1572872 | tf_op jit(solution)/shard_map/ppermute | solution.py:402

commit v7 on v6

--- a/solution.py
+++ b/solution.py
@@ -164,9 +164,9 @@
     group = spectra * rows
     depth = split.shape[1] // 2
 
-    @pl.loop(0, radix // 2)
-    def _(pair):
-        at = pl.ds(pl.multiple_of(pair * 2 * group, 2 * group), 2 * group)
+    @pl.loop(0, radix // 4)
+    def _(four):
+        at = pl.ds(pl.multiple_of(four * 4 * group, 4 * group), 4 * group)
         high = split[at, :depth]
         line = jnp.concatenate([high, split[at, depth:], high], axis=1)
         prod[at, :] = jnp.dot(line, g_ref[...], preferred_element_type=jnp.float32)
@@ -470,6 +470,7 @@
         and chan_count % MXU == 0
         and radix & (radix - 1) == 0
         and radix % dests == 0
+        and radix % 4 == 0
         and radix <= 8
         and blocks & (blocks - 1) == 0
         and blocks > 2

time: 140 us -> 140 us (level)
  no operation moved by 1% of the time
where the time goes in v7:
time: 140 us; the launch traced here: 138 us
  waiting for transfers between devices  53.8 us (38%)
  starting transfers between devices  42.4 us (30%)
  Pallas kernels  27.6 us (20%)
  local copies, waits for them, and re-layouts  9.17 us (7%)
  other arithmetic  4.61 us (3%)
    ppermute x15, waiting for transfers between devices, spread(): lax.ppermute(pieces[d], 'ft', [(i, (i + d) % count) for i in range(count)])  41.7 us
    ppermute x15, starting transfers between devices, spread(): lax.ppermute(pieces[d], 'ft', [(i, (i + d) % count) for i in range(count)])  37.9 us
    pallas_call x4, Pallas kernels, correlate(): pl.pallas_call(functools.partial(correlate_kernel, order, chunks, 1.0 / (...  14.7 us
    ppermute x9, waiting for transfers between devices, exchange(): return lax.ppermute(own, 'bl', [(i, i ^ bit) for i in range(count)])  12.1 us
    pallas_call x2, Pallas kernels, transform_cut(): pl.pallas_call(kernel, grid_spec=pltpu.PrefetchScalarGridSpec(num_scalar_...  7.59 us
    unnamed x10, local copies, waits for them, and re-layouts  5.25 us
    ppermute x9, starting transfers between devices, exchange(): return lax.ppermute(own, 'bl', [(i, i ^ bit) for i in range(count)])  4.47 us
    reshape x2, local copies, waits for them, and re-layouts, per_device_kernels(): coef_table = coefs.reshape(taps, MXU, radix).transpose(0, 2, 1)  3.92 us
  transfers between devices with their start and end apart: 24, of which 11 were waited for; matrix products, arithmetic and copies ran while one was open for 6% of the time, Pallas kernels for 10%

profile of v7, /device:TPU:0, one launch (start us, length us, event | category | flops | bytes accessed | tf_op | source)
XLA Modules:
  0.0 137.9 jit_solution(1588734862013328312)
XLA Ops:
  0.0 0.1 pad_add_fusion.1.place_ref
  0.1 1.6 %copy-done = bf16[2,2048,256]{2,1,0:T(8,128)(2,1)S(1)} copy-done((bf16[2,2048,256]{2,1,0:T(8,128)(2,1)S(1)}, bf16[2,2048,256]{2,1,0:T(8,128)(2,1)}, u32[]{:S(2)}) %copy-start) | copy-done | bytes 2097176
  1.7 2.7 %pack_inputs.1 = (bf16[2,64,2048]{2,1,0:T(8,128)(2,1)S(1)}, bf16[2,64,2048]{2,1,0:T(8,128)(2,1)}, bf16[2,64,2048]{2,1,0:T(8,128)(2,1)S(1)}, bf16[2,64,2048]{2,1,0:T(8,128)(2,1)S(1)}) custom-call(s32[8]{0:T(128)S(1)} %pad_add_fusion.1.place_ref, bf16[2,2048,256]{2,1,0:T(8,128)(2,1)S(1)} %copy-done), custom_call_target="tpu_custom_call" | custom-call | tf_op jit(solution)/shard_map/pack_inputs/pallas_call | solution.py:97
  4.4 3.0 %collective-permute-start = (bf16[2,64,2048]{2,1,0:T(8,128)(2,1)}, bf16[2,64,2048]{2,1,0:T(8,128)(2,1)S(1)}, u32[]{:S(2)}, u32[]{:S(2)}) collective-permute-start(bf16[2,64,2048]{2,1,0:T(8,128)(2,1)} %get-tuple-element.55), channel_id=1, source_target_pairs={{0,4},{4,8},{8,12},{12,0},{1,5},{5,9},{9,13},{13,1},{2,6},{6,10},{... | collective-permute-start | bytes 1572872 | tf_op jit(solution)/shard_map/ppermute | solution.py:395
  7.4 2.6 %collective-permute-start.1 = (bf16[2,64,2048]{2,1,0:T(8,128)(2,1)S(1)}, bf16[2,64,2048]{2,1,0:T(8,128)(2,1)S(1)}, u32[]{:S(2)}, u32[]{:S(2)}) collective-permute-start(bf16[2,64,2048]{2,1,0:T(8,128)(2,1)S(1)} %get-tuple-element.56), channel_id=1, source_target_pairs={{0,8},{4,12},{8,0},{12,4},{1,9},{5,13},{9,1},{13,5},{2,10},{6,14},... | collective-permute-start | bytes 1572872 | tf_op jit(solution)/shard_map/ppermute | solution.py:395
  10.0 1.3 collective-permute-start.2
  11.3 0.8 fusion.1
  12.1 2.4 %reshape.11 = f32[8,256,8]{2,1,0:T(8,128)} reshape(f32[8,2048]{1,0:T(8,128)} %param.16) | data formatting | bytes 131072 | tf_op jit(solution)/shard_map/reshape | solution.py:489
  14.5 1.5 %copy.20 = f32[8,256,8]{1,2,0:T(8,128)S(1)} copy(f32[8,256,8]{2,1,0:T(8,128)} %reshape.11) | data formatting | bytes 131072 | tf_op jit(solution)/shard_map/reshape | solution.py:489
  16.0 0.7 broadcast_compare_fusion
  16.7 0.6 reduce_sum.69
  17.3 0.8 select_reduce_fusion.3
  18.1 1.1 copy-done.1
  19.2 1.1 copy-done.2
  20.4 0.7 copy-done.3
  21.1 0.7 copy-done.4
  21.7 0.1 stage_tables.1
  21.9 0.8 multiply_reduce_fusion
  22.7 0.2 select_reduce_fusion.1
  22.8 0.7 pad_add_fusion.rest_7_.rest_3_.rest_6_.table_ref.rest_2_
  23.6 0.0 collective-permute-done.rest_1_
  23.6 20.6 %collective-permute-done.1.rest_2_ = bf16[2,64,2048]{2,1,0:T(8,128)(2,1)S(1)} collective-permute-done((bf16[2,64,2048]{2,1,0:T(8,128)(2,1)S(1)}, bf16[2,64,2048]{2,1,0:T(8,128)(2,1)S(1)}, u32[]{:S(2)}, u32[]{:S(2)}) %collective-permute-start.1) | collective-permute-done | bytes 524320 | tf_op jit(solution)/shard_map/ppermute | solution.py:395
  44.2 4.5 %filter_transform.1 = (bf16[2,4,64,128]{3,2,1,0:T(8,128)(2,1)S(1)}, bf16[2,4,64,128]{3,2,1,0:T(8,128)(2,1)S(1)}, bf16[2,4,64,128]{3,2,1,0:T(8,128)(2,1)S(1)}, bf...) custom-call(s32[8]{0:T(128)S(1)} %pad_add_fusion.1.place_ref, ...), custom_call_target="tpu_custom_call" | custom-call | flops 1610612736 | bytes 6291456 | tf_op jit(solution)/shard_map/filter_transform/pallas_call | solution.py:226
  48.7 11.8 %collective-permute-start.12 = (bf16[2,4,64,128]{3,2,1,0:T(8,128)(2,1)S(1)}, bf16[2,4,64,128]{3,2,1,0:T(8,128)(2,1)S(1)}, u32[]{:S(2)}, u32[]{:S(2)}) collective-permute-start(bf16[2,4,64,128]{3,2,1,0:T(8,128)(2,1)S(1)} %get-tuple-element.85), channel_id=1, source_target_pairs={{0,4},{4,8},{8,12},{12,0},{1,5},{5,9},{9,13},{13,1},{2,6},{6,10},{... | collective-permute-start | bytes 393224 | tf_op jit(solution)/shard_map/ppermute | solution.py:395
  60.4 1.6 %collective-permute-start.13 = (bf16[2,4,64,128]{3,2,1,0:T(8,128)(2,1)S(1)}, bf16[2,4,64,128]{3,2,1,0:T(8,128)(2,1)S(1)}, u32[]{:S(2)}, u32[]{:S(2)}) collective-permute-start(bf16[2,4,64,128]{3,2,1,0:T(8,128)(2,1)S(1)} %get-tuple-element.86), channel_id=1, source_target_pairs={{0,8},{4,12},{8,0},{12,4},{1,9},{5,13},{9,1},{13,5},{2,10},{6,14},... | collective-permute-start | bytes 393224 | tf_op jit(solution)/shard_map/ppermute | solution.py:395
  62.0 0.8 collective-permute-start.14
  62.8 3.1 %transform_rest.1 = (bf16[2,4,64,128]{3,2,1,0:T(8,128)(2,1)S(1)}, bf16[2,4,64,128]{3,2,1,0:T(8,128)(2,1)S(1)}, bf16[2,4,64,128]{3,2,1,0:T(8,128)(2,1)S(1)}, bf16...) custom-call(s32[8]{0:T(128)S(1)} %pad_add_fusion.1.place_ref, ...), custom_call_target="tpu_custom_call" | custom-call | flops 1610612736 | bytes 6291456 | tf_op jit(solution)/shard_map/transform_rest/pallas_call | solution.py:226
  66.0 0.0 collective-permute-done.12.rest_1_
  66.0 4.1 %collective-permute-done.13.rest_2_ = bf16[2,4,64,128]{3,2,1,0:T(8,128)(2,1)S(1)} collective-permute-done((bf16[2,4,64,128]{3,2,1,0:T(8,128)(2,1)S(1)}, bf16[2,4,64,128]{3,2,1,0:T(8,128)(2,1)S(1)}, u32[]{:S(2)}, u32[]{:S(2)}) %collective-permute-start.13) | collective-permute-done | bytes 131104 | tf_op jit(solution)/shard_map/ppermute | solution.py:395
  70.1 0.0 collective-permute-done.14.rest_3_
  70.1 0.6 join_pieces.4.rest_4_
  70.7 1.6 %collective-permute-start.15 = (bf16[4,2,4,64,128]{4,3,2,1,0:T(8,128)(2,1)S(1)}, bf16[4,2,4,64,128]{4,3,2,1,0:T(8,128)(2,1)S(1)}, u32[]{:S(2)}, u32[]{:S(2)}) collective-permute-start(bf16[4,2,4,64,128]{4,3,2,1,0:T(8,128)(2,1)S(1)} %join_pieces.4.rest_4_), channel_id=1, source_target_pairs={{0,2},{1,3},{2,0},{3,1},{4,6},{5,7},{6,4},{7,5},{8,10},{9,11},{10,... | collective-permute-start | bytes 1572872 | tf_op jit(solution)/shard_map/ppermute | solution.py:402
  72.2 3.3 %collective-permute-start.3 = (bf16[2,4,64,128]{3,2,1,0:T(8,128)(2,1)S(1)}, bf16[2,4,64,128]{3,2,1,0:T(8,128)(2,1)S(1)}, u32[]{:S(2)}, u32[]{:S(2)}) collective-permute-start(bf16[2,4,64,128]{3,2,1,0:T(8,128)(2,1)S(1)} %get-tuple-element.73), channel_id=1, source_target_pairs={{0,4},{4,8},{8,12},{12,0},{1,5},{5,9},{9,13},{13,1},{2,6},{6,10},{... | collective-permute-start | bytes 393224 | tf_op jit(solution)/shard_map/ppermute | solution.py:395
  75.5 2.1 %collective-permute-start.4 = (bf16[2,4,64,128]{3,2,1,0:T(8,128)(2,1)S(1)}, bf16[2,4,64,128]{3,2,1,0:T(8,128)(2,1)S(1)}, u32[]{:S(2)}, u32[]{:S(2)}) collective-permute-start(bf16[2,4,64,128]{3,2,1,0:T(8,128)(2,1)S(1)} %get-tuple-element.74), channel_id=1, source_target_pairs={{0,8},{4,12},{8,0},{12,4},{1,9},{5,13},{9,1},{13,5},{2,10},{6,14},... | collective-permute-start | bytes 393224 | tf_op jit(solution)/shard_map/ppermute | solution.py:395
  77.6 0.3 collective-permute-start.5
  77.9 3.6 %collective-permute-done.3.rest_1_ = bf16[2,4,64,128]{3,2,1,0:T(8,128)(2,1)S(1)} collective-permute-done((bf16[2,4,64,128]{3,2,1,0:T(8,128)(2,1)S(1)}, bf16[2,4,64,128]{3,2,1,0:T(8,128)(2,1)S(1)}, u32[]{:S(2)}, u32[]{:S(2)}) %collective-permute-start.3) | collective-permute-done | bytes 131104 | tf_op jit(solution)/shard_map/ppermute | solution.py:395
  81.5 4.1 %collective-permute-done.4.rest_2_ = bf16[2,4,64,128]{3,2,1,0:T(8,128)(2,1)S(1)} collective-permute-done((bf16[2,4,64,128]{3,2,1,0:T(8,128)(2,1)S(1)}, bf16[2,4,64,128]{3,2,1,0:T(8,128)(2,1)S(1)}, u32[]{:S(2)}, u32[]{:S(2)}) %collective-permute-start.4) | collective-permute-done | bytes 131104 | tf_op jit(solution)/shard_map/ppermute | solution.py:395
  85.6 0.1 collective-permute-done.5.rest_3_
  85.7 0.6 join_pieces.5
  86.4 0.1 collective-permute-start.17
  86.5 0.6 collective-permute-start.16
  87.1 3.1 %collective-permute-start.6 = (bf16[2,4,64,128]{3,2,1,0:T(8,128)(2,1)S(1)}, bf16[2,4,64,128]{3,2,1,0:T(8,128)(2,1)S(1)}, u32[]{:S(2)}, u32[]{:S(2)}) collective-permute-start(bf16[2,4,64,128]{3,2,1,0:T(8,128)(2,1)S(1)} %get-tuple-element.77), channel_id=1, source_target_pairs={{0,4},{4,8},{8,12},{12,0},{1,5},{5,9},{9,13},{13,1},{2,6},{6,10},{... | collective-permute-start | bytes 393224 | tf_op jit(solution)/shard_map/ppermute | solution.py:395
  90.2 1.5 %collective-permute-start.7 = (bf16[2,4,64,128]{3,2,1,0:T(8,128)(2,1)S(1)}, bf16[2,4,64,128]{3,2,1,0:T(8,128)(2,1)S(1)}, u32[]{:S(2)}, u32[]{:S(2)}) collective-permute-start(bf16[2,4,64,128]{3,2,1,0:T(8,128)(2,1)S(1)} %get-tuple-element.78), channel_id=1, source_target_pairs={{0,8},{4,12},{8,0},{12,4},{1,9},{5,13},{9,1},{13,5},{2,10},{6,14},... | collective-permute-start | bytes 393224 | tf_op jit(solution)/shard_map/ppermute | solution.py:395
  91.7 0.9 collective-permute-start.8
  92.6 3.5 %correlate_tiles.4 = (f32[2,8,5,256,256]{4,3,2,1,0:T(8,128)}, f32[8,128]{1,0:T(8,128)S(1)}) custom-call(s32[11]{0:T(128)S(1)} %pad_add_fusion.rest_7_.rest_3_.rest_6_.table_ref.rest_2_, bf16[2,4,2,4,64,128]{5,4,3,2,1,0:T(8,128)(2,1)S(1)} %get-tuple-element.89.rest_0_, bf16[2,4,2,4,64,128]{5,4,3,2,1,0:T(8,128)(2,1)S(1)} %collective-permute-done.17.rest_1_, ...), custom_call_target="tpu_custom_call" | custom-call | tf_op jit(solution)/shard_map/correlate_tiles/pallas_call | solution.py:361
  96.1 4.5 %collective-permute-done.7.rest_2_ = bf16[2,4,64,128]{3,2,1,0:T(8,128)(2,1)S(1)} collective-permute-done((bf16[2,4,64,128]{3,2,1,0:T(8,128)(2,1)S(1)}, bf16[2,4,64,128]{3,2,1,0:T(8,128)(2,1)S(1)}, u32[]{:S(2)}, u32[]{:S(2)}) %collective-permute-start.7) | collective-permute-done | bytes 131104 | tf_op jit(solution)/shard_map/ppermute | solution.py:395
  100.7 0.1 collective-permute-done.16.rest_5_
  100.8 0.6 join_pieces.6
  101.5 0.1 collective-permute-start.19
  101.5 1.3 collective-permute-start.18
  102.9 3.3 %collective-permute-start.9 = (bf16[2,4,64,128]{3,2,1,0:T(8,128)(2,1)S(1)}, bf16[2,4,64,128]{3,2,1,0:T(8,128)(2,1)S(1)}, u32[]{:S(2)}, u32[]{:S(2)}) collective-permute-start(bf16[2,4,64,128]{3,2,1,0:T(8,128)(2,1)S(1)} %get-tuple-element.81), channel_id=1, source_target_pairs={{0,4},{4,8},{8,12},{12,0},{1,5},{5,9},{9,13},{13,1},{2,6},{6,10},{... | collective-permute-start | bytes 393224 | tf_op jit(solution)/shard_map/ppermute | solution.py:395
  106.1 1.5 %collective-permute-start.10 = (bf16[2,4,64,128]{3,2,1,0:T(8,128)(2,1)S(1)}, bf16[2,4,64,128]{3,2,1,0:T(8,128)(2,1)S(1)}, u32[]{:S(2)}, u32[]{:S(2)}) collective-permute-start(bf16[2,4,64,128]{3,2,1,0:T(8,128)(2,1)S(1)} %get-tuple-element.82), channel_id=1, source_target_pairs={{0,8},{4,12},{8,0},{12,4},{1,9},{5,13},{9,1},{13,5},{2,10},{6,14},... | collective-permute-start | bytes 393224 | tf_op jit(solution)/shard_map/ppermute | solution.py:395
  107.7 0.8 collective-permute-start.11
  108.5 3.5 %correlate_tiles.5 = (f32[2,8,5,256,256]{4,3,2,1,0:T(8,128)}, f32[8,128]{1,0:T(8,128)S(1)}) custom-call(s32[11]{0:T(128)S(1)} %pad_add_fusion.rest_7_.rest_3_.rest_6_.table_ref.rest_2_, bf16[2,4,2,4,64,128]{5,4,3,2,1,0:T(8,128)(2,1)S(1)} %get-tuple-element.92.rest_0_, ...), custom_call_target="tpu_custom_call", output_to_operand_aliasing={{0}: (4, {})} | custom-call | tf_op jit(solution)/shard_map/correlate_tiles/pallas_call | solution.py:361
  112.1 4.6 %collective-permute-done.10.rest_2_ = bf16[2,4,64,128]{3,2,1,0:T(8,128)(2,1)S(1)} collective-permute-done((bf16[2,4,64,128]{3,2,1,0:T(8,128)(2,1)S(1)}, bf16[2,4,64,128]{3,2,1,0:T(8,128)(2,1)S(1)}, u32[]{:S(2)}, u32[]{:S(2)}) %collective-permute-start.10) | collective-permute-done | bytes 131104 | tf_op jit(solution)/shard_map/ppermute | solution.py:395
  116.7 0.6 join_pieces.7
  117.3 0.1 collective-permute-start.21
  117.4 0.6 collective-permute-start.20
  118.0 0.2 collective-permute-start.22
  118.2 1.9 %collective-permute-done.21.rest_1_ = bf16[2,4,2,4,64,128]{5,4,3,2,1,0:T(8,128)(2,1)S(1)} collective-permute-done((bf16[2,4,2,4,64,128]{5,4,3,2,1,0:T(8,128)(2,1)S(1)}, bf16[2,4,2,4,64,128]{5,4,3,2,1,0:T(8,128)(2,1)S(1)}, u32[]{:S(2)}, u32[]{:S(2)}) %collective-permute-start.21) | collective-permute-done | bytes 1048608 | tf_op jit(solution)/shard_map/ppermute | solution.py:402
  120.0 3.5 %correlate_tiles.6 = (f32[2,8,5,256,256]{4,3,2,1,0:T(8,128)}, f32[8,128]{1,0:T(8,128)S(1)}) custom-call(s32[11]{0:T(128)S(1)} %pad_add_fusion.rest_7_.rest_3_.rest_6_.table_ref.rest_2_, bf16[2,4,2,4,64,128]{5,4,3,2,1,0:T(8,128)(2,1)S(1)} %get-tuple-element.96.rest_0_, ...), custom_call_target="tpu_custom_call", output_to_operand_aliasing={{0}: (4, {})} | custom-call | tf_op jit(solution)/shard_map/correlate_tiles/pallas_call | solution.py:361
  123.6 8.2 %collective-permute-done.20 = bf16[4,2,4,64,128]{4,3,2,1,0:T(8,128)(2,1)S(1)} collective-permute-done((bf16[4,2,4,64,128]{4,3,2,1,0:T(8,128)(2,1)S(1)}, bf16[4,2,4,64,128]{4,3,2,1,0:T(8,128)(2,1)S(1)}, u32[]{:S(2)}, u32[]{:S(2)}) %collective-permute-start.20) | collective-permute-done | bytes 524320 | tf_op jit(solution)/shard_map/ppermute | solution.py:402
  131.7 1.9 %collective-permute-done.23.rest_3_ = bf16[1,4,2,4,64,128]{5,4,3,2,1,0:T(8,128)(2,1)S(1)} collective-permute-done((bf16[1,4,2,4,64,128]{5,4,3,2,1,0:T(8,128)(2,1)S(1)}, bf16[1,4,2,4,64,128]{5,4,3,2,1,0:T(8,128)(2,1)S(1)}, u32[]{:S(2)}, u32[]{:S(2)}) %collective-permute-start.23) | collective-permute-done | bytes 524320 | tf_op jit(solution)/shard_map/ppermute | solution.py:402
  133.7 4.1 %correlate_tiles.7 = (f32[2,8,5,256,256]{4,3,2,1,0:T(8,128)}, f32[8,128]{1,0:T(8,128)}) custom-call(s32[11]{0:T(128)S(1)} %pad_add_fusion.rest_7_.rest_3_.rest_6_.table_ref.rest_2_, bf16[1,4,2,4,64,128]{5,4,3,2,1,0:T(8,128)(2,1)S(1)} %bitcast.5, bf16[1,4,2,4,64,128]{5,4,3,2,1,0:T(8,128)(2,1)S(1)} %bitcast.7, ...), custom_call_target="tpu_custom_call", output_to_operand_aliasing={{0}: (6, {})} | custom-call | tf_op jit(solution)/shard_map/correlate_tiles/pallas_call | solution.py:361
  (18 shorter events, 0.1 us)
Async XLA Ops:
  0.1 1.6 %copy-start = (bf16[2,2048,256]{2,1,0:T(8,128)(2,1)S(1)}, bf16[2,2048,256]{2,1,0:T(8,128)(2,1)}, u32[]{:S(2)}) copy-start(bf16[2,2048,256]{2,1,0:T(8,128)(2,1)} %v_ref.1) | copy-start | bytes 6291460
  4.4 19.2 %collective-permute-start = (bf16[2,64,2048]{2,1,0:T(8,128)(2,1)}, bf16[2,64,2048]{2,1,0:T(8,128)(2,1)S(1)}, u32[]{:S(2)}, u32[]{:S(2)}) collective-permute-start(bf16[2,64,2048]{2,1,0:T(8,128)(2,1)} %get-tuple-element.55), channel_id=1, source_target_pairs={{0,4},{4,8},{8,12},{12,0},{1,5},{5,9},{9,13},{13,1},{2,6},{6,10},{... | collective-permute-start | bytes 1572872 | tf_op jit(solution)/shard_map/ppermute | solution.py:395
  7.4 36.8 %collective-permute-start.1 = (bf16[2,64,2048]{2,1,0:T(8,128)(2,1)S(1)}, bf16[2,64,2048]{2,1,0:T(8,128)(2,1)S(1)}, u32[]{:S(2)}, u32[]{:S(2)}) collective-permute-start(bf16[2,64,2048]{2,1,0:T(8,128)(2,1)S(1)} %get-tuple-element.56), channel_id=1, source_target_pairs={{0,8},{4,12},{8,0},{12,4},{1,9},{5,13},{9,1},{13,5},{2,10},{6,14},... | collective-permute-start | bytes 1572872 | tf_op jit(solution)/shard_map/ppermute | solution.py:395
  10.0 34.2 %collective-permute-start.2 = (bf16[2,64,2048]{2,1,0:T(8,128)(2,1)S(1)}, bf16[2,64,2048]{2,1,0:T(8,128)(2,1)S(1)}, u32[]{:S(2)}, u32[]{:S(2)}) collective-permute-start(bf16[2,64,2048]{2,1,0:T(8,128)(2,1)S(1)} %get-tuple-element.57), channel_id=1, source_target_pairs={{0,12},{4,0},{8,4},{12,8},{1,13},{5,1},{9,5},{13,9},{2,14},{6,2},{... | collective-permute-start | bytes 1572872 | tf_op jit(solution)/shard_map/ppermute | solution.py:395
  18.1 1.1 copy-start.1
  19.2 1.1 copy-start.2
  20.4 0.7 copy-start.3
  21.1 0.7 copy-start.4
  48.7 17.3 %collective-permute-start.12 = (bf16[2,4,64,128]{3,2,1,0:T(8,128)(2,1)S(1)}, bf16[2,4,64,128]{3,2,1,0:T(8,128)(2,1)S(1)}, u32[]{:S(2)}, u32[]{:S(2)}) collective-permute-start(bf16[2,4,64,128]{3,2,1,0:T(8,128)(2,1)S(1)} %get-tuple-element.85), channel_id=1, source_target_pairs={{0,4},{4,8},{8,12},{12,0},{1,5},{5,9},{9,13},{13,1},{2,6},{6,10},{... | collective-permute-start | bytes 393224 | tf_op jit(solution)/shard_map/ppermute | solution.py:395
  60.4 9.7 %collective-permute-start.13 = (bf16[2,4,64,128]{3,2,1,0:T(8,128)(2,1)S(1)}, bf16[2,4,64,128]{3,2,1,0:T(8,128)(2,1)S(1)}, u32[]{:S(2)}, u32[]{:S(2)}) collective-permute-start(bf16[2,4,64,128]{3,2,1,0:T(8,128)(2,1)S(1)} %get-tuple-element.86), channel_id=1, source_target_pairs={{0,8},{4,12},{8,0},{12,4},{1,9},{5,13},{9,1},{13,5},{2,10},{6,14},... | collective-permute-start | bytes 393224 | tf_op jit(solution)/shard_map/ppermute | solution.py:395
  62.0 8.1 %collective-permute-start.14 = (bf16[2,4,64,128]{3,2,1,0:T(8,128)(2,1)S(1)}, bf16[2,4,64,128]{3,2,1,0:T(8,128)(2,1)S(1)}, u32[]{:S(2)}, u32[]{:S(2)}) collective-permute-start(bf16[2,4,64,128]{3,2,1,0:T(8,128)(2,1)S(1)} %get-tuple-element.87), channel_id=1, source_target_pairs={{0,12},{4,0},{8,4},{12,8},{1,13},{5,1},{9,5},{13,9},{2,14},{6,2},{... | collective-permute-start | bytes 393224 | tf_op jit(solution)/shard_map/ppermute | solution.py:395
  70.7 15.1 %collective-permute-start.15 = (bf16[4,2,4,64,128]{4,3,2,1,0:T(8,128)(2,1)S(1)}, bf16[4,2,4,64,128]{4,3,2,1,0:T(8,128)(2,1)S(1)}, u32[]{:S(2)}, u32[]{:S(2)}) collective-permute-start(bf16[4,2,4,64,128]{4,3,2,1,0:T(8,128)(2,1)S(1)} %join_pieces.4.rest_4_), channel_id=1, source_target_pairs={{0,2},{1,3},{2,0},{3,1},{4,6},{5,7},{6,4},{7,5},{8,10},{9,11},{10,... | collective-permute-start | bytes 1572872 | tf_op jit(solution)/shard_map/ppermute | solution.py:402
  72.2 9.3 %collective-permute-start.3 = (bf16[2,4,64,128]{3,2,1,0:T(8,128)(2,1)S(1)}, bf16[2,4,64,128]{3,2,1,0:T(8,128)(2,1)S(1)}, u32[]{:S(2)}, u32[]{:S(2)}) collective-permute-start(bf16[2,4,64,128]{3,2,1,0:T(8,128)(2,1)S(1)} %get-tuple-element.73), channel_id=1, source_target_pairs={{0,4},{4,8},{8,12},{12,0},{1,5},{5,9},{9,13},{13,1},{2,6},{6,10},{... | collective-permute-start | bytes 393224 | tf_op jit(solution)/shard_map/ppermute | solution.py:395
  75.5 10.1 %collective-permute-start.4 = (bf16[2,4,64,128]{3,2,1,0:T(8,128)(2,1)S(1)}, bf16[2,4,64,128]{3,2,1,0:T(8,128)(2,1)S(1)}, u32[]{:S(2)}, u32[]{:S(2)}) collective-permute-start(bf16[2,4,64,128]{3,2,1,0:T(8,128)(2,1)S(1)} %get-tuple-element.74), channel_id=1, source_target_pairs={{0,8},{4,12},{8,0},{12,4},{1,9},{5,13},{9,1},{13,5},{2,10},{6,14},... | collective-permute-start | bytes 393224 | tf_op jit(solution)/shard_map/ppermute | solution.py:395
  77.6 8.1 %collective-permute-start.5 = (bf16[2,4,64,128]{3,2,1,0:T(8,128)(2,1)S(1)}, bf16[2,4,64,128]{3,2,1,0:T(8,128)(2,1)S(1)}, u32[]{:S(2)}, u32[]{:S(2)}) collective-permute-start(bf16[2,4,64,128]{3,2,1,0:T(8,128)(2,1)S(1)} %get-tuple-element.75), channel_id=1, source_target_pairs={{0,12},{4,0},{8,4},{12,8},{1,13},{5,1},{9,5},{13,9},{2,14},{6,2},{... | collective-permute-start | bytes 393224 | tf_op jit(solution)/shard_map/ppermute | solution.py:395
  86.4 6.2 %collective-permute-start.17 = (bf16[2,4,2,4,64,128]{5,4,3,2,1,0:T(8,128)(2,1)S(1)}, bf16[2,4,2,4,64,128]{5,4,3,2,1,0:T(8,128)(2,1)S(1)}, u32[]{:S(2)}, u32[]{:S(2)}) collective-permute-start(bf16[2,4,2,4,64,128]{5,4,3,2,1,0:T(8,128)(2,1)S(1)} %get-tuple-element.89.rest_0_), channel_id=1, source_target_pairs={{0,1},{1,0},{2,3},{3,2},{4,5},{5,4},{6,7},{7,6},{8,9},{9,8},{10,11... | collective-permute-start | bytes 3145736 | tf_op jit(solution)/shard_map/ppermute | solution.py:402
  86.5 14.3 %collective-permute-start.16 = (bf16[4,2,4,64,128]{4,3,2,1,0:T(8,128)(2,1)S(1)}, bf16[4,2,4,64,128]{4,3,2,1,0:T(8,128)(2,1)S(1)}, u32[]{:S(2)}, u32[]{:S(2)}) collective-permute-start(bf16[4,2,4,64,128]{4,3,2,1,0:T(8,128)(2,1)S(1)} %get-tuple-element.88.rest_4_), channel_id=1, source_target_pairs={{0,2},{1,3},{2,0},{3,1},{4,6},{5,7},{6,4},{7,5},{8,10},{9,11},{10,... | collective-permute-start | bytes 1572872 | tf_op jit(solution)/shard_map/ppermute | solution.py:402
  87.1 9.1 %collective-permute-start.6 = (bf16[2,4,64,128]{3,2,1,0:T(8,128)(2,1)S(1)}, bf16[2,4,64,128]{3,2,1,0:T(8,128)(2,1)S(1)}, u32[]{:S(2)}, u32[]{:S(2)}) collective-permute-start(bf16[2,4,64,128]{3,2,1,0:T(8,128)(2,1)S(1)} %get-tuple-element.77), channel_id=1, source_target_pairs={{0,4},{4,8},{8,12},{12,0},{1,5},{5,9},{9,13},{13,1},{2,6},{6,10},{... | collective-permute-start | bytes 393224 | tf_op jit(solution)/shard_map/ppermute | solution.py:395
  90.2 10.5 %collective-permute-start.7 = (bf16[2,4,64,128]{3,2,1,0:T(8,128)(2,1)S(1)}, bf16[2,4,64,128]{3,2,1,0:T(8,128)(2,1)S(1)}, u32[]{:S(2)}, u32[]{:S(2)}) collective-permute-start(bf16[2,4,64,128]{3,2,1,0:T(8,128)(2,1)S(1)} %get-tuple-element.78), channel_id=1, source_target_pairs={{0,8},{4,12},{8,0},{12,4},{1,9},{5,13},{9,1},{13,5},{2,10},{6,14},... | collective-permute-start | bytes 393224 | tf_op jit(solution)/shard_map/ppermute | solution.py:395
  91.7 9.0 %collective-permute-start.8 = (bf16[2,4,64,128]{3,2,1,0:T(8,128)(2,1)S(1)}, bf16[2,4,64,128]{3,2,1,0:T(8,128)(2,1)S(1)}, u32[]{:S(2)}, u32[]{:S(2)}) collective-permute-start(bf16[2,4,64,128]{3,2,1,0:T(8,128)(2,1)S(1)} %get-tuple-element.79), channel_id=1, source_target_pairs={{0,12},{4,0},{8,4},{12,8},{1,13},{5,1},{9,5},{13,9},{2,14},{6,2},{... | collective-permute-start | bytes 393224 | tf_op jit(solution)/shard_map/ppermute | solution.py:395
  101.5 7.1 %collective-permute-start.19 = (bf16[2,4,2,4,64,128]{5,4,3,2,1,0:T(8,128)(2,1)S(1)}, bf16[2,4,2,4,64,128]{5,4,3,2,1,0:T(8,128)(2,1)S(1)}, u32[]{:S(2)}, u32[]{:S(2)}) collective-permute-start(bf16[2,4,2,4,64,128]{5,4,3,2,1,0:T(8,128)(2,1)S(1)} %get-tuple-element.92.rest_0_), channel_id=1, source_target_pairs={{0,1},{1,0},{2,3},{3,2},{4,5},{5,4},{6,7},{7,6},{8,9},{9,8},{10,11... | collective-permute-start | bytes 3145736 | tf_op jit(solution)/shard_map/ppermute | solution.py:402
  101.5 15.1 %collective-permute-start.18 = (bf16[4,2,4,64,128]{4,3,2,1,0:T(8,128)(2,1)S(1)}, bf16[4,2,4,64,128]{4,3,2,1,0:T(8,128)(2,1)S(1)}, u32[]{:S(2)}, u32[]{:S(2)}) collective-permute-start(bf16[4,2,4,64,128]{4,3,2,1,0:T(8,128)(2,1)S(1)} %get-tuple-element.91.rest_4_), channel_id=1, source_target_pairs={{0,2},{1,3},{2,0},{3,1},{4,6},{5,7},{6,4},{7,5},{8,10},{9,11},{10,... | collective-permute-start | bytes 1572872 | tf_op jit(solution)/shard_map/ppermute | solution.py:402
  102.9 9.2 %collective-permute-start.9 = (bf16[2,4,64,128]{3,2,1,0:T(8,128)(2,1)S(1)}, bf16[2,4,64,128]{3,2,1,0:T(8,128)(2,1)S(1)}, u32[]{:S(2)}, u32[]{:S(2)}) collective-permute-start(bf16[2,4,64,128]{3,2,1,0:T(8,128)(2,1)S(1)} %get-tuple-element.81), channel_id=1, source_target_pairs={{0,4},{4,8},{8,12},{12,0},{1,5},{5,9},{9,13},{13,1},{2,6},{6,10},{... | collective-permute-start | bytes 393224 | tf_op jit(solution)/shard_map/ppermute | solution.py:395
  106.1 10.5 %collective-permute-start.10 = (bf16[2,4,64,128]{3,2,1,0:T(8,128)(2,1)S(1)}, bf16[2,4,64,128]{3,2,1,0:T(8,128)(2,1)S(1)}, u32[]{:S(2)}, u32[]{:S(2)}) collective-permute-start(bf16[2,4,64,128]{3,2,1,0:T(8,128)(2,1)S(1)} %get-tuple-element.82), channel_id=1, source_target_pairs={{0,8},{4,12},{8,0},{12,4},{1,9},{5,13},{9,1},{13,5},{2,10},{6,14},... | collective-permute-start | bytes 393224 | tf_op jit(solution)/shard_map/ppermute | solution.py:395
  107.7 9.0 %collective-permute-start.11 = (bf16[2,4,64,128]{3,2,1,0:T(8,128)(2,1)S(1)}, bf16[2,4,64,128]{3,2,1,0:T(8,128)(2,1)S(1)}, u32[]{:S(2)}, u32[]{:S(2)}) collective-permute-start(bf16[2,4,64,128]{3,2,1,0:T(8,128)(2,1)S(1)} %get-tuple-element.83), channel_id=1, source_target_pairs={{0,12},{4,0},{8,4},{12,8},{1,13},{5,1},{9,5},{13,9},{2,14},{6,2},{... | collective-permute-start | bytes 393224 | tf_op jit(solution)/shard_map/ppermute | solution.py:395
  117.3 2.7 %collective-permute-start.21 = (bf16[2,4,2,4,64,128]{5,4,3,2,1,0:T(8,128)(2,1)S(1)}, bf16[2,4,2,4,64,128]{5,4,3,2,1,0:T(8,128)(2,1)S(1)}, u32[]{:S(2)}, u32[]{:S(2)}) collective-permute-start(bf16[2,4,2,4,64,128]{5,4,3,2,1,0:T(8,128)(2,1)S(1)} %get-tuple-element.96.rest_0_), channel_id=1, source_target_pairs={{0,1},{1,0},{2,3},{3,2},{4,5},{5,4},{6,7},{7,6},{8,9},{9,8},{10,11... | collective-permute-start | bytes 3145736 | tf_op jit(solution)/shard_map/ppermute | solution.py:402
  117.4 14.3 %collective-permute-start.20 = (bf16[4,2,4,64,128]{4,3,2,1,0:T(8,128)(2,1)S(1)}, bf16[4,2,4,64,128]{4,3,2,1,0:T(8,128)(2,1)S(1)}, u32[]{:S(2)}, u32[]{:S(2)}) collective-permute-start(bf16[4,2,4,64,128]{4,3,2,1,0:T(8,128)(2,1)S(1)} %get-tuple-element.95), channel_id=1, source_target_pairs={{0,2},{1,3},{2,0},{3,1},{4,6},{5,7},{6,4},{7,5},{8,10},{9,11},{10,... | collective-permute-start | bytes 1572872 | tf_op jit(solution)/shard_map/ppermute | solution.py:402
  118.0 13.7 %collective-permute-start.22 = (bf16[1,4,2,4,64,128]{5,4,3,2,1,0:T(8,128)(2,1)S(1)}, bf16[1,4,2,4,64,128]{5,4,3,2,1,0:T(8,128)(2,1)S(1)}, u32[]{:S(2)}, u32[]{:S(2)}) collective-permute-start(bf16[1,4,2,4,64,128]{5,4,3,2,1,0:T(8,128)(2,1)S(1)} %bitcast.4), channel_id=1, source_target_pairs={{0,1},{1,0},{2,3},{3,2},{4,5},{5,4},{6,7},{7,6},{8,9},{9,8},{10,11... | collective-permute-start | bytes 1572872 | tf_op jit(solution)/shard_map/ppermute | solution.py:402
  131.7 1.9 %collective-permute-start.23 = (bf16[1,4,2,4,64,128]{5,4,3,2,1,0:T(8,128)(2,1)S(1)}, bf16[1,4,2,4,64,128]{5,4,3,2,1,0:T(8,128)(2,1)S(1)}, u32[]{:S(2)}, u32[]{:S(2)}) collective-permute-start(bf16[1,4,2,4,64,128]{5,4,3,2,1,0:T(8,128)(2,1)S(1)} %bitcast.6), channel_id=1, source_target_pairs={{0,1},{1,0},{2,3},{3,2},{4,5},{5,4},{6,7},{7,6},{8,9},{9,8},{10,11... | collective-permute-start | bytes 1572872 | tf_op jit(solution)/shard_map/ppermute | solution.py:402
